TPU v7x, 32 devices: a whole 2x2x4 slice. The times are simulated.
32 devices in a mesh: groups: 2 (over x), seq: 8 (over z, y), chan: 2 (over core).
Axes of the slice: x: 2, y: 2, z: 4, core: 2. Of those that a mesh axis runs over, the one named last changes fastest.
Arguments:
- query_feat: bfloat16 [4096, 2048], P('chan', ('groups', 'seq')), parts along dimension 1, may hold values from -6 to 6
- key_feat: bfloat16 [4096, 2048], P('chan', ('groups', 'seq')), parts along dimension 1, may hold values from -6 to 6
- value_feat: bfloat16 [4096, 2048], P('chan', ('groups', 'seq')), parts along dimension 1, may hold values from -6 to 6
- filter_seed: int32 [16], replicated, may hold values from 1 to 511
- filter_in: float32 [32, 64], replicated, may hold values from -1 to 1
- filter_bias: float32 [64], replicated, may hold values from -3.140625 to 3.140625
- filter_out: float32 [64, 256], P(None, 'chan'), may hold values from -0.75 to 0.75
- decay_rate: float32 [256], P('chan'), may hold values from 0.000390625 to 0.0078125
- reach_blocks: int32 [256], P('chan'), may hold values from 1 to 2, as said below
- skip_gain: float32 [4096], P('chan'), may hold values from -4 to 4
- out_weight: bfloat16 [4096, 2048], P('chan'), may hold values from -0.09375 to 0.09375
Outputs:
- projected: bfloat16 [2048, 2048], P(('groups', 'seq'), 'chan'), parts along dimension 0
There are 2 independent parts, one for each index of `groups`. A program takes and returns all parts, laid end to end along the dimension named above; an argument that names none is the same for every part. Nothing has to cross between parts.
Inputs may be any that keep to these rules, and one draw needn't show every extreme that they name: `reach_blocks`: some filter group reaches 2 blocks and some filter group only one.
All inputs are finite; a program needn't handle non-finite values.
Results may differ from a plain program's by a relative error of at most 0.0059.
Values may be sent and summed in bfloat16 or wider, within the bound.
No kernel may reach another device: no remote copies, remote signals or barrier semaphores. Data moves between devices by JAX's collectives and lax.ppermute only.
A program may use at most 128 MiB of HBM per device.

v0:
```python
import math

import jax
import jax.numpy as jnp
from jax import lax
from jax.sharding import PartitionSpec as P


def filter_rows(
    lag_index,
    filter_seed,
    filter_in,
    filter_bias,
    filter_out,
    decay_rate,
    reach_blocks,
    block_len,
    seq_len,
    reach_max,
):
    safe_lag = jnp.maximum(lag_index, 0)
    phases = safe_lag[:, None] * filter_seed[None, :] % seq_len
    angles = phases.astype(jnp.float32) * (2.0 * math.pi / seq_len)
    features = jnp.concatenate([jnp.cos(angles), jnp.sin(angles)], axis=1)
    hidden = jnp.sin(
        jnp.dot(
            features, filter_in, precision=lax.Precision.HIGHEST, preferred_element_type=jnp.float32
        )
        + filter_bias
    )
    shaped = jnp.dot(
        hidden, filter_out, precision=lax.Precision.HIGHEST, preferred_element_type=jnp.float32
    )
    envelope = jnp.exp(-decay_rate[None, :] * safe_lag.astype(jnp.float32)[:, None]) * (
        1.0 / math.sqrt(reach_max * block_len)
    )
    inside = (lag_index[:, None] >= 0) & (lag_index[:, None] < reach_blocks[None, :] * block_len)
    return jnp.where(inside, shaped * envelope, 0.0).astype(jnp.bfloat16)


def hankel_rows(tap_rows, sub_len, span_len):
    return jnp.stack(
        [
            tap_rows[:, sub_len - 1 - offset : sub_len - 1 - offset + span_len]
            for offset in range(sub_len)
        ],
        axis=1,
    )


def body(
    query_feat,
    key_feat,
    value_feat,
    filter_seed,
    filter_in,
    filter_bias,
    filter_out,
    decay_rate,
    reach_blocks,
    skip_gain,
    out_weight,
):
    channels, block = query_feat.shape
    seq_count = lax.axis_size("seq")
    reach_max = seq_count // 4
    seq_len = block * seq_count
    sub_len = min(128, block)
    span_len = reach_max * block + sub_len
    rev_len = span_len + sub_len - 1
    filter_count = decay_rate.shape[0]
    per_group = channels // filter_count
    product = (key_feat.astype(jnp.float32) * value_feat.astype(jnp.float32)).astype(jnp.bfloat16)
    lag_index = reach_max * block + sub_len - 1 - lax.iota(jnp.int32, rev_len)
    taps = filter_rows(
        lag_index,
        filter_seed,
        filter_in,
        filter_bias,
        filter_out,
        decay_rate,
        reach_blocks,
        block,
        seq_len,
        reach_max,
    ).T
    seq_index = lax.axis_index("seq")
    spread, query_all = (
        lax.all_to_all(product, "seq", split_axis=0, concat_axis=1, tiled=True),
        lax.all_to_all(query_feat, "seq", split_axis=0, concat_axis=1, tiled=True),
    )
    chan_dev = spread.shape[0]
    full_len = spread.shape[1]
    padded = jnp.concatenate(
        [jnp.zeros((chan_dev, reach_max * block), jnp.bfloat16), spread], axis=1
    )
    pieces = padded.reshape(chan_dev, -1, sub_len)
    count_tiles = full_len // sub_len
    span_blocks = span_len // sub_len
    windows = jnp.concatenate([pieces[:, k : k + count_tiles] for k in range(span_blocks)], axis=2)
    first_chan = seq_index * chan_dev
    group_ids = (first_chan + lax.iota(jnp.int32, chan_dev)) // per_group
    chan_taps = jnp.take(taps, group_ids, axis=0)
    chan_block = math.gcd(8, chan_dev)
    windows = windows.reshape(chan_dev // chan_block, chan_block, count_tiles, span_len)
    chan_taps = chan_taps.reshape(chan_dev // chan_block, chan_block, rev_len)

    def convolve_chan(inputs_pair):
        window_part, tap_part = inputs_pair
        hankel = hankel_rows(tap_part, sub_len, span_len)
        return jnp.einsum("ctw,caw->cta", window_part, hankel, preferred_element_type=jnp.float32)

    convolved = lax.map(convolve_chan, (windows, chan_taps))
    convolved = convolved.reshape(chan_dev, full_len)
    skip_part = lax.dynamic_slice_in_dim(skip_gain, first_chan, chan_dev)
    mixed_part = convolved + skip_part[:, None] * spread.astype(jnp.float32)
    gated_part = (query_all.astype(jnp.float32) * mixed_part).astype(jnp.bfloat16)
    gated = lax.all_to_all(gated_part, "seq", split_axis=1, concat_axis=0, tiled=True)
    reduced = lax.psum_scatter(
        lax.dot_general(
            out_weight, gated, (((0,), (0,)), ((), ())), preferred_element_type=jnp.float32
        ),
        "chan",
        scatter_dimension=0,
        tiled=True,
    )
    return reduced.T.astype(jnp.bfloat16)


def solution(mesh):
    return jax.shard_map(
        body,
        mesh=mesh,
        in_specs=(
            P("chan", ("groups", "seq")),
            P("chan", ("groups", "seq")),
            P("chan", ("groups", "seq")),
            P(),
            P(),
            P(),
            P(None, "chan"),
            P("chan"),
            P("chan"),
            P("chan"),
            P("chan", None),
        ),
        out_specs=P(("groups", "seq"), "chan"),
        check_vma=False,
    )
```

profile of v0, /device:TPU:9, one launch (start us, length us, event | category | flops | bytes accessed | tf_op | source)
XLA Modules:
  0.0 349.9 jit_solution(17772065564736948912)
XLA Ops:
  6.5 2.1 multiply_convert_fusion
  8.7 5.7 %all-to-all-start.1 = ((bf16[8,256,128]{2,1,0:T(8,128)(2,1)}), bf16[8,256,128]{2,1,0:T(8,128)(2,1)S(1)}, u32[]{:S(2)}, u32[]{:S(2)}) async-start(bf16[8,256,128]{2,1,0:T(8,128)(2,1)} %bitcast.133), calls=%async_computation.1 | async-start | bytes 1048576 | tf_op jit(solution)/shard_map/all_to_all | solution.py:89
  16.6 1.5 fusion.6
  21.7 3.7 %all-to-all-done.1 = bf16[8,256,128]{2,1,0:T(8,128)(2,1)S(1)} async-done(((bf16[8,256,128]{2,1,0:T(8,128)(2,1)}), bf16[8,256,128]{2,1,0:T(8,128)(2,1)S(1)}, u32[]{:S(2)}, u32[]{:S(2)}) %all-to-all-start.1) | async-done | bytes 524320 | tf_op jit(solution)/shard_map/all_to_all | solution.py:89
  25.4 7.3 %all-to-all-start = ((bf16[8,256,128]{2,1,0:T(8,128)(2,1)}), bf16[8,256,128]{2,1,0:T(8,128)(2,1)S(1)}, u32[]{:S(2)}, u32[]{:S(2)}) async-start(bf16[8,256,128]{2,1,0:T(8,128)(2,1)} %bitcast.131), calls=%async_computation | async-start | bytes 1048576 | tf_op jit(solution)/shard_map/all_to_all | solution.py:90
  33.3 2.1 copy.4333
  35.4 270.5 %while.10 = (s32[]{:T(128)}, f32[32,8,8,128]{3,1,0,2:T(8,128)}, bf16[32,8,8,384]{3,2,1,0:T(8,128)(2,1)}, bf16[32,8,511]{2,1,0:T(8,128)(2,1)}, s32[]{:T(128)}) while((s32[]{:T(128)}, f32[32,8,8,128]{3,1,0,2:T(8,128)}, bf16[32,8,8,384]{3,2,1,0:T(8,128)(2,1)}, bf16[32,8,511]{2,1,0:T(8,128)(2,1)}, s32[]{:T(128)}) %tuple.163), condition=%wide.region_1.2_spmd, body=%wide.region_0.1_spmd.sunk | while | flops 6291458 | bytes 5669921 | solution.py:113
  39.3 2.7 stack.388
  42.0 1.2 convolution_bitcast_fusion.4
  47.8 2.7 stack.388
  50.5 1.2 convolution_bitcast_fusion.4
  56.2 2.7 stack.388
  58.9 1.2 convolution_bitcast_fusion.4
  64.7 2.7 stack.388
  67.4 1.2 convolution_bitcast_fusion.4
  73.1 2.7 stack.388
  81.6 2.7 stack.388
  90.0 2.7 stack.388
  98.5 2.7 stack.388
  106.9 2.7 stack.388
  115.4 2.7 stack.388
  123.9 2.7 stack.388
  132.3 2.7 stack.388
  140.8 2.7 stack.388
  149.2 2.7 stack.388
  157.7 2.7 stack.388
  166.1 2.7 stack.388
  174.6 2.7 stack.388
  183.0 2.7 stack.388
  191.5 2.7 stack.388
  199.9 2.7 stack.388
  208.4 2.7 stack.388
  216.8 2.7 stack.388
  225.3 2.7 stack.388
  233.7 2.7 stack.388
  242.2 2.7 stack.388
  250.6 2.7 stack.388
  259.1 2.7 stack.388
  267.5 2.7 stack.388
  276.0 2.7 stack.388
  284.4 2.7 stack.388
  292.9 2.7 stack.388
  301.3 2.7 stack.388
  305.8 1.5 fusion.8
  307.4 17.2 %all_to_all.48 = bf16[256,8,128]{2,0,1:T(8,128)(2,1)S(1)} all-to-all(bf16[256,8,128]{2,0,1:T(8,128)(2,1)S(1)} %fusion.8), channel_id=1, replica_groups=mesh['groups'=2,'seq'=8,'chan'=2] {'seq'}, dimensions={1} | all-to-all | bytes 1048576 | tf_op jit(solution)/shard_map/all_to_all | solution.py:118
  324.6 5.6 %convolution_bitcast_fusion.1 = f32[2048,128]{0,1:T(8,128)} fusion(bf16[2048,128]{1,0:T(8,128)(2,1)S(1)} %bitcast.326, bf16[2048,2048]{1,0:T(8,128)(2,1)} %param.23), kind=kOutput, calls=%fused_computation.135 | convolution fusion | flops 1073741824 | bytes 9961472 | tf_op jit(solution)/shard_map/dot_general | solution.py:120
  330.2 11.0 %reduce-scatter.2.cloned.1.call-done = f32[1024,128]{0,1:T(8,128)} async-done(((f32[2048,128]{0,1:T(8,128)}), f32[1024,128]{0,1:T(8,128)}) %reduce-scatter.2.cloned.1.call-update) | async-done | bytes 524304 | tf_op jit(solution)/shard_map/reduce_scatter | solution.py:119
  341.2 1.8 convert_bitcast_fusion
  (4436 shorter events, 152.0 us)
Async XLA Ops:
  6.5 11.5 %copy-start = (f32[64,128]{1,0:T(8,128)S(1)}, f32[64,128]{1,0:T(8,128)}, u32[]{:S(2)}) copy-start(f32[64,128]{1,0:T(8,128)} %param.19) | copy-start | bytes 98308
  8.7 16.7 %all-to-all-start.1 = ((bf16[8,256,128]{2,1,0:T(8,128)(2,1)}), bf16[8,256,128]{2,1,0:T(8,128)(2,1)S(1)}, u32[]{:S(2)}, u32[]{:S(2)}) async-start(bf16[8,256,128]{2,1,0:T(8,128)(2,1)} %bitcast.133), calls=%async_computation.1 | async-start | bytes 1048576 | tf_op jit(solution)/shard_map/all_to_all | solution.py:89
  25.4 280.4 %all-to-all-start = ((bf16[8,256,128]{2,1,0:T(8,128)(2,1)}), bf16[8,256,128]{2,1,0:T(8,128)(2,1)S(1)}, u32[]{:S(2)}, u32[]{:S(2)}) async-start(bf16[8,256,128]{2,1,0:T(8,128)(2,1)} %bitcast.131), calls=%async_computation | async-start | bytes 1048576 | tf_op jit(solution)/shard_map/all_to_all | solution.py:90
  32.7 308.5 %reduce-scatter.2.cloned.1.call-start = ((), (), s32[]{:S(2)}) async-start(), calls=%async_computation.4 | async-start | bytes 1572864 | tf_op jit(solution)/shard_map/reduce_scatter | solution.py:119
Sparse Core Ops, SparseCore 0:
  330.3 10.8 reduce-scatter.1
where the time goes:
time: 354 us; the launch traced here: 350 us
  local copies, waits for them, and re-layouts  203 us (57%)
  matrix products  45.3 us (13%)
  loops' own time  34.2 us (10%)
  blocking collectives  17.2 us (5%)
  waiting for transfers between devices  14.7 us (4%)
  between operations  13.5 us (4%)
  starting transfers between devices  13 us (4%)
  other arithmetic  8.58 us (2%)
    another operation x4352, local copies, waits for them, and re-layouts, hankel_rows(): jnp.stack([tap_rows[:, sub_len - 1 - offset:sub_len - 1 - offset + span_l...  156 us
    dot_general x32, matrix products, convolve_chan(): jnp.einsum('ctw,caw->cta', window_part, hankel, preferred_element_type=jn...  37.5 us
    another operation x1, loops' own time, body(): convolved = lax.map(convolve_chan, (windows, chan_taps))  34.2 us
    squeeze x32, local copies, waits for them, and re-layouts, body(): convolved = lax.map(convolve_chan, (windows, chan_taps))  22.3 us
    dynamic_update_slice x32, local copies, waits for them, and re-layouts, body(): convolved = lax.map(convolve_chan, (windows, chan_taps))  20.6 us
    all_to_all x1, blocking collectives, body(): lax.all_to_all(gated_part, 'seq', split_axis=1, concat_axis=0, tiled=True)  17.2 us
    reduce_scatter x1, waiting for transfers between devices, body(): lax.psum_scatter(lax.dot_general(out_weight, gated, (((0,), (0,)), ((), (...  11 us
    all_to_all x1, starting transfers between devices, body(): lax.all_to_all(query_feat, 'seq', split_axis=0, concat_axis=1, tiled=True)  7.28 us

commit v1 on v0

v1 whole, which is shorter than its diff:
```python
import math

import jax
import jax.numpy as jnp
import numpy as np
from jax import lax
from jax.experimental import pallas as pl
from jax.experimental.pallas import tpu as pltpu
from jax.sharding import PartitionSpec as P

VMEM_BYTES = 32 * 1024 * 1024


def split_bf16(array):
    high = array.astype(jnp.bfloat16)
    low = (array - high.astype(np.float64)).astype(jnp.bfloat16)
    return high, low


def transform_tables(window, first_out, block):
    half = 128 * math.ceil(window / 256)
    omega = (np.arange(half) + 0.5) * (math.pi / half)
    angle = np.arange(window)[:, None] * omega[None, :]
    forward = np.concatenate([np.cos(angle), np.sin(angle)], axis=1)
    back = omega[:, None] * (first_out + np.arange(block))[None, :]
    inverse = np.concatenate([np.cos(back), np.sin(back)], axis=0) / half
    return split_bf16(forward), split_bf16(inverse)


def spectrum_kernel(seq_len, block, scale, seed, f_in, bias, f_out, decay, reach, fwd_hi, fwd_lo, out):
    lags = fwd_hi.shape[0]
    lag = lax.broadcasted_iota(jnp.int32, (lags, 1), 0)
    if seq_len & (seq_len - 1) == 0:
        phases = (lag * seed[...]) & (seq_len - 1)
    else:
        phases = lax.rem(lag * seed[...], seq_len)
    angles = phases.astype(jnp.float32) * (2.0 * math.pi / seq_len)
    features = jnp.concatenate([jnp.cos(angles), jnp.sin(angles)], axis=1)
    exact = dict(precision=lax.Precision.HIGHEST, preferred_element_type=jnp.float32)
    hidden = jnp.sin(jnp.dot(features, f_in[...], **exact) + bias[...])
    shaped = jnp.dot(hidden, f_out[...], **exact)
    envelope = jnp.exp(-decay[...] * lag.astype(jnp.float32)) * scale
    taps = jnp.where(lag < reach[...] * block, shaped * envelope, 0.0).astype(jnp.bfloat16)
    dims = (((0,), (0,)), ((), ()))
    out[...] = lax.dot_general(taps, fwd_hi[...], dims, preferred_element_type=jnp.float32) + lax.dot_general(
        taps, fwd_lo[...], dims, preferred_element_type=jnp.float32
    )


def conv_kernel(reach_max, per_group, core, *refs):
    xs = refs[: reach_max + 1]
    query, direct, spectrum, fwd_hi, fwd_lo, inverse, weight, part, gated_t, total, mult = refs[reach_max + 1 :]
    step = pl.program_id(0)
    half = fwd_hi.shape[1] // 2
    block = query.shape[1]
    window = jnp.concatenate([x[...] for x in xs], axis=1)
    freq = jnp.dot(window, fwd_hi[...], preferred_element_type=jnp.float32) + jnp.dot(
        window, fwd_lo[...], preferred_element_type=jnp.float32
    )
    for g in range(spectrum.shape[0]):
        rows = slice(g * per_group, (g + 1) * per_group)
        xc, xs_ = freq[rows, :half], freq[rows, half:]
        hc, hs = spectrum[g : g + 1, :half], spectrum[g : g + 1, half:]
        mult[rows, :half] = (xc * hc - xs_ * hs).astype(jnp.bfloat16)
        mult[rows, half:] = (xc * hs + xs_ * hc).astype(jnp.bfloat16)
    both = jnp.dot(mult[...], inverse[...], preferred_element_type=jnp.float32)
    mixed = both[:, :block] + both[:, block:] + direct[...]
    gated = (query[...].astype(jnp.float32) * mixed).astype(jnp.bfloat16).T
    gated_t[...] = gated

    @pl.when(step == 0)
    def _():
        total[...] = jnp.zeros_like(total)

    total[...] += jnp.dot(gated, weight[...], preferred_element_type=jnp.float32)

    @pl.when(step == pl.num_programs(0) - 1)
    def _():
        part[...] = total[...].astype(part.dtype)


def project_kernel(core, gated_t, weight, out):
    @pl.when(pl.program_id(0) == 0)
    def _():
        out[...] = jnp.zeros_like(out)

    out[...] += jnp.dot(gated_t[...], weight[...], preferred_element_type=jnp.float32)


def body(
    query_feat,
    key_feat,
    value_feat,
    filter_seed,
    filter_in,
    filter_bias,
    filter_out,
    decay_rate,
    reach_blocks,
    skip_gain,
    out_weight,
):
    channels, block = query_feat.shape
    seq_count = lax.axis_size("seq")
    reach_max = seq_count // 4
    filters = decay_rate.shape[0]
    per_group = channels // filters
    lags = reach_max * block
    window = lags + block
    (fwd_hi, fwd_lo), (inv_hi, inv_lo) = transform_tables(window, lags, block)
    inverse = np.concatenate([inv_hi, inv_lo], axis=1)
    length = fwd_hi.shape[1]
    cols = out_weight.shape[1] // 2
    params = pltpu.CompilerParams(vmem_limit_bytes=VMEM_BYTES)

    wide = key_feat.astype(jnp.float32) * value_feat.astype(jnp.float32)
    product = wide.astype(jnp.bfloat16)
    halos = [
        lax.ppermute(product, "seq", [(i, i + back) for i in range(seq_count - back)])
        for back in range(reach_max, 0, -1)
    ]
    direct = skip_gain[:, None] * product.astype(jnp.float32)

    spectrum = pl.pallas_call(
        lambda *refs: spectrum_kernel(block * seq_count, block, 1.0 / math.sqrt(lags), *refs),
        out_shape=jax.ShapeDtypeStruct((filters, length), jnp.float32),
        compiler_params=params,
    )(
        filter_seed[None],
        filter_in,
        filter_bias[None],
        filter_out,
        decay_rate[None],
        reach_blocks[None],
        jnp.asarray(fwd_hi[:lags]),
        jnp.asarray(fwd_lo[:lags]),
    )

    tile = math.gcd(256, channels)
    tiles = channels // tile
    core = lax.axis_index("chan").astype(jnp.int32).reshape(1)
    by_rows = lambda i, c: (i, 0)
    whole = lambda i, c: (0, 0)
    part, gated_t = pl.pallas_call(
        lambda core, *refs: conv_kernel(reach_max, per_group, core, *refs),
        grid_spec=pltpu.PrefetchScalarGridSpec(
            num_scalar_prefetch=1,
            grid=(tiles,),
            in_specs=[pl.BlockSpec((tile, block), by_rows)] * (reach_max + 3)
            + [
                pl.BlockSpec((tile // per_group, length), by_rows),
                pl.BlockSpec((window, length), whole),
                pl.BlockSpec((window, length), whole),
                pl.BlockSpec((length, 2 * block), whole),
                pl.BlockSpec((tile, cols), lambda i, c: (i, 1 - c[0])),
            ],
            out_specs=[
                pl.BlockSpec((block, cols), whole),
                pl.BlockSpec((block, tile), lambda i, c: (0, i)),
            ],
            scratch_shapes=[pltpu.VMEM((block, cols), jnp.float32), pltpu.VMEM((tile, length), jnp.bfloat16)],
        ),
        out_shape=[
            jax.ShapeDtypeStruct((block, cols), jnp.bfloat16),
            jax.ShapeDtypeStruct((block, channels), jnp.bfloat16),
        ],
        compiler_params=params,
    )(
        core,
        *halos,
        product,
        query_feat,
        direct,
        spectrum,
        jnp.asarray(fwd_hi),
        jnp.asarray(fwd_lo),
        jnp.asarray(inverse),
        out_weight,
    )
    received = lax.ppermute(part, "chan", [(0, 1), (1, 0)])
    own = pl.pallas_call(
        project_kernel,
        grid_spec=pltpu.PrefetchScalarGridSpec(
            num_scalar_prefetch=1,
            grid=(tiles,),
            in_specs=[
                pl.BlockSpec((block, tile), lambda i, c: (0, i)),
                pl.BlockSpec((tile, cols), lambda i, c: (i, c[0])),
            ],
            out_specs=pl.BlockSpec((block, cols), whole),
        ),
        out_shape=jax.ShapeDtypeStruct((block, cols), jnp.float32),
        compiler_params=params,
    )(core, gated_t, out_weight)
    return (own + received.astype(jnp.float32)).astype(jnp.bfloat16)


def solution(mesh):
    return jax.shard_map(
        body,
        mesh=mesh,
        in_specs=(
            P("chan", ("groups", "seq")),
            P("chan", ("groups", "seq")),
            P("chan", ("groups", "seq")),
            P(),
            P(),
            P(),
            P(None, "chan"),
            P("chan"),
            P("chan"),
            P("chan"),
            P("chan", None),
        ),
        out_specs=P(("groups", "seq"), "chan"),
        check_vma=False,
    )
```

time: 354 us -> 48.5 us (0.14)
  the two profiles are of different devices: /device:TPU:9 before, /device:TPU:15 now
where the time goes in v1:
time: 48.5 us; the launch traced here: 47.9 us
  local copies, waits for them, and re-layouts  13.4 us (28%)
  Pallas kernels  12.5 us (26%)
  waiting for transfers between devices  11.7 us (24%)
  starting transfers between devices  7.97 us (16%)
  other arithmetic  2.31 us (5%)
    unnamed x28, local copies, waits for them, and re-layouts  13.4 us
    ppermute x2, waiting for transfers between devices, body(): lax.ppermute(product, 'seq', [(i, i + back) for i in range(seq_count - ba...  11.7 us
    pallas_call x1, Pallas kernels, body(): pl.pallas_call(lambda core, *refs: conv_kernel(reach_max, per_group, core...  8.28 us
    ppermute x2, starting transfers between devices, body(): lax.ppermute(product, 'seq', [(i, i + back) for i in range(seq_count - ba...  6.35 us
    pallas_call x1, Pallas kernels, body(): pl.pallas_call(project_kernel, grid_spec=pltpu.PrefetchScalarGridSpec(num...  2.45 us
    pallas_call x1, Pallas kernels, body(): pl.pallas_call(lambda *refs: spectrum_kernel(block * seq_count, block, 1....  1.82 us
    ppermute x1, starting transfers between devices, body(): received = lax.ppermute(part, 'chan', [(0, 1), (1, 0)])  1.61 us
    mul x1, other arithmetic, body(): direct = skip_gain[:, None] * product.astype(jnp.float32)  1.55 us
  transfers between devices with their start and end apart: 3, of which 2 were waited for; matrix products, arithmetic and copies ran while one was open for 0% of the time, Pallas kernels for 9%

profile of v1, /device:TPU:15, one launch (start us, length us, event | category | flops | bytes accessed | tf_op | source)
XLA Modules:
  0.0 47.9 jit_solution(4183710528876433020)
XLA Ops:
  0.0 1.6 %convert_multiply_fusion = (f32[2048,128]{1,0:T(8,128)S(1)}, bf16[2048,128]{1,0:T(8,128)(2,1)S(1)}) fusion(f32[2048]{0:T(1024)} %param.25, bf16[2048,128]{1,0:T(8,128)(2,1)} %param.18, bf16[2048,128]{1,0:T(8,128)(2,1)} %param.17), kind=kLoop, calls=%fused_computation | loop fusion | flops 1572864 | bytes 2629632 | tf_op jit(solution)/shard_map/mul | solution.py:122
  1.6 3.1 %collective-permute-start.1 = (bf16[2048,128]{1,0:T(8,128)(2,1)S(1)}, bf16[2048,128]{1,0:T(8,128)(2,1)S(1)}, u32[]{:S(2)}, u32[]{:S(2)}) collective-permute-start(bf16[2048,128]{1,0:T(8,128)(2,1)S(1)} %get-tuple-element.10.refs_2_), channel_id=1, source_target_pairs={{0,2},{2,4},{4,6},{6,8},{8,10},{10,12},{12,14},{1,3},{3,5},{5,7},{... | collective-permute-start | bytes 1572872 | tf_op jit(solution)/shard_map/ppermute | solution.py:119
  4.7 3.2 %collective-permute-start = (bf16[2048,128]{1,0:T(8,128)(2,1)S(1)}, bf16[2048,128]{1,0:T(8,128)(2,1)S(1)}, u32[]{:S(2)}, u32[]{:S(2)}) collective-permute-start(bf16[2048,128]{1,0:T(8,128)(2,1)S(1)} %get-tuple-element.10.refs_2_), channel_id=1, source_target_pairs={{0,4},{2,6},{4,8},{6,10},{8,12},{10,14},{1,5},{3,7},{5,9},{7,11},{... | collective-permute-start | bytes 1572872 | tf_op jit(solution)/shard_map/ppermute | solution.py:119
  7.9 0.0 copy-start.6
  7.9 0.9 %copy-done.6 = bf16[256,512]{1,0:T(8,128)(2,1)S(1)} copy-done((bf16[256,512]{1,0:T(8,128)(2,1)S(1)}, bf16[256,512]{1,0:T(8,128)(2,1)}, u32[]{:S(2)}) %copy-start.6) | copy-done | bytes 262168
  8.9 0.0 copy-start.7
  8.9 0.9 %copy-done.7 = bf16[256,512]{1,0:T(8,128)(2,1)S(1)} copy-done((bf16[256,512]{1,0:T(8,128)(2,1)S(1)}, bf16[256,512]{1,0:T(8,128)(2,1)}, u32[]{:S(2)}) %copy-start.7) | copy-done | bytes 262168
  9.8 0.0 copy-start.8
  9.8 0.8 %copy-done.8 = f32[64,128]{1,0:T(8,128)S(1)} copy-done((f32[64,128]{1,0:T(8,128)S(1)}, f32[64,128]{1,0:T(8,128)}, u32[]{:S(2)}) %copy-start.8) | copy-done | bytes 32792
  10.6 0.0 copy-start.9
  10.6 0.7 %copy-done.9 = f32[32,64]{1,0:T(8,128)S(1)} copy-done((f32[32,64]{1,0:T(8,128)S(1)}, f32[32,64]{1,0:T(8,128)}, u32[]{:S(2)}) %copy-start.9) | copy-done | bytes 8216
  11.3 0.0 copy-start.10
  11.3 0.7 %copy-done.10 = s32[16]{0:T(128)S(1)} copy-done((s32[16]{0:T(128)S(1)}, s32[16]{0:T(128)}, u32[]{:S(2)}) %copy-start.10) | copy-done | bytes 88
  12.0 0.0 copy-start.11
  12.0 0.7 %copy-done.11 = f32[64]{0:T(128)S(1)} copy-done((f32[64]{0:T(128)S(1)}, f32[64]{0:T(128)}, u32[]{:S(2)}) %copy-start.11) | copy-done | bytes 280
  12.6 0.0 copy-start.12
  12.6 0.7 %copy-done.12 = f32[128]{0:T(128)S(1)} copy-done((f32[128]{0:T(128)S(1)}, f32[128]{0:T(128)}, u32[]{:S(2)}) %copy-start.12) | copy-done | bytes 536
  13.3 0.0 copy-start.13
  13.3 0.7 %copy-done.13 = s32[128]{0:T(128)S(1)} copy-done((s32[128]{0:T(128)S(1)}, s32[128]{0:T(128)}, u32[]{:S(2)}) %copy-start.13) | copy-done | bytes 536
  13.9 1.8 %shard_map.154.refs_5_ = f32[128,512]{1,0:T(8,128)S(1)} custom-call(s32[1,16]{1,0:T(1,128)S(1)} %bitcast.5, f32[32,64]{1,0:T(8,128)S(1)} %copy-done.9, f32[1,64]{1,0:T(1,128)S(1)} %bitcast.6, f32[64,128]{1,0:T(8,128)S(1)} %copy-done.8, f32[1,128]{1,0:T(1,128)S(1)} %bitcast.7, s32[1,128]{1,0:T(1,128)S(1)} %bitcast.8, bf16[256,512]{1,0:T(8,128)(2,1)S(1)} %copy-done.7, ...), custom_call_target="tpu_custom_call" | custom-call | tf_op jit(solution)/shard_map/pallas_call | solution.py:124
  15.8 0.5 %collective-permute-done.1.refs_1_ = bf16[2048,128]{1,0:T(8,128)(2,1)S(1)} collective-permute-done((bf16[2048,128]{1,0:T(8,128)(2,1)S(1)}, bf16[2048,128]{1,0:T(8,128)(2,1)S(1)}, u32[]{:S(2)}, u32[]{:S(2)}) %collective-permute-start.1) | collective-permute-done | bytes 524320 | tf_op jit(solution)/shard_map/ppermute | solution.py:119
  16.2 11.2 %collective-permute-done.refs_0_ = bf16[2048,128]{1,0:T(8,128)(2,1)S(1)} collective-permute-done((bf16[2048,128]{1,0:T(8,128)(2,1)S(1)}, bf16[2048,128]{1,0:T(8,128)(2,1)S(1)}, u32[]{:S(2)}, u32[]{:S(2)}) %collective-permute-start) | collective-permute-done | bytes 524320 | tf_op jit(solution)/shard_map/ppermute | solution.py:119
  27.4 0.0 copy-start
  27.4 3.4 %copy-done = bf16[2048,2048]{1,0:T(8,128)(2,1)S(1)} copy-done((bf16[2048,2048]{1,0:T(8,128)(2,1)S(1)}, bf16[2048,2048]{1,0:T(8,128)(2,1)}, u32[]{:S(2)}) %copy-start) | copy-done | bytes 8388632
  30.8 0.0 copy-start.2
  30.8 1.0 %copy-done.2 = bf16[2048,128]{1,0:T(8,128)(2,1)S(1)} copy-done((bf16[2048,128]{1,0:T(8,128)(2,1)S(1)}, bf16[2048,128]{1,0:T(8,128)(2,1)}, u32[]{:S(2)}) %copy-start.2) | copy-done | bytes 524312
  31.8 0.0 copy-start.3
  31.8 1.0 %copy-done.3 = bf16[384,512]{1,0:T(8,128)(2,1)S(1)} copy-done((bf16[384,512]{1,0:T(8,128)(2,1)S(1)}, bf16[384,512]{1,0:T(8,128)(2,1)}, u32[]{:S(2)}) %copy-start.3) | copy-done | bytes 393240
  32.8 0.0 copy-start.4
  32.8 1.0 %copy-done.4 = bf16[384,512]{1,0:T(8,128)(2,1)S(1)} copy-done((bf16[384,512]{1,0:T(8,128)(2,1)S(1)}, bf16[384,512]{1,0:T(8,128)(2,1)}, u32[]{:S(2)}) %copy-start.4) | copy-done | bytes 393240
  33.8 0.0 copy-start.5
  33.8 0.9 %copy-done.5 = bf16[512,256]{1,0:T(8,128)(2,1)S(1)} copy-done((bf16[512,256]{1,0:T(8,128)(2,1)S(1)}, bf16[512,256]{1,0:T(8,128)(2,1)}, u32[]{:S(2)}) %copy-start.5) | copy-done | bytes 262168
  34.8 0.0 copy-start.1
  34.8 8.3 %shard_map.155 = (bf16[128,1024]{1,0:T(8,128)(2,1)S(1)}, bf16[128,2048]{1,0:T(8,128)(2,1)S(1)}) custom-call(s32[1]{0:T(128)} %bitcast.core, bf16[2048,128]{1,0:T(8,128)(2,1)S(1)} %collective-permute-done.refs_0_, bf16[2048,128]{1,0:T(8,128)(2,1)S(1)} %collective-permute-done.1.refs_1_, bf16[2048,128]{1,0:T(8,128)(2,1)S(1)} %get-tuple-element.10.refs_2_, ...), custom_call_target="tpu_custom_call" | custom-call | tf_op jit(solution)/shard_map/pallas_call | solution.py:144
  43.1 1.6 %collective-permute-start.2 = (bf16[128,1024]{1,0:T(8,128)(2,1)S(1)}, bf16[128,1024]{1,0:T(8,128)(2,1)S(1)}, u32[]{:S(2)}, u32[]{:S(2)}) collective-permute-start(bf16[128,1024]{1,0:T(8,128)(2,1)S(1)} %get-tuple-element.8), channel_id=1, source_target_pairs={{0,1},{1,0},{2,3},{3,2},{4,5},{5,4},{6,7},{7,6},{8,9},{9,8},{10,11... | collective-permute-start | bytes 786440 | tf_op jit(solution)/shard_map/ppermute | solution.py:180
  44.7 0.0 copy-done.1
  44.7 2.5 %shard_map.156 = f32[128,1024]{1,0:T(8,128)S(1)} custom-call(s32[1]{0:T(128)} %bitcast.core, bf16[128,2048]{1,0:T(8,128)(2,1)S(1)} %get-tuple-element.7.gated_t, bf16[2048,2048]{1,0:T(8,128)(2,1)S(1)} %copy-done.1), custom_call_target="tpu_custom_call" | custom-call | tf_op jit(solution)/shard_map/pallas_call | solution.py:181
  47.2 0.0 collective-permute-done.2
  47.2 0.8 %add_convert_fusion = bf16[128,1024]{1,0:T(8,128)(2,1)} fusion(f32[128,1024]{1,0:T(8,128)S(1)} %shard_map.156, bf16[128,1024]{1,0:T(8,128)(2,1)S(1)} %collective-permute-done.2), kind=kLoop, calls=%fused_computation.2 | loop fusion | flops 393216 | bytes 1048576 | tf_op jit(solution)/shard_map/convert_element_type | solution.py:195
Async XLA Ops:
  1.6 14.7 %collective-permute-start.1 = (bf16[2048,128]{1,0:T(8,128)(2,1)S(1)}, bf16[2048,128]{1,0:T(8,128)(2,1)S(1)}, u32[]{:S(2)}, u32[]{:S(2)}) collective-permute-start(bf16[2048,128]{1,0:T(8,128)(2,1)S(1)} %get-tuple-element.10.refs_2_), channel_id=1, source_target_pairs={{0,2},{2,4},{4,6},{6,8},{8,10},{10,12},{12,14},{1,3},{3,5},{5,7},{... | collective-permute-start | bytes 1572872 | tf_op jit(solution)/shard_map/ppermute | solution.py:119
  4.7 22.7 %collective-permute-start = (bf16[2048,128]{1,0:T(8,128)(2,1)S(1)}, bf16[2048,128]{1,0:T(8,128)(2,1)S(1)}, u32[]{:S(2)}, u32[]{:S(2)}) collective-permute-start(bf16[2048,128]{1,0:T(8,128)(2,1)S(1)} %get-tuple-element.10.refs_2_), channel_id=1, source_target_pairs={{0,4},{2,6},{4,8},{6,10},{8,12},{10,14},{1,5},{3,7},{5,9},{7,11},{... | collective-permute-start | bytes 1572872 | tf_op jit(solution)/shard_map/ppermute | solution.py:119
  7.9 1.0 %copy-start.6 = (bf16[256,512]{1,0:T(8,128)(2,1)S(1)}, bf16[256,512]{1,0:T(8,128)(2,1)}, u32[]{:S(2)}) copy-start(bf16[256,512]{1,0:T(8,128)(2,1)} %constant.15.clone.refs_7_) | copy-start | bytes 786436
  8.9 0.9 %copy-start.7 = (bf16[256,512]{1,0:T(8,128)(2,1)S(1)}, bf16[256,512]{1,0:T(8,128)(2,1)}, u32[]{:S(2)}) copy-start(bf16[256,512]{1,0:T(8,128)(2,1)} %constant.14.clone.refs_6_) | copy-start | bytes 786436
  9.8 0.8 %copy-start.8 = (f32[64,128]{1,0:T(8,128)S(1)}, f32[64,128]{1,0:T(8,128)}, u32[]{:S(2)}) copy-start(f32[64,128]{1,0:T(8,128)} %refs_3_.2) | copy-start | bytes 98308
  10.6 0.7 %copy-start.9 = (f32[32,64]{1,0:T(8,128)S(1)}, f32[32,64]{1,0:T(8,128)}, u32[]{:S(2)}) copy-start(f32[32,64]{1,0:T(8,128)} %refs_1_.1) | copy-start | bytes 24580
  11.3 0.7 %copy-start.10 = (s32[16]{0:T(128)S(1)}, s32[16]{0:T(128)}, u32[]{:S(2)}) copy-start(s32[16]{0:T(128)} %param.19) | copy-start | bytes 196
  12.0 0.7 %copy-start.11 = (f32[64]{0:T(128)S(1)}, f32[64]{0:T(128)}, u32[]{:S(2)}) copy-start(f32[64]{0:T(128)} %param.21) | copy-start | bytes 772
  12.6 0.7 %copy-start.12 = (f32[128]{0:T(128)S(1)}, f32[128]{0:T(128)}, u32[]{:S(2)}) copy-start(f32[128]{0:T(128)} %param.23) | copy-start | bytes 1540
  13.3 0.7 %copy-start.13 = (s32[128]{0:T(128)S(1)}, s32[128]{0:T(128)}, u32[]{:S(2)}) copy-start(s32[128]{0:T(128)} %param.24) | copy-start | bytes 1540
  27.4 3.4 %copy-start = (bf16[2048,2048]{1,0:T(8,128)(2,1)S(1)}, bf16[2048,2048]{1,0:T(8,128)(2,1)}, u32[]{:S(2)}) copy-start(bf16[2048,2048]{1,0:T(8,128)(2,1)} %weight.1) | copy-start | bytes 25165828
  30.8 1.0 %copy-start.2 = (bf16[2048,128]{1,0:T(8,128)(2,1)S(1)}, bf16[2048,128]{1,0:T(8,128)(2,1)}, u32[]{:S(2)}) copy-start(bf16[2048,128]{1,0:T(8,128)(2,1)} %refs_3_.3) | copy-start | bytes 1572868
  31.8 1.0 %copy-start.3 = (bf16[384,512]{1,0:T(8,128)(2,1)S(1)}, bf16[384,512]{1,0:T(8,128)(2,1)}, u32[]{:S(2)}) copy-start(bf16[384,512]{1,0:T(8,128)(2,1)} %constant.17.clone.refs_7_) | copy-start | bytes 1179652
  32.8 1.0 %copy-start.4 = (bf16[384,512]{1,0:T(8,128)(2,1)S(1)}, bf16[384,512]{1,0:T(8,128)(2,1)}, u32[]{:S(2)}) copy-start(bf16[384,512]{1,0:T(8,128)(2,1)} %constant.16.clone.refs_6_) | copy-start | bytes 1179652
  33.8 0.9 %copy-start.5 = (bf16[512,256]{1,0:T(8,128)(2,1)S(1)}, bf16[512,256]{1,0:T(8,128)(2,1)}, u32[]{:S(2)}) copy-start(bf16[512,256]{1,0:T(8,128)(2,1)} %constant.18.clone.refs_8_) | copy-start | bytes 786436
  34.8 9.9 %copy-start.1 = (bf16[2048,2048]{1,0:T(8,128)(2,1)S(1)}, bf16[2048,2048]{1,0:T(8,128)(2,1)}, u32[]{:S(2)}) copy-start(bf16[2048,2048]{1,0:T(8,128)(2,1)} %weight.1) | copy-start | bytes 25165828
  43.1 4.1 %collective-permute-start.2 = (bf16[128,1024]{1,0:T(8,128)(2,1)S(1)}, bf16[128,1024]{1,0:T(8,128)(2,1)S(1)}, u32[]{:S(2)}, u32[]{:S(2)}) collective-permute-start(bf16[128,1024]{1,0:T(8,128)(2,1)S(1)} %get-tuple-element.8), channel_id=1, source_target_pairs={{0,1},{1,0},{2,3},{3,2},{4,5},{5,4},{6,7},{7,6},{8,9},{9,8},{10,11... | collective-permute-start | bytes 786440 | tf_op jit(solution)/shard_map/ppermute | solution.py:180

commit v2 on v1

v2 whole, which is shorter than its diff:
```python
import math

import jax
import jax.numpy as jnp
import numpy as np
from jax import lax
from jax.experimental import pallas as pl
from jax.experimental.pallas import tpu as pltpu
from jax.sharding import PartitionSpec as P

SETUP_COST = 30_000_000
TAIL_COST = 1
VMEM_BYTES = 24 * 1024 * 1024
PART_A = 768


def split_bf16(array):
    high = array.astype(jnp.bfloat16)
    low = (array - high.astype(np.float64)).astype(jnp.bfloat16)
    return high, low


def transform_tables(window, first_out, block):
    half = 128 * math.ceil(window / 256)
    omega = (np.arange(half) + 0.5) * (math.pi / half)
    angle = np.arange(window)[:, None] * omega[None, :]
    forward = np.concatenate([np.cos(angle), np.sin(angle)], axis=1)
    back = omega[:, None] * (first_out + np.arange(block))[None, :]
    inverse = np.concatenate([np.cos(back), np.sin(back)], axis=0) / half
    return split_bf16(forward), split_bf16(inverse)


def setup_kernel(seq_len, block, scale, *refs):
    small, spectrum, local, sems = refs[:6], refs[10], refs[15:21], refs[21]
    table = refs[11]
    pairs = list(zip(small, local)) + list(zip(refs[6:10], refs[11:15]))
    copies = [pltpu.make_async_copy(source, target, sems.at[k]) for k, (source, target) in enumerate(pairs)]
    for copy in copies:
        copy.start()
    for copy in copies[:7]:
        copy.wait()
    seed, f_in, bias, f_out, decay, reach = local
    window = table.shape[0] // 2 - block
    lags = window - block
    lag = lax.broadcasted_iota(jnp.int32, (lags, 1), 0)
    if seq_len & (seq_len - 1) == 0:
        phases = (lag * seed[...]) & (seq_len - 1)
    else:
        phases = lax.rem(lag * seed[...], seq_len)
    angles = phases.astype(jnp.float32) * (2.0 * math.pi / seq_len)
    features = jnp.concatenate([jnp.cos(angles), jnp.sin(angles)], axis=1)
    exact = dict(precision=lax.Precision.HIGHEST, preferred_element_type=jnp.float32)
    hidden = jnp.sin(jnp.dot(features, f_in[...], **exact) + bias[...])
    shaped = jnp.dot(hidden, f_out[...], **exact)
    envelope = jnp.exp(-decay[...] * lag.astype(jnp.float32)) * scale
    taps = jnp.where(lag < reach[...] * block, shaped * envelope, 0.0).astype(jnp.bfloat16).T
    spectrum[...] = jnp.dot(taps, table[:lags], preferred_element_type=jnp.float32) + jnp.dot(
        taps, table[window : window + lags], preferred_element_type=jnp.float32
    )
    for copy in copies[7:]:
        copy.wait()


def convolve(first, per_group, xs, query, skip, spectrum, table, gated_t):
    channels, block = xs[0].shape
    half = table.shape[1] // 2
    depth = len(xs) * block
    tile = math.gcd(256, channels)
    for start in range(0, channels, tile):
        rows = slice(start, start + tile)
        window = jnp.concatenate([x[rows] for x in xs], axis=1)
        freq = jnp.dot(
            jnp.concatenate([window, window], axis=1), table[: 2 * depth], preferred_element_type=jnp.float32
        )
        mult = []
        for g in range(tile // per_group):
            part = freq[g * per_group : (g + 1) * per_group]
            group = (first + start) // per_group + g
            hc, hs = spectrum[group : group + 1, :half], spectrum[group : group + 1, half:]
            xc, xs_ = part[:, :half], part[:, half:]
            mult.append(jnp.concatenate([xc * hc - xs_ * hs, xc * hs + xs_ * hc], axis=1).astype(jnp.bfloat16))
        both = lax.dot_general(
            jnp.concatenate(mult, axis=0),
            table[2 * depth :],
            (((1,), (1,)), ((), ())),
            preferred_element_type=jnp.float32,
        )
        for low in range(0, tile, 128):
            row = (first + start + low) // 128
            gain = jnp.broadcast_to(skip[row : row + 1], (128, 128)).T
            if block != 128:
                gain = jnp.broadcast_to(gain[:, :1], (128, block))
            near = both[low : low + 128]
            here = slice(start + low, start + low + 128)
            mixed = near[:, :block] + near[:, block:] + gain * xs[-1][here].astype(jnp.float32)
            total = slice(first + start + low, first + start + low + 128)
            gated = (query[total].astype(jnp.float32) * mixed).astype(jnp.bfloat16)
            gated_t[:, here] = gated.T


def column_halves(weight):
    cols = weight.shape[1] // 2
    core = lax.axis_index("chan")
    return [pl.ds(pl.multiple_of(part * cols, 128), cols) for part in (core, 1 - core)]


def first_kernel(reach_max, per_group, *refs):
    xs = refs[: reach_max + 1]
    query, skip, spectrum, table, weight, part, own, gated_t = refs[reach_max + 1 :]
    convolve(0, per_group, xs, query, skip, spectrum, table, gated_t)
    here, there = column_halves(weight)
    depth = gated_t.shape[1]
    part[...] = jnp.dot(gated_t[...], weight[:depth, there], preferred_element_type=jnp.float32)
    own[...] = jnp.dot(gated_t[...], weight[:depth, here], preferred_element_type=jnp.float32)


def second_kernel(reach_max, per_group, first, *refs):
    xs = refs[: reach_max + 1]
    query, skip, spectrum, table, weight, before, part, gated_t = refs[reach_max + 1 :]
    convolve(first, per_group, xs, query, skip, spectrum, table, gated_t)
    depth = gated_t.shape[1]
    there = column_halves(weight)[1]
    total = before[...] + jnp.dot(
        gated_t[...], weight[first : first + depth, there], preferred_element_type=jnp.float32
    )
    part[...] = total.astype(part.dtype)


def own_kernel(first, gated_t, weight, before, out):
    here = column_halves(weight)[0]
    depth = gated_t.shape[1]
    out[...] = before[...] + jnp.dot(
        gated_t[...], weight[first : first + depth, here], preferred_element_type=jnp.float32
    )


def cost(bytes_accessed):
    return pl.CostEstimate(flops=1, bytes_accessed=bytes_accessed, transcendentals=0)


def shift(array, back):
    count = lax.axis_size("seq")
    return lax.ppermute(array, "seq", [(i, i + back) for i in range(count - back)])


def body(
    query_feat,
    key_feat,
    value_feat,
    filter_seed,
    filter_in,
    filter_bias,
    filter_out,
    decay_rate,
    reach_blocks,
    skip_gain,
    out_weight,
):
    channels, block = query_feat.shape
    seq_count = lax.axis_size("seq")
    reach_max = seq_count // 4
    filters = decay_rate.shape[0]
    per_group = channels // filters
    lags = reach_max * block
    window = lags + block
    (fwd_hi, fwd_lo), (inv_hi, inv_lo) = transform_tables(window, lags, block)
    table = np.concatenate([fwd_hi, fwd_lo, inv_hi.T, inv_lo.T], axis=0)
    length = table.shape[1]
    rows, out_cols = out_weight.shape
    cols = out_cols // 2
    params = pltpu.CompilerParams(vmem_limit_bytes=VMEM_BYTES)
    vmem = pl.BlockSpec(memory_space=pltpu.VMEM)
    f32, bf16 = jnp.float32, jnp.bfloat16
    shape = jax.ShapeDtypeStruct

    first = PART_A
    bounds = (slice(0, first), slice(first, channels))
    own_a, own_b = [
        (key_feat[cut].astype(f32) * value_feat[cut].astype(f32)).astype(bf16) for cut in bounds
    ]
    if reach_max == 2:
        far_a = shift(own_a, 2)
        odd = lax.axis_index("seq") % 2 == 1
        near_a = lax.ppermute(jnp.where(odd, far_a, own_a), "seq", [(i, i ^ 1) for i in range(seq_count)])
        halo_a = [far_a, near_a]
        halo_b = [shift(own_b, 2), shift(own_b, 1)]
    else:
        halo_a, halo_b = [[shift(own, back) for back in range(reach_max, 0, -1)] for own in (own_a, own_b)]

    small = (
        filter_seed[None],
        filter_in,
        filter_bias[None],
        filter_out,
        decay_rate[None],
        reach_blocks[None],
    )
    large = (
        jnp.asarray(table),
        out_weight,
        query_feat,
        skip_gain.reshape(-1, 128),
    )
    spectrum, table, weight, query, skip = pl.pallas_call(
        lambda *refs: setup_kernel(block * seq_count, block, 1.0 / math.sqrt(lags), *refs),
        in_specs=[pl.BlockSpec(memory_space=pltpu.HBM)] * 10,
        out_specs=[vmem] * 5,
        out_shape=[pltpu.VMEM((filters, length), f32)] + [pltpu.VMEM(a.shape, a.dtype) for a in large],
        scratch_shapes=[pltpu.VMEM(a.shape, a.dtype) for a in small] + [pltpu.SemaphoreType.DMA((10,))],
        compiler_params=params,
        cost_estimate=cost(SETUP_COST),
    )(*[pltpu.with_memory_space_constraint(a, pltpu.HBM) for a in small + large])
    common = (query, skip, spectrum, table)
    part_a, total_a = pl.pallas_call(
        lambda *refs: first_kernel(reach_max, per_group, *refs),
        in_specs=[vmem] * (reach_max + 6),
        out_specs=[vmem] * 2,
        out_shape=[shape((block, cols), f32)] * 2,
        scratch_shapes=[pltpu.VMEM((block, first), bf16)],
        compiler_params=params,
        cost_estimate=cost(TAIL_COST),
    )(*halo_a, own_a, *common, weight)
    part, gated_b = pl.pallas_call(
        lambda *refs: second_kernel(reach_max, per_group, first, *refs),
        in_specs=[vmem] * (reach_max + 7),
        out_specs=[vmem] * 2,
        out_shape=[shape((block, cols), bf16), shape((block, channels - first), bf16)],
        compiler_params=params,
        cost_estimate=cost(TAIL_COST),
    )(*halo_b, own_b, *common, weight, part_a)
    received = lax.ppermute(part, "chan", [(0, 1), (1, 0)])
    own = pl.pallas_call(
        lambda *refs: own_kernel(first, *refs),
        in_specs=[vmem] * 3,
        out_specs=vmem,
        out_shape=shape((block, cols), f32),
        compiler_params=params,
        cost_estimate=cost(TAIL_COST),
    )(gated_b, weight, total_a)
    return (own + received.astype(f32)).astype(bf16)


def solution(mesh):
    return jax.shard_map(
        body,
        mesh=mesh,
        in_specs=(
            P("chan", ("groups", "seq")),
            P("chan", ("groups", "seq")),
            P("chan", ("groups", "seq")),
            P(),
            P(),
            P(),
            P(None, "chan"),
            P("chan"),
            P("chan"),
            P("chan"),
            P("chan", None),
        ),
        out_specs=P(("groups", "seq"), "chan"),
        check_vma=False,
    )
```

time: 48.5 us -> 29.6 us (0.61)
  the two profiles are of different devices: /device:TPU:15 before, /device:TPU:9 now
where the time goes in v2:
time: 29.6 us; the launch traced here: 29.4 us
  starting transfers between devices  10.2 us (34%)
  Pallas kernels  9.22 us (31%)
  waiting for transfers between devices  6.82 us (23%)
  other arithmetic  3.02 us (10%)
    ppermute x3, starting transfers between devices, shift(): lax.ppermute(array, 'seq', [(i, i + back) for i in range(count - back)])  9.56 us
    ppermute x1, waiting for transfers between devices, body(): lax.ppermute(jnp.where(odd, far_a, own_a), 'seq', [(i, i ^ 1) for i in ra...  6.18 us
    pallas_call x1, Pallas kernels, body(): pl.pallas_call(lambda *refs: setup_kernel(block * seq_count, block, 1.0 /...  3.94 us
    pallas_call x1, Pallas kernels, body(): pl.pallas_call(lambda *refs: second_kernel(reach_max, per_group, first, *...  2.67 us
    convert_element_type x2, other arithmetic, body(): (key_feat[cut].astype(f32) * value_feat[cut].astype(f32)).astype(bf16)  2.24 us
    pallas_call x1, Pallas kernels, body(): pl.pallas_call(lambda *refs: first_kernel(reach_max, per_group, *refs), i...  2.09 us
    convert_element_type x1, other arithmetic, body(): return (own + received.astype(f32)).astype(bf16)  0.76 us
    ppermute x1, waiting for transfers between devices, body(): received = lax.ppermute(part, 'chan', [(0, 1), (1, 0)])  0.63 us
  transfers between devices with their start and end apart: 5, of which 2 were waited for; matrix products, arithmetic and copies ran while one was open for 4% of the time, Pallas kernels for 22%

profile of v2, /device:TPU:9, one launch (start us, length us, event | category | flops | bytes accessed | tf_op | source)
XLA Modules:
  0.0 29.4 jit_solution(2700903904777323372)
XLA Ops:
  0.0 1.1 %multiply_convert_fusion.1.refs_2_ = bf16[768,128]{1,0:T(8,128)(2,1)S(1)} fusion(bf16[2048,128]{1,0:T(8,128)(2,1)} %param.14, bf16[2048,128]{1,0:T(8,128)(2,1)} %param.13), kind=kLoop, calls=%fused_computation.2 | loop fusion | flops 393216 | bytes 589824 | tf_op jit(solution)/shard_map/convert_element_type | solution.py:179
  1.1 3.2 %collective-permute-start.2 = (bf16[768,128]{1,0:T(8,128)(2,1)S(1)}, bf16[768,128]{1,0:T(8,128)(2,1)S(1)}, u32[]{:S(2)}, u32[]{:S(2)}) collective-permute-start(bf16[768,128]{1,0:T(8,128)(2,1)S(1)} %multiply_convert_fusion.1.refs_2_), channel_id=1, source_target_pairs={{0,4},{2,6},{4,8},{6,10},{8,12},{10,14},{1,5},{3,7},{5,9},{7,11},{... | collective-permute-start | bytes 589832 | tf_op jit(solution)/shard_map/ppermute | solution.py:143
  4.3 1.2 %multiply_convert_fusion.refs_2_ = bf16[1280,128]{1,0:T(8,128)(2,1)S(1)} fusion(bf16[2048,128]{1,0:T(8,128)(2,1)} %param.14, bf16[2048,128]{1,0:T(8,128)(2,1)} %param.13), kind=kLoop, calls=%fused_computation | loop fusion | flops 655360 | bytes 983040 | tf_op jit(solution)/shard_map/convert_element_type | solution.py:179
  5.5 3.1 %collective-permute-start.1 = (bf16[1280,128]{1,0:T(8,128)(2,1)S(1)}, bf16[1280,128]{1,0:T(8,128)(2,1)S(1)}, u32[]{:S(2)}, u32[]{:S(2)}) collective-permute-start(bf16[1280,128]{1,0:T(8,128)(2,1)S(1)} %multiply_convert_fusion.refs_2_), channel_id=1, source_target_pairs={{0,2},{2,4},{4,6},{6,8},{8,10},{10,12},{12,14},{1,3},{3,5},{5,7},{... | collective-permute-start | bytes 983048 | tf_op jit(solution)/shard_map/ppermute | solution.py:143
  8.6 3.2 %collective-permute-start = (bf16[1280,128]{1,0:T(8,128)(2,1)S(1)}, bf16[1280,128]{1,0:T(8,128)(2,1)S(1)}, u32[]{:S(2)}, u32[]{:S(2)}) collective-permute-start(bf16[1280,128]{1,0:T(8,128)(2,1)S(1)} %multiply_convert_fusion.refs_2_), channel_id=1, source_target_pairs={{0,4},{2,6},{4,8},{6,10},{8,12},{10,14},{1,5},{3,7},{5,9},{7,11},{... | collective-permute-start | bytes 983048 | tf_op jit(solution)/shard_map/ppermute | solution.py:143
  11.8 0.0 collective-permute-done.2.refs_0_
  11.9 0.1 collective-permute-start.3
  12.0 3.9 %shard_map.118 = (f32[128,512]{1,0:T(8,128)S(1)}, bf16[1024,512]{1,0:T(8,128)(2,1)S(1)}, bf16[2048,2048]{1,0:T(8,128)(2,1)S(1)}, bf16[2048,128]{1,0:T(8,128)(2,1)S(1)}, f32[16,128]{1,0:T(8,128)S(1)}) custom-call(s32[1,16]{1,0:T(1,128)} %bitcast.6, f32[32,64]{1,0:T(8,128)} %refs_1_.1, f32[1,64]{1,0:T(1,128)} %bitcast.7, f32[64,128]{1,0:T(8,128)} %refs_3_.1, ...), custom_call_target="tpu_custom_call" | custom-call | flops 1 | bytes 30000000 | tf_op jit(solution)/shard_map/pallas_call | solution.py:204
  15.9 6.2 %collective-permute-done.3.refs_1_ = bf16[768,128]{1,0:T(8,128)(2,1)S(1)} collective-permute-done((bf16[768,128]{1,0:T(8,128)(2,1)S(1)}, bf16[768,128]{1,0:T(8,128)(2,1)S(1)}, u32[]{:S(2)}, u32[]{:S(2)}) %collective-permute-start.3) | collective-permute-done | bytes 196640 | tf_op jit(solution)/shard_map/ppermute | solution.py:184
  22.1 2.1 %shard_map.119 = (f32[128,1024]{1,0:T(8,128)S(1)}, f32[128,1024]{1,0:T(8,128)S(1)}) custom-call(bf16[768,128]{1,0:T(8,128)(2,1)S(1)} %collective-permute-done.2.refs_0_, bf16[768,128]{1,0:T(8,128)(2,1)S(1)} %collective-permute-done.3.refs_1_, bf16[768,128]{1,0:T(8,128)(2,1)S(1)} %multiply_convert_fusion.1.refs_2_, ...), custom_call_target="tpu_custom_call" | custom-call | flops 1 | bytes 1 | tf_op jit(solution)/shard_map/pallas_call | solution.py:214
  24.2 0.0 collective-permute-done.1.refs_1_
  24.2 0.0 collective-permute-done.refs_0_
  24.2 2.7 %shard_map.120 = (bf16[128,1024]{1,0:T(8,128)(2,1)S(1)}, bf16[128,1280]{1,0:T(8,128)(2,1)S(1)}) custom-call(bf16[1280,128]{1,0:T(8,128)(2,1)S(1)} %collective-permute-done.refs_0_, bf16[1280,128]{1,0:T(8,128)(2,1)S(1)} %collective-permute-done.1.refs_1_, bf16[1280,128]{1,0:T(8,128)(2,1)S(1)} %multiply_convert_fusion.refs_2_, ...), custom_call_target="tpu_custom_call" | custom-call | flops 1 | bytes 1 | tf_op jit(solution)/shard_map/pallas_call | solution.py:223
  26.9 0.6 %collective-permute-start.4 = (bf16[128,1024]{1,0:T(8,128)(2,1)S(1)}, bf16[128,1024]{1,0:T(8,128)(2,1)S(1)}, u32[]{:S(2)}, u32[]{:S(2)}) collective-permute-start(bf16[128,1024]{1,0:T(8,128)(2,1)S(1)} %get-tuple-element.22), channel_id=1, source_target_pairs={{0,1},{1,0},{2,3},{3,2},{4,5},{5,4},{6,7},{7,6},{8,9},{9,8},{10,11... | collective-permute-start | bytes 786440 | tf_op jit(solution)/shard_map/ppermute | solution.py:231
  27.5 0.5 %shard_map.121 = f32[128,1024]{1,0:T(8,128)S(1)} custom-call(bf16[128,1280]{1,0:T(8,128)(2,1)S(1)} %get-tuple-element.20.refs_0_, bf16[2048,2048]{1,0:T(8,128)(2,1)S(1)} %get-tuple-element.18.refs_7_.refs_1_, f32[128,1024]{1,0:T(8,128)S(1)} %get-tuple-element.21.refs_2_), custom_call_target="tpu_custom_call" | custom-call | flops 1 | bytes 1 | tf_op jit(solution)/shard_map/pallas_call | solution.py:232
  28.0 0.6 %collective-permute-done.4 = bf16[128,1024]{1,0:T(8,128)(2,1)S(1)} collective-permute-done((bf16[128,1024]{1,0:T(8,128)(2,1)S(1)}, bf16[128,1024]{1,0:T(8,128)(2,1)S(1)}, u32[]{:S(2)}, u32[]{:S(2)}) %collective-permute-start.4) | collective-permute-done | bytes 262176 | tf_op jit(solution)/shard_map/ppermute | solution.py:231
  28.6 0.8 %add_convert_fusion = bf16[128,1024]{1,0:T(8,128)(2,1)} fusion(f32[128,1024]{1,0:T(8,128)S(1)} %shard_map.121, bf16[128,1024]{1,0:T(8,128)(2,1)S(1)} %collective-permute-done.4), kind=kLoop, calls=%fused_computation.1 | loop fusion | flops 393216 | bytes 1048576 | tf_op jit(solution)/shard_map/convert_element_type | solution.py:240
  (1 shorter events, 0.0 us)
Async XLA Ops:
  1.1 10.8 %collective-permute-start.2 = (bf16[768,128]{1,0:T(8,128)(2,1)S(1)}, bf16[768,128]{1,0:T(8,128)(2,1)S(1)}, u32[]{:S(2)}, u32[]{:S(2)}) collective-permute-start(bf16[768,128]{1,0:T(8,128)(2,1)S(1)} %multiply_convert_fusion.1.refs_2_), channel_id=1, source_target_pairs={{0,4},{2,6},{4,8},{6,10},{8,12},{10,14},{1,5},{3,7},{5,9},{7,11},{... | collective-permute-start | bytes 589832 | tf_op jit(solution)/shard_map/ppermute | solution.py:143
  5.5 18.7 %collective-permute-start.1 = (bf16[1280,128]{1,0:T(8,128)(2,1)S(1)}, bf16[1280,128]{1,0:T(8,128)(2,1)S(1)}, u32[]{:S(2)}, u32[]{:S(2)}) collective-permute-start(bf16[1280,128]{1,0:T(8,128)(2,1)S(1)} %multiply_convert_fusion.refs_2_), channel_id=1, source_target_pairs={{0,2},{2,4},{4,6},{6,8},{8,10},{10,12},{12,14},{1,3},{3,5},{5,7},{... | collective-permute-start | bytes 983048 | tf_op jit(solution)/shard_map/ppermute | solution.py:143
  8.6 15.6 %collective-permute-start = (bf16[1280,128]{1,0:T(8,128)(2,1)S(1)}, bf16[1280,128]{1,0:T(8,128)(2,1)S(1)}, u32[]{:S(2)}, u32[]{:S(2)}) collective-permute-start(bf16[1280,128]{1,0:T(8,128)(2,1)S(1)} %multiply_convert_fusion.refs_2_), channel_id=1, source_target_pairs={{0,4},{2,6},{4,8},{6,10},{8,12},{10,14},{1,5},{3,7},{5,9},{7,11},{... | collective-permute-start | bytes 983048 | tf_op jit(solution)/shard_map/ppermute | solution.py:143
  11.9 10.2 %collective-permute-start.3 = (bf16[768,128]{1,0:T(8,128)(2,1)S(1)}, bf16[768,128]{1,0:T(8,128)(2,1)S(1)}, u32[]{:S(2)}, u32[]{:S(2)}) collective-permute-start(bf16[768,128]{1,0:T(8,128)(2,1)S(1)} %broadcast_select_fusion), channel_id=1, source_target_pairs={{0,2},{2,0},{4,6},{6,4},{8,10},{10,8},{12,14},{14,12},{1,3},{3,1},... | collective-permute-start | bytes 589832 | tf_op jit(solution)/shard_map/ppermute | solution.py:184
  26.9 1.7 %collective-permute-start.4 = (bf16[128,1024]{1,0:T(8,128)(2,1)S(1)}, bf16[128,1024]{1,0:T(8,128)(2,1)S(1)}, u32[]{:S(2)}, u32[]{:S(2)}) collective-permute-start(bf16[128,1024]{1,0:T(8,128)(2,1)S(1)} %get-tuple-element.22), channel_id=1, source_target_pairs={{0,1},{1,0},{2,3},{3,2},{4,5},{5,4},{6,7},{7,6},{8,9},{9,8},{10,11... | collective-permute-start | bytes 786440 | tf_op jit(solution)/shard_map/ppermute | solution.py:231

commit v3 on v2

--- a/solution.py
+++ b/solution.py
@@ -1,3 +1,4 @@
+import functools
 import math
 
 import jax
@@ -11,7 +12,10 @@
 SETUP_COST = 30_000_000
 TAIL_COST = 1
 VMEM_BYTES = 24 * 1024 * 1024
-PART_A = 768
+PARTS = (0, 768, 2048)
+RELAYED = (True, False)
+WRAP_FAR = True
+WRAP_DIRECT = False
 
 
 def split_bf16(array):
@@ -65,12 +69,16 @@
     channels, block = xs[0].shape
     half = table.shape[1] // 2
     depth = len(xs) * block
-    tile = math.gcd(256, channels)
-    for start in range(0, channels, tile):
+    seq = lax.axis_index("seq")
+    for start in range(0, channels, 256):
+        tile = min(256, channels - start)
         rows = slice(start, start + tile)
-        window = jnp.concatenate([x[rows] for x in xs], axis=1)
+        blocks = [
+            jnp.where(seq >= len(xs) - 1 - k, x[rows], jnp.zeros((tile, block), x.dtype))
+            for k, x in enumerate(xs[:-1])
+        ] + [xs[-1][rows]]
         freq = jnp.dot(
-            jnp.concatenate([window, window], axis=1), table[: 2 * depth], preferred_element_type=jnp.float32
+            jnp.concatenate(blocks + blocks, axis=1), table[: 2 * depth], preferred_element_type=jnp.float32
         )
         mult = []
         for g in range(tile // per_group):
@@ -104,26 +112,19 @@
     return [pl.ds(pl.multiple_of(part * cols, 128), cols) for part in (core, 1 - core)]
 
 
-def first_kernel(reach_max, per_group, *refs):
-    xs = refs[: reach_max + 1]
-    query, skip, spectrum, table, weight, part, own, gated_t = refs[reach_max + 1 :]
-    convolve(0, per_group, xs, query, skip, spectrum, table, gated_t)
+def part_kernel(blocks, per_group, first, is_first, is_last, *refs):
+    xs, refs = refs[:blocks], refs[blocks:]
+    (query, skip, spectrum, table, weight), refs = refs[:5], refs[5:]
+    before, refs = ((), refs) if is_first else (refs[:1] if is_last else refs[:2], refs[1 if is_last else 2 :])
+    outs, gated_t = refs[:-1], refs[-1]
+    convolve(first, per_group, xs, query, skip, spectrum, table, gated_t)
     here, there = column_halves(weight)
-    depth = gated_t.shape[1]
-    part[...] = jnp.dot(gated_t[...], weight[:depth, there], preferred_element_type=jnp.float32)
-    own[...] = jnp.dot(gated_t[...], weight[:depth, here], preferred_element_type=jnp.float32)
-
-
-def second_kernel(reach_max, per_group, first, *refs):
-    xs = refs[: reach_max + 1]
-    query, skip, spectrum, table, weight, before, part, gated_t = refs[reach_max + 1 :]
-    convolve(first, per_group, xs, query, skip, spectrum, table, gated_t)
-    depth = gated_t.shape[1]
-    there = column_halves(weight)[1]
-    total = before[...] + jnp.dot(
-        gated_t[...], weight[first : first + depth, there], preferred_element_type=jnp.float32
-    )
-    part[...] = total.astype(part.dtype)
+    rows = slice(first, first + gated_t.shape[1])
+    for k, columns in enumerate((there,) if is_last else (there, here)):
+        total = jnp.dot(gated_t[...], weight[rows, columns], preferred_element_type=jnp.float32)
+        if before:
+            total = before[k][...] + total
+        outs[k][...] = total.astype(outs[k].dtype)
 
 
 def own_kernel(first, gated_t, weight, before, out):
@@ -138,9 +139,13 @@
     return pl.CostEstimate(flops=1, bytes_accessed=bytes_accessed, transcendentals=0)
 
 
-def shift(array, back):
+def shift(array, back, cyclic):
     count = lax.axis_size("seq")
-    return lax.ppermute(array, "seq", [(i, i + back) for i in range(count - back)])
+    return lax.ppermute(array, "seq", [(i, (i + back) % count) for i in range(count if cyclic else count - back)])
+
+
+def swap_pairs(array):
+    return lax.ppermute(array, "seq", [(i, i ^ 1) for i in range(lax.axis_size("seq"))])
 
 
 def body(
@@ -166,26 +171,26 @@
     (fwd_hi, fwd_lo), (inv_hi, inv_lo) = transform_tables(window, lags, block)
     table = np.concatenate([fwd_hi, fwd_lo, inv_hi.T, inv_lo.T], axis=0)
     length = table.shape[1]
-    rows, out_cols = out_weight.shape
+    out_cols = out_weight.shape[1]
     cols = out_cols // 2
     params = pltpu.CompilerParams(vmem_limit_bytes=VMEM_BYTES)
     vmem = pl.BlockSpec(memory_space=pltpu.VMEM)
     f32, bf16 = jnp.float32, jnp.bfloat16
     shape = jax.ShapeDtypeStruct
 
-    first = PART_A
-    bounds = (slice(0, first), slice(first, channels))
-    own_a, own_b = [
-        (key_feat[cut].astype(f32) * value_feat[cut].astype(f32)).astype(bf16) for cut in bounds
+    bounds = list(zip(PARTS[:-1], PARTS[1:]))
+    products = [
+        (key_feat[low:high].astype(f32) * value_feat[low:high].astype(f32)).astype(bf16) for low, high in bounds
     ]
-    if reach_max == 2:
-        far_a = shift(own_a, 2)
-        odd = lax.axis_index("seq") % 2 == 1
-        near_a = lax.ppermute(jnp.where(odd, far_a, own_a), "seq", [(i, i ^ 1) for i in range(seq_count)])
-        halo_a = [far_a, near_a]
-        halo_b = [shift(own_b, 2), shift(own_b, 1)]
-    else:
-        halo_a, halo_b = [[shift(own, back) for back in range(reach_max, 0, -1)] for own in (own_a, own_b)]
+    odd = lax.axis_index("seq") % 2 == 1
+    windows = []
+    for own, relayed in zip(products, RELAYED):
+        if reach_max == 2 and relayed:
+            far = shift(own, 2, WRAP_FAR)
+            near = swap_pairs(jnp.where(odd, far, own))
+            windows.append([far, near, own])
+        else:
+            windows.append([shift(own, back, WRAP_DIRECT) for back in range(reach_max, 0, -1)] + [own])
 
     small = (
         filter_seed[None],
@@ -210,33 +215,37 @@
         compiler_params=params,
         cost_estimate=cost(SETUP_COST),
     )(*[pltpu.with_memory_space_constraint(a, pltpu.HBM) for a in small + large])
-    common = (query, skip, spectrum, table)
-    part_a, total_a = pl.pallas_call(
-        lambda *refs: first_kernel(reach_max, per_group, *refs),
-        in_specs=[vmem] * (reach_max + 6),
-        out_specs=[vmem] * 2,
-        out_shape=[shape((block, cols), f32)] * 2,
-        scratch_shapes=[pltpu.VMEM((block, first), bf16)],
-        compiler_params=params,
-        cost_estimate=cost(TAIL_COST),
-    )(*halo_a, own_a, *common, weight)
-    part, gated_b = pl.pallas_call(
-        lambda *refs: second_kernel(reach_max, per_group, first, *refs),
-        in_specs=[vmem] * (reach_max + 7),
-        out_specs=[vmem] * 2,
-        out_shape=[shape((block, cols), bf16), shape((block, channels - first), bf16)],
-        compiler_params=params,
-        cost_estimate=cost(TAIL_COST),
-    )(*halo_b, own_b, *common, weight, part_a)
+
+    common = (query, skip, spectrum, table, weight)
+    sums = ()
+    for k, ((low, high), blocks) in enumerate(zip(bounds, windows)):
+        is_first, is_last = k == 0, k == len(bounds) - 1
+        operands = (*blocks, *common, *(sums[:1] if is_last else sums))
+        gated_shape = (block, high - low)
+        results = pl.pallas_call(
+            functools.partial(part_kernel, len(blocks), per_group, low, is_first, is_last),
+            in_specs=[vmem] * len(operands),
+            out_specs=[vmem] * 2,
+            out_shape=[shape((block, cols), bf16), shape(gated_shape, bf16)]
+            if is_last
+            else [shape((block, cols), f32)] * 2,
+            scratch_shapes=[] if is_last else [pltpu.VMEM(gated_shape, bf16)],
+            compiler_params=params,
+            cost_estimate=cost(TAIL_COST),
+        )(*operands)
+        if is_last:
+            part, gated = results
+        else:
+            sums = results
     received = lax.ppermute(part, "chan", [(0, 1), (1, 0)])
     own = pl.pallas_call(
-        lambda *refs: own_kernel(first, *refs),
+        functools.partial(own_kernel, bounds[-1][0]),
         in_specs=[vmem] * 3,
         out_specs=vmem,
         out_shape=shape((block, cols), f32),
         compiler_params=params,
         cost_estimate=cost(TAIL_COST),
-    )(gated_b, weight, total_a)
+    )(gated, weight, sums[1])
     return (own + received.astype(f32)).astype(bf16)
 
 

time: 29.6 us -> 27.7 us (0.936)
  starting transfers between devices: 10.2 us -> 8.35 us
    ppermute x4, starting transfers between devices: 9.63 us -> 7.78 us  [the longest x3 7.7 us: shift(): lax.ppermute(array, 'seq', [(i, (i + back) % count) for i in range(count...]
  transfers between devices with their start and end apart: 5 -> 5, of which waited for: 2 -> 2; matrix products, arithmetic and copies ran while one was open for 4% -> 4% of each run, Pallas kernels for 22% -> 24%
where the time goes in v3:
time: 27.7 us; the launch traced here: 27.5 us
  Pallas kernels  9.23 us (33%)
  starting transfers between devices  8.35 us (30%)
  waiting for transfers between devices  6.82 us (25%)
  other arithmetic  3.02 us (11%)
    ppermute x3, starting transfers between devices, shift(): lax.ppermute(array, 'seq', [(i, (i + back) % count) for i in range(count...  7.7 us
    ppermute x1, waiting for transfers between devices, swap_pairs(): lax.ppermute(array, 'seq', [(i, i ^ 1) for i in range(lax.axis_size('seq'...  6.18 us
    pallas_call x2, Pallas kernels, body(): pl.pallas_call(functools.partial(part_kernel, len(blocks), per_group, low...  4.76 us
    pallas_call x1, Pallas kernels, body(): pl.pallas_call(lambda *refs: setup_kernel(block * seq_count, block, 1.0 /...  3.94 us
    convert_element_type x2, other arithmetic, body(): (key_feat[low:high].astype(f32) * value_feat[low:high].astype(f32)).astyp...  2.23 us
    convert_element_type x1, other arithmetic, body(): return (own + received.astype(f32)).astype(bf16)  0.76 us
    ppermute x1, waiting for transfers between devices, body(): received = lax.ppermute(part, 'chan', [(0, 1), (1, 0)])  0.63 us
    ppermute x1, starting transfers between devices, body(): received = lax.ppermute(part, 'chan', [(0, 1), (1, 0)])  0.57 us
  transfers between devices with their start and end apart: 5, of which 2 were waited for; matrix products, arithmetic and copies ran while one was open for 4% of the time, Pallas kernels for 24%

profile of v3, /device:TPU:9, one launch (start us, length us, event | category | flops | bytes accessed | tf_op | source)
XLA Modules:
  0.0 27.5 jit_solution(11663712308948049268)
XLA Ops:
  0.0 1.1 %multiply_convert_fusion.1.refs_2_ = bf16[768,128]{1,0:T(8,128)(2,1)S(1)} fusion(bf16[2048,128]{1,0:T(8,128)(2,1)} %param.14, bf16[2048,128]{1,0:T(8,128)(2,1)} %param.13), kind=kLoop, calls=%fused_computation.2 | loop fusion | flops 393216 | bytes 589824 | tf_op jit(solution)/shard_map/convert_element_type | solution.py:183
  1.1 1.3 %collective-permute-start.2 = (bf16[768,128]{1,0:T(8,128)(2,1)S(1)}, bf16[768,128]{1,0:T(8,128)(2,1)S(1)}, u32[]{:S(2)}, u32[]{:S(2)}) collective-permute-start(bf16[768,128]{1,0:T(8,128)(2,1)S(1)} %multiply_convert_fusion.1.refs_2_), channel_id=1, source_target_pairs={{0,4},{2,6},{4,8},{6,10},{8,12},{10,14},{12,0},{14,2},{1,5},{3,7},... | collective-permute-start | bytes 589832 | tf_op jit(solution)/shard_map/ppermute | solution.py:144
  2.4 1.2 %multiply_convert_fusion.refs_2_ = bf16[1280,128]{1,0:T(8,128)(2,1)S(1)} fusion(bf16[2048,128]{1,0:T(8,128)(2,1)} %param.14, bf16[2048,128]{1,0:T(8,128)(2,1)} %param.13), kind=kLoop, calls=%fused_computation | loop fusion | flops 655360 | bytes 983040 | tf_op jit(solution)/shard_map/convert_element_type | solution.py:183
  3.6 3.1 %collective-permute-start.1 = (bf16[1280,128]{1,0:T(8,128)(2,1)S(1)}, bf16[1280,128]{1,0:T(8,128)(2,1)S(1)}, u32[]{:S(2)}, u32[]{:S(2)}) collective-permute-start(bf16[1280,128]{1,0:T(8,128)(2,1)S(1)} %multiply_convert_fusion.refs_2_), channel_id=1, source_target_pairs={{0,2},{2,4},{4,6},{6,8},{8,10},{10,12},{12,14},{1,3},{3,5},{5,7},{... | collective-permute-start | bytes 983048 | tf_op jit(solution)/shard_map/ppermute | solution.py:144
  6.7 3.2 %collective-permute-start = (bf16[1280,128]{1,0:T(8,128)(2,1)S(1)}, bf16[1280,128]{1,0:T(8,128)(2,1)S(1)}, u32[]{:S(2)}, u32[]{:S(2)}) collective-permute-start(bf16[1280,128]{1,0:T(8,128)(2,1)S(1)} %multiply_convert_fusion.refs_2_), channel_id=1, source_target_pairs={{0,4},{2,6},{4,8},{6,10},{8,12},{10,14},{1,5},{3,7},{5,9},{7,11},{... | collective-permute-start | bytes 983048 | tf_op jit(solution)/shard_map/ppermute | solution.py:144
  10.0 0.0 collective-permute-done.2.refs_0_
  10.0 0.1 collective-permute-start.3
  10.1 3.9 %shard_map.118 = (f32[128,512]{1,0:T(8,128)S(1)}, bf16[1024,512]{1,0:T(8,128)(2,1)S(1)}, bf16[2048,2048]{1,0:T(8,128)(2,1)S(1)}, bf16[2048,128]{1,0:T(8,128)(2,1)S(1)}, f32[16,128]{1,0:T(8,128)S(1)}) custom-call(s32[1,16]{1,0:T(1,128)} %bitcast.6, f32[32,64]{1,0:T(8,128)} %refs_1_.1, f32[1,64]{1,0:T(1,128)} %bitcast.7, f32[64,128]{1,0:T(8,128)} %refs_3_.1, ...), custom_call_target="tpu_custom_call" | custom-call | flops 1 | bytes 30000000 | tf_op jit(solution)/shard_map/pallas_call | solution.py:209
  14.0 6.2 %collective-permute-done.3.refs_1_ = bf16[768,128]{1,0:T(8,128)(2,1)S(1)} collective-permute-done((bf16[768,128]{1,0:T(8,128)(2,1)S(1)}, bf16[768,128]{1,0:T(8,128)(2,1)S(1)}, u32[]{:S(2)}, u32[]{:S(2)}) %collective-permute-start.3) | collective-permute-done | bytes 196640 | tf_op jit(solution)/shard_map/ppermute | solution.py:148
  20.2 2.1 %shard_map.119 = (f32[128,1024]{1,0:T(8,128)S(1)}, f32[128,1024]{1,0:T(8,128)S(1)}) custom-call(bf16[768,128]{1,0:T(8,128)(2,1)S(1)} %collective-permute-done.2.refs_0_, bf16[768,128]{1,0:T(8,128)(2,1)S(1)} %collective-permute-done.3.refs_1_, bf16[768,128]{1,0:T(8,128)(2,1)S(1)} %multiply_convert_fusion.1.refs_2_, ...), custom_call_target="tpu_custom_call" | custom-call | flops 1 | bytes 1 | tf_op jit(solution)/shard_map/pallas_call | solution.py:225
  22.3 0.0 collective-permute-done.1.refs_1_
  22.3 0.0 collective-permute-done.refs_0_
  22.3 2.7 %shard_map.120 = (bf16[128,1024]{1,0:T(8,128)(2,1)S(1)}, bf16[128,1280]{1,0:T(8,128)(2,1)S(1)}) custom-call(bf16[1280,128]{1,0:T(8,128)(2,1)S(1)} %collective-permute-done.refs_0_, bf16[1280,128]{1,0:T(8,128)(2,1)S(1)} %collective-permute-done.1.refs_1_, bf16[1280,128]{1,0:T(8,128)(2,1)S(1)} %multiply_convert_fusion.refs_2_, ...), custom_call_target="tpu_custom_call" | custom-call | flops 1 | bytes 1 | tf_op jit(solution)/shard_map/pallas_call | solution.py:225
  25.0 0.6 %collective-permute-start.4 = (bf16[128,1024]{1,0:T(8,128)(2,1)S(1)}, bf16[128,1024]{1,0:T(8,128)(2,1)S(1)}, u32[]{:S(2)}, u32[]{:S(2)}) collective-permute-start(bf16[128,1024]{1,0:T(8,128)(2,1)S(1)} %get-tuple-element.22), channel_id=1, source_target_pairs={{0,1},{1,0},{2,3},{3,2},{4,5},{5,4},{6,7},{7,6},{8,9},{9,8},{10,11... | collective-permute-start | bytes 786440 | tf_op jit(solution)/shard_map/ppermute | solution.py:240
  25.6 0.5 %shard_map.121 = f32[128,1024]{1,0:T(8,128)S(1)} custom-call(bf16[128,1280]{1,0:T(8,128)(2,1)S(1)} %get-tuple-element.20.gated_t, bf16[2048,2048]{1,0:T(8,128)(2,1)S(1)} %get-tuple-element.18.refs_7_.weight, f32[128,1024]{1,0:T(8,128)S(1)} %get-tuple-element.21.before), custom_call_target="tpu_custom_call" | custom-call | flops 1 | bytes 1 | tf_op jit(solution)/shard_map/pallas_call | solution.py:241
  26.1 0.6 %collective-permute-done.4 = bf16[128,1024]{1,0:T(8,128)(2,1)S(1)} collective-permute-done((bf16[128,1024]{1,0:T(8,128)(2,1)S(1)}, bf16[128,1024]{1,0:T(8,128)(2,1)S(1)}, u32[]{:S(2)}, u32[]{:S(2)}) %collective-permute-start.4) | collective-permute-done | bytes 262176 | tf_op jit(solution)/shard_map/ppermute | solution.py:240
  26.8 0.8 %add_convert_fusion = bf16[128,1024]{1,0:T(8,128)(2,1)} fusion(f32[128,1024]{1,0:T(8,128)S(1)} %shard_map.121, bf16[128,1024]{1,0:T(8,128)(2,1)S(1)} %collective-permute-done.4), kind=kLoop, calls=%fused_computation.1 | loop fusion | flops 393216 | bytes 1048576 | tf_op jit(solution)/shard_map/convert_element_type | solution.py:249
  (1 shorter events, 0.0 us)
Async XLA Ops:
  1.1 8.9 %collective-permute-start.2 = (bf16[768,128]{1,0:T(8,128)(2,1)S(1)}, bf16[768,128]{1,0:T(8,128)(2,1)S(1)}, u32[]{:S(2)}, u32[]{:S(2)}) collective-permute-start(bf16[768,128]{1,0:T(8,128)(2,1)S(1)} %multiply_convert_fusion.1.refs_2_), channel_id=1, source_target_pairs={{0,4},{2,6},{4,8},{6,10},{8,12},{10,14},{12,0},{14,2},{1,5},{3,7},... | collective-permute-start | bytes 589832 | tf_op jit(solution)/shard_map/ppermute | solution.py:144
  3.6 18.7 %collective-permute-start.1 = (bf16[1280,128]{1,0:T(8,128)(2,1)S(1)}, bf16[1280,128]{1,0:T(8,128)(2,1)S(1)}, u32[]{:S(2)}, u32[]{:S(2)}) collective-permute-start(bf16[1280,128]{1,0:T(8,128)(2,1)S(1)} %multiply_convert_fusion.refs_2_), channel_id=1, source_target_pairs={{0,2},{2,4},{4,6},{6,8},{8,10},{10,12},{12,14},{1,3},{3,5},{5,7},{... | collective-permute-start | bytes 983048 | tf_op jit(solution)/shard_map/ppermute | solution.py:144
  6.7 15.6 %collective-permute-start = (bf16[1280,128]{1,0:T(8,128)(2,1)S(1)}, bf16[1280,128]{1,0:T(8,128)(2,1)S(1)}, u32[]{:S(2)}, u32[]{:S(2)}) collective-permute-start(bf16[1280,128]{1,0:T(8,128)(2,1)S(1)} %multiply_convert_fusion.refs_2_), channel_id=1, source_target_pairs={{0,4},{2,6},{4,8},{6,10},{8,12},{10,14},{1,5},{3,7},{5,9},{7,11},{... | collective-permute-start | bytes 983048 | tf_op jit(solution)/shard_map/ppermute | solution.py:144
  10.0 10.2 %collective-permute-start.3 = (bf16[768,128]{1,0:T(8,128)(2,1)S(1)}, bf16[768,128]{1,0:T(8,128)(2,1)S(1)}, u32[]{:S(2)}, u32[]{:S(2)}) collective-permute-start(bf16[768,128]{1,0:T(8,128)(2,1)S(1)} %broadcast_select_fusion), channel_id=1, source_target_pairs={{0,2},{2,0},{4,6},{6,4},{8,10},{10,8},{12,14},{14,12},{1,3},{3,1},... | collective-permute-start | bytes 589832 | tf_op jit(solution)/shard_map/ppermute | solution.py:148
  25.0 1.7 %collective-permute-start.4 = (bf16[128,1024]{1,0:T(8,128)(2,1)S(1)}, bf16[128,1024]{1,0:T(8,128)(2,1)S(1)}, u32[]{:S(2)}, u32[]{:S(2)}) collective-permute-start(bf16[128,1024]{1,0:T(8,128)(2,1)S(1)} %get-tuple-element.22), channel_id=1, source_target_pairs={{0,1},{1,0},{2,3},{3,2},{4,5},{5,4},{6,7},{7,6},{8,9},{9,8},{10,11... | collective-permute-start | bytes 786440 | tf_op jit(solution)/shard_map/ppermute | solution.py:240

commit v4 on v3

--- a/solution.py
+++ b/solution.py
@@ -12,10 +12,11 @@
 SETUP_COST = 30_000_000
 TAIL_COST = 1
 VMEM_BYTES = 24 * 1024 * 1024
-PARTS = (0, 768, 2048)
-RELAYED = (True, False)
-WRAP_FAR = True
-WRAP_DIRECT = False
+RELAYED = 768
+FAR_CUTS = ()
+ORDER = (0, 1)
+EARLY_RELAYED = (0, 2)
+EARLY_DIRECT = (1, 2)
 
 
 def split_bf16(array):
@@ -65,21 +66,39 @@
         copy.wait()
 
 
-def convolve(first, per_group, xs, query, skip, spectrum, table, gated_t):
-    channels, block = xs[0].shape
-    half = table.shape[1] // 2
-    depth = len(xs) * block
+def transform(window, places, offsets, xs, table, start, tile):
+    block = xs[0].shape[1]
+    oldest = window // block - 1
     seq = lax.axis_index("seq")
+    blocks, factors = [], []
+    for place, offset, x in zip(places, offsets, xs):
+        rows = x[offset + start : offset + start + tile]
+        if place < oldest:
+            rows = jnp.where(seq >= oldest - place, rows, jnp.zeros_like(rows))
+        blocks.append(rows)
+    for base in (0, window):
+        factors += [table[base + place * block : base + (place + 1) * block] for place in places]
+    return jnp.dot(
+        jnp.concatenate(blocks + blocks, axis=1),
+        jnp.concatenate(factors, axis=0),
+        preferred_element_type=jnp.float32,
+    )
+
+
+def early_kernel(window, places, offsets, *refs):
+    xs, (table, out) = refs[: len(places)], refs[len(places) :]
+    channels = out.shape[0]
     for start in range(0, channels, 256):
         tile = min(256, channels - start)
-        rows = slice(start, start + tile)
-        blocks = [
-            jnp.where(seq >= len(xs) - 1 - k, x[rows], jnp.zeros((tile, block), x.dtype))
-            for k, x in enumerate(xs[:-1])
-        ] + [xs[-1][rows]]
-        freq = jnp.dot(
-            jnp.concatenate(blocks + blocks, axis=1), table[: 2 * depth], preferred_element_type=jnp.float32
-        )
+        out[start : start + tile] = transform(window, places, offsets, xs, table, start, tile)
+
+
+def convolve(first, window, places, offsets, per_group, xs, early, own, own_offset, query, skip, spectrum, table, gated_t):
+    block, channels = gated_t.shape
+    half = table.shape[1] // 2
+    for start in range(0, channels, 256):
+        tile = min(256, channels - start)
+        freq = early[start : start + tile] + transform(window, places, offsets, xs, table, start, tile)
         mult = []
         for g in range(tile // per_group):
             part = freq[g * per_group : (g + 1) * per_group]
@@ -89,7 +108,7 @@
             mult.append(jnp.concatenate([xc * hc - xs_ * hs, xc * hs + xs_ * hc], axis=1).astype(jnp.bfloat16))
         both = lax.dot_general(
             jnp.concatenate(mult, axis=0),
-            table[2 * depth :],
+            table[2 * window :],
             (((1,), (1,)), ((), ())),
             preferred_element_type=jnp.float32,
         )
@@ -99,8 +118,9 @@
             if block != 128:
                 gain = jnp.broadcast_to(gain[:, :1], (128, block))
             near = both[low : low + 128]
+            product = own[own_offset + start + low : own_offset + start + low + 128]
             here = slice(start + low, start + low + 128)
-            mixed = near[:, :block] + near[:, block:] + gain * xs[-1][here].astype(jnp.float32)
+            mixed = near[:, :block] + near[:, block:] + gain * product.astype(jnp.float32)
             total = slice(first + start + low, first + start + low + 128)
             gated = (query[total].astype(jnp.float32) * mixed).astype(jnp.bfloat16)
             gated_t[:, here] = gated.T
@@ -112,12 +132,14 @@
     return [pl.ds(pl.multiple_of(part * cols, 128), cols) for part in (core, 1 - core)]
 
 
-def part_kernel(blocks, per_group, first, is_first, is_last, *refs):
-    xs, refs = refs[:blocks], refs[blocks:]
+def part_kernel(window, places, offsets, own_offset, per_group, first, is_first, is_last, *refs):
+    xs, (early, own), refs = refs[: len(places)], refs[len(places) : len(places) + 2], refs[len(places) + 2 :]
     (query, skip, spectrum, table, weight), refs = refs[:5], refs[5:]
     before, refs = ((), refs) if is_first else (refs[:1] if is_last else refs[:2], refs[1 if is_last else 2 :])
     outs, gated_t = refs[:-1], refs[-1]
-    convolve(first, per_group, xs, query, skip, spectrum, table, gated_t)
+    convolve(
+        first, window, places, offsets, per_group, xs, early, own, own_offset, query, skip, spectrum, table, gated_t
+    )
     here, there = column_halves(weight)
     rows = slice(first, first + gated_t.shape[1])
     for k, columns in enumerate((there,) if is_last else (there, here)):
@@ -178,19 +200,26 @@
     f32, bf16 = jnp.float32, jnp.bfloat16
     shape = jax.ShapeDtypeStruct
 
-    bounds = list(zip(PARTS[:-1], PARTS[1:]))
     products = [
-        (key_feat[low:high].astype(f32) * value_feat[low:high].astype(f32)).astype(bf16) for low, high in bounds
+        (key_feat[low:high].astype(f32) * value_feat[low:high].astype(f32)).astype(bf16)
+        for low, high in ((0, RELAYED), (RELAYED, channels))
     ]
-    odd = lax.axis_index("seq") % 2 == 1
-    windows = []
-    for own, relayed in zip(products, RELAYED):
-        if reach_max == 2 and relayed:
-            far = shift(own, 2, WRAP_FAR)
-            near = swap_pairs(jnp.where(odd, far, own))
-            windows.append([far, near, own])
-        else:
-            windows.append([shift(own, back, WRAP_DIRECT) for back in range(reach_max, 0, -1)] + [own])
+    parts = []
+    if reach_max == 2:
+        own = products[0]
+        far = shift(own, 2, True)
+        near = swap_pairs(jnp.where(lax.axis_index("seq") % 2 == 1, far, own))
+        parts.append((0, RELAYED, EARLY_RELAYED, [(far, 0), (near, 0), (own, 0)]))
+        own = products[1]
+        near = shift(own, 1, False)
+        for low, high in zip((0,) + FAR_CUTS, FAR_CUTS + (channels - RELAYED,)):
+            far = shift(own[low:high], 2, True)
+            parts.append((RELAYED + low, RELAYED + high, EARLY_DIRECT, [(far, 0), (near, low), (own, low)]))
+        parts = [parts[k] for k in ORDER]
+    else:
+        for own, low, high in zip(products, (0, RELAYED), (RELAYED, channels)):
+            halo = [shift(own, back, False) for back in range(reach_max, 0, -1)]
+            parts.append((low, high, [reach_max], [(array, 0) for array in (*halo, own)]))
 
     small = (
         filter_seed[None],
@@ -218,12 +247,28 @@
 
     common = (query, skip, spectrum, table, weight)
     sums = ()
-    for k, ((low, high), blocks) in enumerate(zip(bounds, windows)):
-        is_first, is_last = k == 0, k == len(bounds) - 1
-        operands = (*blocks, *common, *(sums[:1] if is_last else sums))
+    for k, (low, high, before, blocks) in enumerate(parts):
+        is_first, is_last = k == 0, k == len(parts) - 1
+        now = [place for place in range(reach_max + 1) if place not in before]
+        early = pl.pallas_call(
+            functools.partial(early_kernel, window, before, [blocks[place][1] for place in before]),
+            in_specs=[vmem] * (len(before) + 1),
+            out_specs=vmem,
+            out_shape=shape((high - low, length), f32),
+            compiler_params=params,
+            cost_estimate=cost(TAIL_COST),
+        )(*[blocks[place][0] for place in before], table)
+        operands = (
+            *[blocks[place][0] for place in now],
+            early,
+            blocks[-1][0],
+            *common,
+            *(sums[:1] if is_last else sums),
+        )
+        offsets = [blocks[place][1] for place in now]
         gated_shape = (block, high - low)
         results = pl.pallas_call(
-            functools.partial(part_kernel, len(blocks), per_group, low, is_first, is_last),
+            functools.partial(part_kernel, window, now, offsets, blocks[-1][1], per_group, low, is_first, is_last),
             in_specs=[vmem] * len(operands),
             out_specs=[vmem] * 2,
             out_shape=[shape((block, cols), bf16), shape(gated_shape, bf16)]
@@ -239,7 +284,7 @@
             sums = results
     received = lax.ppermute(part, "chan", [(0, 1), (1, 0)])
     own = pl.pallas_call(
-        functools.partial(own_kernel, bounds[-1][0]),
+        functools.partial(own_kernel, parts[-1][0]),
         in_specs=[vmem] * 3,
         out_specs=vmem,
         out_shape=shape((block, cols), f32),

time: 27.7 us -> 26.4 us (0.953)
  the two profiles are of different devices: /device:TPU:9 before, /device:TPU:23 now
where the time goes in v4:
time: 26.4 us; the launch traced here: 26.2 us
  Pallas kernels  8.92 us (34%)
  waiting for transfers between devices  8.66 us (33%)
  starting transfers between devices  5.56 us (21%)
  other arithmetic  3.01 us (11%)
    ppermute x3, waiting for transfers between devices, shift(): lax.ppermute(array, 'seq', [(i, (i + back) % count) for i in range(count...  4.36 us
    pallas_call x1, Pallas kernels, body(): pl.pallas_call(lambda *refs: setup_kernel(block * seq_count, block, 1.0 /...  3.93 us
    ppermute x1, waiting for transfers between devices, swap_pairs(): lax.ppermute(array, 'seq', [(i, i ^ 1) for i in range(lax.axis_size('seq'...  3.66 us
    ppermute x3, starting transfers between devices, shift(): lax.ppermute(array, 'seq', [(i, (i + back) % count) for i in range(count...  3.33 us
    pallas_call x2, Pallas kernels, body(): pl.pallas_call(functools.partial(part_kernel, window, now, offsets, block...  3.06 us
    convert_element_type x2, other arithmetic, body(): (key_feat[low:high].astype(f32) * value_feat[low:high].astype(f32)).astyp...  2.23 us
    ppermute x1, starting transfers between devices, body(): received = lax.ppermute(part, 'chan', [(0, 1), (1, 0)])  1.94 us
    pallas_call x2, Pallas kernels, body(): pl.pallas_call(functools.partial(early_kernel, window, before, [blocks[pl...  1.41 us
  transfers between devices with their start and end apart: 5, of which 5 were waited for; matrix products, arithmetic and copies ran while one was open for 5% of the time, Pallas kernels for 28%

profile of v4, /device:TPU:23, one launch (start us, length us, event | category | flops | bytes accessed | tf_op | source)
XLA Modules:
  0.0 26.2 jit_solution(10061570704336813002)
XLA Ops:
  0.0 1.1 %multiply_convert_fusion.1.refs_1_.refs_2_ = bf16[768,128]{1,0:T(8,128)(2,1)S(1)} fusion(bf16[2048,128]{1,0:T(8,128)(2,1)} %param.14, bf16[2048,128]{1,0:T(8,128)(2,1)} %param.13), kind=kLoop, calls=%fused_computation.2 | loop fusion | flops 393216 | bytes 589824 | tf_op jit(solution)/shard_map/convert_element_type | solution.py:204
  1.1 1.3 %collective-permute-start.2 = (bf16[768,128]{1,0:T(8,128)(2,1)S(1)}, bf16[768,128]{1,0:T(8,128)(2,1)S(1)}, u32[]{:S(2)}, u32[]{:S(2)}) collective-permute-start(bf16[768,128]{1,0:T(8,128)(2,1)S(1)} %multiply_convert_fusion.1.refs_1_.refs_2_), channel_id=1, source_target_pairs={{0,4},{2,6},{4,8},{6,10},{8,12},{10,14},{12,0},{14,2},{1,5},{3,7},... | collective-permute-start | bytes 589832 | tf_op jit(solution)/shard_map/ppermute | solution.py:166
  2.4 1.2 %multiply_convert_fusion.refs_1_.refs_2_ = bf16[1280,128]{1,0:T(8,128)(2,1)S(1)} fusion(bf16[2048,128]{1,0:T(8,128)(2,1)} %param.14, bf16[2048,128]{1,0:T(8,128)(2,1)} %param.13), kind=kLoop, calls=%fused_computation | loop fusion | flops 655360 | bytes 983040 | tf_op jit(solution)/shard_map/convert_element_type | solution.py:204
  3.6 1.9 %collective-permute-start.1 = (bf16[1280,128]{1,0:T(8,128)(2,1)S(1)}, bf16[1280,128]{1,0:T(8,128)(2,1)S(1)}, u32[]{:S(2)}, u32[]{:S(2)}) collective-permute-start(bf16[1280,128]{1,0:T(8,128)(2,1)S(1)} %multiply_convert_fusion.refs_1_.refs_2_), channel_id=1, source_target_pairs={{0,2},{2,4},{4,6},{6,8},{8,10},{10,12},{12,14},{1,3},{3,5},{5,7},{... | collective-permute-start | bytes 983048 | tf_op jit(solution)/shard_map/ppermute | solution.py:166
  5.5 0.1 collective-permute-start
  5.6 1.3 %collective-permute-done.2.refs_0_ = bf16[768,128]{1,0:T(8,128)(2,1)S(1)} collective-permute-done((bf16[768,128]{1,0:T(8,128)(2,1)S(1)}, bf16[768,128]{1,0:T(8,128)(2,1)S(1)}, u32[]{:S(2)}, u32[]{:S(2)}) %collective-permute-start.2) | collective-permute-done | bytes 196640 | tf_op jit(solution)/shard_map/ppermute | solution.py:166
  6.9 0.3 %collective-permute-start.3 = (bf16[768,128]{1,0:T(8,128)(2,1)S(1)}, bf16[768,128]{1,0:T(8,128)(2,1)S(1)}, u32[]{:S(2)}, u32[]{:S(2)}) collective-permute-start(bf16[768,128]{1,0:T(8,128)(2,1)S(1)} %broadcast_select_fusion), channel_id=1, source_target_pairs={{0,2},{2,0},{4,6},{6,4},{8,10},{10,8},{12,14},{14,12},{1,3},{3,1},... | collective-permute-start | bytes 589832 | tf_op jit(solution)/shard_map/ppermute | solution.py:170
  7.2 3.9 %shard_map.118 = (f32[128,512]{1,0:T(8,128)S(1)}, bf16[1024,512]{1,0:T(8,128)(2,1)S(1)}, bf16[2048,2048]{1,0:T(8,128)(2,1)S(1)}, bf16[2048,128]{1,0:T(8,128)(2,1)S(1)}, f32[16,128]{1,0:T(8,128)S(1)}) custom-call(s32[1,16]{1,0:T(1,128)} %bitcast.6, f32[32,64]{1,0:T(8,128)} %refs_1_.1, f32[1,64]{1,0:T(1,128)} %bitcast.7, f32[64,128]{1,0:T(8,128)} %refs_3_.1, ...), custom_call_target="tpu_custom_call" | custom-call | flops 1 | bytes 30000000 | tf_op jit(solution)/shard_map/pallas_call | solution.py:238
  11.2 0.6 %shard_map.120.refs_1_ = f32[768,512]{1,0:T(8,128)S(1)} custom-call(bf16[768,128]{1,0:T(8,128)(2,1)S(1)} %collective-permute-done.2.refs_0_, bf16[768,128]{1,0:T(8,128)(2,1)S(1)} %multiply_convert_fusion.1.refs_1_.refs_2_, bf16[1024,512]{1,0:T(8,128)(2,1)S(1)} %get-tuple-element.14.refs_2_.refs_6_), custom_call_target="tpu_custom_call" | custom-call | flops 1 | bytes 1 | tf_op jit(solution)/shard_map/pallas_call | solution.py:253
  11.7 2.0 %collective-permute-done.1.refs_0_ = bf16[1280,128]{1,0:T(8,128)(2,1)S(1)} collective-permute-done((bf16[1280,128]{1,0:T(8,128)(2,1)S(1)}, bf16[1280,128]{1,0:T(8,128)(2,1)S(1)}, u32[]{:S(2)}, u32[]{:S(2)}) %collective-permute-start.1) | collective-permute-done | bytes 327712 | tf_op jit(solution)/shard_map/ppermute | solution.py:166
  13.7 0.8 %shard_map.119.refs_1_ = f32[1280,512]{1,0:T(8,128)S(1)} custom-call(bf16[1280,128]{1,0:T(8,128)(2,1)S(1)} %collective-permute-done.1.refs_0_, bf16[1280,128]{1,0:T(8,128)(2,1)S(1)} %multiply_convert_fusion.refs_1_.refs_2_, bf16[1024,512]{1,0:T(8,128)(2,1)S(1)} %get-tuple-element.14.refs_2_.refs_6_), custom_call_target="tpu_custom_call" | custom-call | flops 1 | bytes 1 | tf_op jit(solution)/shard_map/pallas_call | solution.py:253
  14.6 3.7 %collective-permute-done.3.refs_0_ = bf16[768,128]{1,0:T(8,128)(2,1)S(1)} collective-permute-done((bf16[768,128]{1,0:T(8,128)(2,1)S(1)}, bf16[768,128]{1,0:T(8,128)(2,1)S(1)}, u32[]{:S(2)}, u32[]{:S(2)}) %collective-permute-start.3) | collective-permute-done | bytes 196640 | tf_op jit(solution)/shard_map/ppermute | solution.py:170
  18.3 1.4 %shard_map.121 = (f32[128,1024]{1,0:T(8,128)S(1)}, f32[128,1024]{1,0:T(8,128)S(1)}) custom-call(bf16[768,128]{1,0:T(8,128)(2,1)S(1)} %collective-permute-done.3.refs_0_, f32[768,512]{1,0:T(8,128)S(1)} %shard_map.120.refs_1_, bf16[768,128]{1,0:T(8,128)(2,1)S(1)} %multiply_convert_fusion.1.refs_1_.refs_2_, bf16[2048,128]{1,0:T(8,128)(2,1)S(1)} %get-tuple-element.15.refs_3_, ...), custom_call_target="tpu_custom_call" | custom-call | flops 1 | bytes 1 | tf_op jit(solution)/shard_map/pallas_call | solution.py:270
  19.7 1.1 %collective-permute-done.refs_0_ = bf16[1280,128]{1,0:T(8,128)(2,1)S(1)} collective-permute-done((bf16[1280,128]{1,0:T(8,128)(2,1)S(1)}, bf16[1280,128]{1,0:T(8,128)(2,1)S(1)}, u32[]{:S(2)}, u32[]{:S(2)}) %collective-permute-start) | collective-permute-done | bytes 327712 | tf_op jit(solution)/shard_map/ppermute | solution.py:166
  20.8 1.6 %shard_map.122 = (bf16[128,1024]{1,0:T(8,128)(2,1)S(1)}, bf16[128,1280]{1,0:T(8,128)(2,1)S(1)}) custom-call(bf16[1280,128]{1,0:T(8,128)(2,1)S(1)} %collective-permute-done.refs_0_, f32[1280,512]{1,0:T(8,128)S(1)} %shard_map.119.refs_1_, bf16[1280,128]{1,0:T(8,128)(2,1)S(1)} %multiply_convert_fusion.refs_1_.refs_2_, ...), custom_call_target="tpu_custom_call" | custom-call | flops 1 | bytes 1 | tf_op jit(solution)/shard_map/pallas_call | solution.py:270
  22.4 1.9 %collective-permute-start.4 = (bf16[128,1024]{1,0:T(8,128)(2,1)S(1)}, bf16[128,1024]{1,0:T(8,128)(2,1)S(1)}, u32[]{:S(2)}, u32[]{:S(2)}) collective-permute-start(bf16[128,1024]{1,0:T(8,128)(2,1)S(1)} %get-tuple-element.22), channel_id=1, source_target_pairs={{0,1},{1,0},{2,3},{3,2},{4,5},{5,4},{6,7},{7,6},{8,9},{9,8},{10,11... | collective-permute-start | bytes 786440 | tf_op jit(solution)/shard_map/ppermute | solution.py:285
  24.3 0.5 %shard_map.123 = f32[128,1024]{1,0:T(8,128)S(1)} custom-call(bf16[128,1280]{1,0:T(8,128)(2,1)S(1)} %get-tuple-element.20.gated_t, bf16[2048,2048]{1,0:T(8,128)(2,1)S(1)} %get-tuple-element.18.refs_7_.weight, f32[128,1024]{1,0:T(8,128)S(1)} %get-tuple-element.21.before), custom_call_target="tpu_custom_call" | custom-call | flops 1 | bytes 1 | tf_op jit(solution)/shard_map/pallas_call | solution.py:286
  24.8 0.6 %collective-permute-done.4 = bf16[128,1024]{1,0:T(8,128)(2,1)S(1)} collective-permute-done((bf16[128,1024]{1,0:T(8,128)(2,1)S(1)}, bf16[128,1024]{1,0:T(8,128)(2,1)S(1)}, u32[]{:S(2)}, u32[]{:S(2)}) %collective-permute-start.4) | collective-permute-done | bytes 262176 | tf_op jit(solution)/shard_map/ppermute | solution.py:285
  25.5 0.8 %add_convert_fusion = bf16[128,1024]{1,0:T(8,128)(2,1)} fusion(f32[128,1024]{1,0:T(8,128)S(1)} %shard_map.123, bf16[128,1024]{1,0:T(8,128)(2,1)S(1)} %collective-permute-done.4), kind=kLoop, calls=%fused_computation.1 | loop fusion | flops 393216 | bytes 1048576 | tf_op jit(solution)/shard_map/convert_element_type | solution.py:294
  (1 shorter events, 0.0 us)
Async XLA Ops:
  1.1 5.8 %collective-permute-start.2 = (bf16[768,128]{1,0:T(8,128)(2,1)S(1)}, bf16[768,128]{1,0:T(8,128)(2,1)S(1)}, u32[]{:S(2)}, u32[]{:S(2)}) collective-permute-start(bf16[768,128]{1,0:T(8,128)(2,1)S(1)} %multiply_convert_fusion.1.refs_1_.refs_2_), channel_id=1, source_target_pairs={{0,4},{2,6},{4,8},{6,10},{8,12},{10,14},{12,0},{14,2},{1,5},{3,7},... | collective-permute-start | bytes 589832 | tf_op jit(solution)/shard_map/ppermute | solution.py:166
  3.6 10.2 %collective-permute-start.1 = (bf16[1280,128]{1,0:T(8,128)(2,1)S(1)}, bf16[1280,128]{1,0:T(8,128)(2,1)S(1)}, u32[]{:S(2)}, u32[]{:S(2)}) collective-permute-start(bf16[1280,128]{1,0:T(8,128)(2,1)S(1)} %multiply_convert_fusion.refs_1_.refs_2_), channel_id=1, source_target_pairs={{0,2},{2,4},{4,6},{6,8},{8,10},{10,12},{12,14},{1,3},{3,5},{5,7},{... | collective-permute-start | bytes 983048 | tf_op jit(solution)/shard_map/ppermute | solution.py:166
  5.5 15.2 %collective-permute-start = (bf16[1280,128]{1,0:T(8,128)(2,1)S(1)}, bf16[1280,128]{1,0:T(8,128)(2,1)S(1)}, u32[]{:S(2)}, u32[]{:S(2)}) collective-permute-start(bf16[1280,128]{1,0:T(8,128)(2,1)S(1)} %multiply_convert_fusion.refs_1_.refs_2_), channel_id=1, source_target_pairs={{0,4},{2,6},{4,8},{6,10},{8,12},{10,14},{12,0},{14,2},{1,5},{3,7},... | collective-permute-start | bytes 983048 | tf_op jit(solution)/shard_map/ppermute | solution.py:166
  6.9 11.3 %collective-permute-start.3 = (bf16[768,128]{1,0:T(8,128)(2,1)S(1)}, bf16[768,128]{1,0:T(8,128)(2,1)S(1)}, u32[]{:S(2)}, u32[]{:S(2)}) collective-permute-start(bf16[768,128]{1,0:T(8,128)(2,1)S(1)} %broadcast_select_fusion), channel_id=1, source_target_pairs={{0,2},{2,0},{4,6},{6,4},{8,10},{10,8},{12,14},{14,12},{1,3},{3,1},... | collective-permute-start | bytes 589832 | tf_op jit(solution)/shard_map/ppermute | solution.py:170
  22.4 3.1 %collective-permute-start.4 = (bf16[128,1024]{1,0:T(8,128)(2,1)S(1)}, bf16[128,1024]{1,0:T(8,128)(2,1)S(1)}, u32[]{:S(2)}, u32[]{:S(2)}) collective-permute-start(bf16[128,1024]{1,0:T(8,128)(2,1)S(1)} %get-tuple-element.22), channel_id=1, source_target_pairs={{0,1},{1,0},{2,3},{3,2},{4,5},{5,4},{6,7},{7,6},{8,9},{9,8},{10,11... | collective-permute-start | bytes 786440 | tf_op jit(solution)/shard_map/ppermute | solution.py:285

commit v5 on v3

v5 whole, which is shorter than its diff:
```python
import functools
import math

import jax
import jax.numpy as jnp
import numpy as np
from jax import lax
from jax.experimental import pallas as pl
from jax.experimental.pallas import tpu as pltpu
from jax.sharding import PartitionSpec as P

SETUP_COST = 30_000_000
TAIL_COST = 1
VMEM_BYTES = 24 * 1024 * 1024
RELAYED = 1024
WRAP_FAR = False
WRAP_SENT = True


def split_bf16(array):
    high = array.astype(jnp.bfloat16)
    low = (array - high.astype(np.float64)).astype(jnp.bfloat16)
    return high, low


def transform_tables(window, first_out, block):
    half = 128 * math.ceil(window / 256)
    omega = (np.arange(half) + 0.5) * (math.pi / half)
    angle = np.arange(window)[:, None] * omega[None, :]
    forward = np.concatenate([np.cos(angle), np.sin(angle)], axis=1)
    back = omega[:, None] * (first_out + np.arange(block))[None, :]
    inverse = np.concatenate([np.cos(back), np.sin(back)], axis=0) / half
    return split_bf16(forward), split_bf16(inverse)


def setup_kernel(seq_len, block, scale, *refs):
    small, weight, spectrum, weight_out, local, sems = refs[:6], refs[9], refs[10], refs[14], refs[15:21], refs[21]
    table = refs[11]
    pairs = list(zip(small, local)) + list(zip(refs[6:9], refs[11:14]))
    pairs.append((weight.at[: weight_out.shape[0]], weight_out))
    copies = [pltpu.make_async_copy(source, target, sems.at[k]) for k, (source, target) in enumerate(pairs)]
    for copy in copies:
        copy.start()
    for copy in copies[:7]:
        copy.wait()
    seed, f_in, bias, f_out, decay, reach = local
    window = table.shape[0] // 2 - block
    lags = window - block
    lag = lax.broadcasted_iota(jnp.int32, (lags, 1), 0)
    if seq_len & (seq_len - 1) == 0:
        phases = (lag * seed[...]) & (seq_len - 1)
    else:
        phases = lax.rem(lag * seed[...], seq_len)
    angles = phases.astype(jnp.float32).T * (2.0 * math.pi / seq_len)
    features = jnp.concatenate([jnp.cos(angles), jnp.sin(angles)], axis=0)
    dims = (((0,), (0,)), ((), ()))
    exact = dict(precision=lax.Precision.HIGHEST, preferred_element_type=jnp.float32)
    shift = jnp.broadcast_to(bias[...], (8, bias.shape[1])).T[:, :1]
    hidden = jnp.sin(lax.dot_general(f_in[...], features, dims, **exact) + shift)
    shaped = lax.dot_general(hidden, f_out[...], dims, **exact)
    envelope = jnp.exp(-decay[...] * lag.astype(jnp.float32)) * scale
    taps = jnp.where(lag < reach[...] * block, shaped * envelope, 0.0).astype(jnp.bfloat16).T
    spectrum[...] = jnp.dot(taps, table[:lags], preferred_element_type=jnp.float32) + jnp.dot(
        taps, table[window : window + lags], preferred_element_type=jnp.float32
    )
    for copy in copies[7:]:
        copy.wait()


def transform(window, places, offsets, xs, valid, table, start, tile):
    block = xs[0].shape[1]
    blocks, factors = [], []
    for offset, x, there in zip(offsets, xs, valid):
        rows = x[offset + start : offset + start + tile]
        blocks.append(rows if there is None else jnp.where(there, rows, jnp.zeros_like(rows)))
    for base in (0, window):
        factors += [table[base + place * block : base + (place + 1) * block] for place in places]
    return jnp.dot(
        jnp.concatenate(blocks + blocks, axis=1),
        jnp.concatenate(factors, axis=0),
        preferred_element_type=jnp.float32,
    )


def block_there(window, block, place):
    back = window // block - 1 - place
    return None if back == 0 else lax.axis_index("seq") >= back


def respond(freq, group, per_group, window, spectrum, table):
    half = table.shape[1] // 2
    mult = []
    for g in range(freq.shape[0] // per_group):
        part = freq[g * per_group : (g + 1) * per_group]
        hc, hs = spectrum[group + g : group + g + 1, :half], spectrum[group + g : group + g + 1, half:]
        xc, xs = part[:, :half], part[:, half:]
        mult.append(jnp.concatenate([xc * hc - xs * hs, xc * hs + xs * hc], axis=1).astype(jnp.bfloat16))
    both = lax.dot_general(
        jnp.concatenate(mult, axis=0),
        table[2 * window :],
        (((1,), (1,)), ((), ())),
        preferred_element_type=jnp.float32,
    )
    block = both.shape[1] // 2
    return both[:, :block] + both[:, block:]


def tiles_of(channels):
    return [(start, min(256, channels - start)) for start in range(0, channels, 256)]


def early_kernel(window, places, *refs):
    xs, (table, *fetch) = refs[: len(places)], refs[len(places) :]
    if len(fetch) > 1:
        weight, out, weight_out, sem = fetch
        copy = pltpu.make_async_copy(weight.at[weight.shape[0] - weight_out.shape[0] :], weight_out, sem)
        copy.start()
    else:
        (out,), copy = fetch, None
    valid = [block_there(window, xs[0].shape[1], place) for place in places]
    for start, tile in tiles_of(out.shape[0]):
        out[start : start + tile] = transform(window, places, [0] * len(xs), xs, valid, table, start, tile)
    if copy is not None:
        copy.wait()


def ahead_kernel(window, per_group, first, own, other, spectrum, table, out):
    even = lax.axis_index("seq") % 2 == 0
    for start, tile in tiles_of(out.shape[0]):
        freq = transform(window, (0, 1), (0, 0), (own, other), (None, even), table, start, tile)
        ahead = respond(freq, (first + start) // per_group, per_group, window, spectrum, table)
        out[start : start + tile] = ahead.astype(out.dtype)


def gains(skip, row, block):
    gain = jnp.broadcast_to(skip[row : row + 1], (128, 128)).T
    return gain if block == 128 else jnp.broadcast_to(gain[:, :1], (128, block))


def base_kernel(window, per_group, first, other, own, skip, spectrum, table, out):
    oldest = window // own.shape[1] - 1
    odd = lax.axis_index("seq") % 2 == 1
    for start, tile in tiles_of(out.shape[0]):
        freq = transform(window, (oldest - 1, oldest), (0, 0), (other, own), (odd, None), table, start, tile)
        mixed = respond(freq, (first + start) // per_group, per_group, window, spectrum, table)
        for low in range(0, tile, 128):
            here = slice(start + low, start + low + 128)
            gain = gains(skip, (first + start + low) // 128, own.shape[1])
            out[here] = mixed[low : low + 128] + gain * own[here].astype(jnp.float32)


def last_kernel(first, carried, base, query, weight, before, part, gated_t):
    there = column_halves(weight)[1]
    arrived = lax.axis_index("seq") >= 2
    for start, tile in tiles_of(base.shape[0]):
        rows = slice(start, start + tile)
        mixed = base[rows] + jnp.where(arrived, carried[rows].astype(jnp.float32), 0.0)
        gated = query[first + start : first + start + tile].astype(jnp.float32) * mixed
        gated_t[:, rows] = gated.astype(jnp.bfloat16).T
    total = jnp.dot(gated_t[...], weight[:, there], preferred_element_type=jnp.float32)
    part[...] = (before[...] + total).astype(part.dtype)


def column_halves(weight):
    cols = weight.shape[1] // 2
    core = lax.axis_index("chan")
    return [pl.ds(pl.multiple_of(part * cols, 128), cols) for part in (core, 1 - core)]


def hand_kernel(far, own, out):
    out[...] = jnp.where(lax.axis_index("seq") % 2 == 1, far[...], own[...])


def part_kernel(window, places, per_group, first, is_first, *refs):
    xs, refs = refs[: len(places)], refs[len(places) :]
    (early, own, query, skip, spectrum, table, weight), refs = refs[:7], refs[7:]
    part, gated_t = refs[-2:]
    block, channels = gated_t.shape
    valid = [block_there(window, block, place) for place in places]
    for start, tile in tiles_of(channels):
        freq = early[start : start + tile] + transform(window, places, [0] * len(xs), xs, valid, table, start, tile)
        mixed = respond(freq, (first + start) // per_group, per_group, window, spectrum, table)
        for low in range(0, tile, 128):
            here = slice(start + low, start + low + 128)
            total = slice(first + start + low, first + start + low + 128)
            gain = gains(skip, (first + start + low) // 128, block)
            sums = mixed[low : low + 128] + gain * own[here].astype(jnp.float32)
            gated_t[:, here] = (query[total].astype(jnp.float32) * sums).astype(jnp.bfloat16).T
    there = column_halves(weight)[1]
    total = jnp.dot(gated_t[...], weight[:, there], preferred_element_type=jnp.float32)
    if not is_first:
        total = refs[0][...] + total
    part[...] = total.astype(part.dtype)


def own_kernel(gated_a, gated_b, weight_a, weight_b, out):
    here = column_halves(weight_a)[0]
    out[...] = jnp.dot(gated_a[...], weight_a[:, here], preferred_element_type=jnp.float32) + jnp.dot(
        gated_b[...], weight_b[:, here], preferred_element_type=jnp.float32
    )


def cost(bytes_accessed):
    return pl.CostEstimate(flops=1, bytes_accessed=bytes_accessed, transcendentals=0)


def shift(array, back, cyclic):
    count = lax.axis_size("seq")
    return lax.ppermute(array, "seq", [(i, (i + back) % count) for i in range(count if cyclic else count - back)])


def swap_pairs(array):
    return lax.ppermute(array, "seq", [(i, i ^ 1) for i in range(lax.axis_size("seq"))])


def body(
    query_feat,
    key_feat,
    value_feat,
    filter_seed,
    filter_in,
    filter_bias,
    filter_out,
    decay_rate,
    reach_blocks,
    skip_gain,
    out_weight,
):
    channels, block = query_feat.shape
    seq_count = lax.axis_size("seq")
    reach_max = seq_count // 4
    filters = decay_rate.shape[0]
    per_group = channels // filters
    lags = reach_max * block
    window = lags + block
    (fwd_hi, fwd_lo), (inv_hi, inv_lo) = transform_tables(window, lags, block)
    table = np.concatenate([fwd_hi, fwd_lo, inv_hi.T, inv_lo.T], axis=0)
    length = table.shape[1]
    out_cols = out_weight.shape[1]
    cols = out_cols // 2
    params = pltpu.CompilerParams(vmem_limit_bytes=VMEM_BYTES)
    vmem = pl.BlockSpec(memory_space=pltpu.VMEM)
    f32, bf16 = jnp.float32, jnp.bfloat16
    shape = jax.ShapeDtypeStruct

    products = [
        (key_feat[low:high].astype(f32) * value_feat[low:high].astype(f32)).astype(bf16)
        for low, high in ((0, RELAYED), (RELAYED, channels))
    ]
    if reach_max == 2:
        other = swap_pairs(products[1])
        far = shift(products[0], 2, WRAP_FAR)

    small = (
        filter_seed[None],
        filter_in,
        filter_bias[None],
        filter_out,
        decay_rate[None],
        reach_blocks[None],
    )
    large = (
        jnp.asarray(table),
        query_feat,
        skip_gain.reshape(-1, 128),
    )
    weight_in = pltpu.with_memory_space_constraint(out_weight, pltpu.HBM)
    spectrum, table, query, skip, weight = pl.pallas_call(
        lambda *refs: setup_kernel(block * seq_count, block, 1.0 / math.sqrt(lags), *refs),
        in_specs=[pl.BlockSpec(memory_space=pltpu.HBM)] * 10,
        out_specs=[vmem] * 5,
        out_shape=[pltpu.VMEM((filters, length), f32)] + [pltpu.VMEM(a.shape, a.dtype) for a in large]
        + [pltpu.VMEM((RELAYED, out_cols), bf16)],
        scratch_shapes=[pltpu.VMEM(a.shape, a.dtype) for a in small] + [pltpu.SemaphoreType.DMA((10,))],
        compiler_params=params,
        cost_estimate=cost(SETUP_COST),
    )(*[pltpu.with_memory_space_constraint(a, pltpu.HBM) for a in small + large], weight_in)

    def kernel(call, ins, *outs, fetch=None):
        return pl.pallas_call(
            call,
            in_specs=[vmem] * len(ins) + [pl.BlockSpec(memory_space=pltpu.HBM)] * (fetch is not None),
            out_specs=[vmem] * len(outs),
            out_shape=outs,
            scratch_shapes=[pltpu.SemaphoreType.DMA] * (fetch is not None),
            compiler_params=params,
            cost_estimate=cost(TAIL_COST),
        )(*ins, *[weight_in] * (fetch is not None))

    def early(own, before, fetch=None):
        outs = [shape((own.shape[0], length), f32)]
        if fetch is not None:
            outs.append(pltpu.VMEM((fetch, out_cols), bf16))
        call = functools.partial(early_kernel, window, tuple(before))
        return kernel(call, (*before.values(), table), *outs, fetch=fetch)

    def part(own, first, late, transformed, weight, sums, dtype):
        ins = (*late.values(), transformed, own, query, skip, spectrum, table, weight, *sums)
        call = functools.partial(part_kernel, window, tuple(late), per_group, first, not sums)
        return kernel(call, ins, shape((block, cols), dtype), shape((block, own.shape[0]), bf16))

    own_a, own_b = products
    rest = channels - RELAYED
    if reach_max == 2:
        (sent,) = kernel(
            functools.partial(ahead_kernel, window, per_group, RELAYED),
            (own_b, other, spectrum, table),
            shape(own_b.shape, bf16),
        )
        carried = shift(sent, 2, WRAP_SENT)
        ready, _ = lax.optimization_barrier((own_a, sent))
        (handed,) = kernel(hand_kernel, (far, ready), shape(own_a.shape, bf16))
        near = swap_pairs(handed)
        transformed, weight_b = early(own_a, {0: far, 2: own_a}, rest)
        (base,) = kernel(
            functools.partial(base_kernel, window, per_group, RELAYED),
            (other, own_b, skip, spectrum, table),
            shape(own_b.shape, f32),
        )
        sums, gated_a = part(own_a, 0, {1: near}, transformed, weight, (), f32)
        sums, gated_b = kernel(
            functools.partial(last_kernel, RELAYED),
            (carried, base, query, weight_b, sums),
            shape((block, cols), bf16),
            shape((block, rest), bf16),
        )
    else:
        halos = [{reach_max - back: shift(own, back, False) for back in range(1, reach_max + 1)} for own in products]
        transformed, weight_b = early(own_a, {reach_max: own_a}, rest)
        sums, gated_a = part(own_a, 0, halos[0], transformed, weight, (), f32)
        (transformed,) = early(own_b, {reach_max: own_b})
        sums, gated_b = part(own_b, RELAYED, halos[1], transformed, weight_b, (sums,), bf16)
    received = lax.ppermute(sums, "chan", [(0, 1), (1, 0)])
    (own,) = kernel(own_kernel, (gated_a, gated_b, weight, weight_b), shape((block, cols), f32))
    return (own + received.astype(f32)).astype(bf16)


def solution(mesh):
    return jax.shard_map(
        body,
        mesh=mesh,
        in_specs=(
            P("chan", ("groups", "seq")),
            P("chan", ("groups", "seq")),
            P("chan", ("groups", "seq")),
            P(),
            P(),
            P(),
            P(None, "chan"),
            P("chan"),
            P("chan"),
            P("chan"),
            P("chan", None),
        ),
        out_specs=P(("groups", "seq"), "chan"),
        check_vma=False,
    )
```

time: 27.7 us -> 26.2 us (0.946)
  the two profiles are of different devices: /device:TPU:9 before, /device:TPU:0 now
where the time goes in v5:
time: 26.2 us; the launch traced here: 26 us
  Pallas kernels  11.4 us (44%)
  starting transfers between devices  9.64 us (37%)
  waiting for transfers between devices  2.74 us (10%)
  other arithmetic  2.08 us (8%)
    pallas_call x7, Pallas kernels, kernel(): pl.pallas_call(call, in_specs=[vmem] * len(ins) + [pl.BlockSpec(memory_sp...  8.54 us
    ppermute x2, starting transfers between devices, shift(): lax.ppermute(array, 'seq', [(i, (i + back) % count) for i in range(count...  5.61 us
    ppermute x2, starting transfers between devices, swap_pairs(): lax.ppermute(array, 'seq', [(i, i ^ 1) for i in range(lax.axis_size('seq'...  3.96 us
    pallas_call x1, Pallas kernels, body(): pl.pallas_call(lambda *refs: setup_kernel(block * seq_count, block, 1.0 /...  2.86 us
    ppermute x2, waiting for transfers between devices, shift(): lax.ppermute(array, 'seq', [(i, (i + back) % count) for i in range(count...  1.96 us
    convert_element_type x1, other arithmetic, body(): (key_feat[low:high].astype(f32) * value_feat[low:high].astype(f32)).astyp...  1.32 us
    ppermute x1, waiting for transfers between devices, body(): received = lax.ppermute(sums, 'chan', [(0, 1), (1, 0)])  0.78 us
    convert_element_type x1, other arithmetic, body(): return (own + received.astype(f32)).astype(bf16)  0.76 us
  transfers between devices with their start and end apart: 5, of which 3 were waited for; matrix products, arithmetic and copies ran while one was open for 0% of the time, Pallas kernels for 42%

profile of v5, /device:TPU:0, one launch (start us, length us, event | category | flops | bytes accessed | tf_op | source)
XLA Modules:
  0.0 26.0 jit_solution(766879571901053427)
XLA Ops:
  0.0 1.3 %multiply_convert_fusion = (bf16[1024,128]{1,0:T(8,128)(2,1)S(1)}, bf16[1024,128]{1,0:T(8,128)(2,1)S(1)}) fusion(bf16[2048,128]{1,0:T(8,128)(2,1)} %param.14, bf16[2048,128]{1,0:T(8,128)(2,1)} %param.13), kind=kLoop, calls=%fused_computation.1 | loop fusion | flops 1048576 | bytes 1572864 | tf_op jit(solution)/shard_map/convert_element_type | solution.py:247
  1.3 3.0 %collective-permute-start.1 = (bf16[1024,128]{1,0:T(8,128)(2,1)S(1)}, bf16[1024,128]{1,0:T(8,128)(2,1)S(1)}, u32[]{:S(2)}, u32[]{:S(2)}) collective-permute-start(bf16[1024,128]{1,0:T(8,128)(2,1)S(1)} %get-tuple-element.29.own), channel_id=1, source_target_pairs={{0,2},{2,0},{4,6},{6,4},{8,10},{10,8},{12,14},{14,12},{1,3},{3,1},... | collective-permute-start | bytes 786440 | tf_op jit(solution)/shard_map/ppermute | solution.py:213
  4.4 3.5 %collective-permute-start = (bf16[1024,128]{1,0:T(8,128)(2,1)S(1)}, bf16[1024,128]{1,0:T(8,128)(2,1)S(1)}, u32[]{:S(2)}, u32[]{:S(2)}) collective-permute-start(bf16[1024,128]{1,0:T(8,128)(2,1)S(1)} %get-tuple-element.19.own.refs_1_.refs_2_), channel_id=1, source_target_pairs={{0,4},{2,6},{4,8},{6,10},{8,12},{10,14},{1,5},{3,7},{5,9},{7,11},{... | collective-permute-start | bytes 786440 | tf_op jit(solution)/shard_map/ppermute | solution.py:209
  7.9 2.9 %shard_map.118 = (f32[128,512]{1,0:T(8,128)S(1)}, bf16[1024,512]{1,0:T(8,128)(2,1)S(1)}, bf16[2048,128]{1,0:T(8,128)(2,1)S(1)}, f32[16,128]{1,0:T(8,128)S(1)}, bf16[1024,2048]{1,0:T(8,128)(2,1)S(1)}) custom-call(s32[1,16]{1,0:T(1,128)} %bitcast.6, f32[32,64]{1,0:T(8,128)} %refs_1_.1, f32[1,64]{1,0:T(1,128)} %bitcast.7, f32[64,128]{1,0:T(8,128)} %refs_3_.2, ...), custom_call_target="tpu_custom_call" | custom-call | flops 1 | bytes 30000000 | tf_op jit(solution)/shard_map/pallas_call | solution.py:268
  10.7 0.0 collective-permute-done.1.other
  10.7 1.5 %shard_map.119 = bf16[1024,128]{1,0:T(8,128)(2,1)S(1)} custom-call(bf16[1024,128]{1,0:T(8,128)(2,1)S(1)} %get-tuple-element.29.own, bf16[1024,128]{1,0:T(8,128)(2,1)S(1)} %collective-permute-done.1.other, f32[128,512]{1,0:T(8,128)S(1)} %get-tuple-element.17.spectrum.refs_5_, bf16[1024,512]{1,0:T(8,128)(2,1)S(1)} %get-tuple-element.18.table.refs_2_.refs_6_), custom_call_target="tpu_custom_call" | custom-call | flops 1 | bytes 1 | tf_op jit(solution)/shard_map/pallas_call | solution.py:280
  12.3 0.8 %collective-permute-done.far.refs_0_ = bf16[1024,128]{1,0:T(8,128)(2,1)S(1)} collective-permute-done((bf16[1024,128]{1,0:T(8,128)(2,1)S(1)}, bf16[1024,128]{1,0:T(8,128)(2,1)S(1)}, u32[]{:S(2)}, u32[]{:S(2)}) %collective-permute-start) | collective-permute-done | bytes 262176 | tf_op jit(solution)/shard_map/ppermute | solution.py:209
  13.1 0.1 shard_map.120
  13.2 0.9 %collective-permute-start.2 = (bf16[1024,128]{1,0:T(8,128)(2,1)S(1)}, bf16[1024,128]{1,0:T(8,128)(2,1)S(1)}, u32[]{:S(2)}, u32[]{:S(2)}) collective-permute-start(bf16[1024,128]{1,0:T(8,128)(2,1)S(1)} %shard_map.120), channel_id=1, source_target_pairs={{0,2},{2,0},{4,6},{6,4},{8,10},{10,8},{12,14},{14,12},{1,3},{3,1},... | collective-permute-start | bytes 786440 | tf_op jit(solution)/shard_map/ppermute | solution.py:213
  14.1 2.1 %collective-permute-start.3 = (bf16[1024,128]{1,0:T(8,128)(2,1)S(1)}, bf16[1024,128]{1,0:T(8,128)(2,1)S(1)}, u32[]{:S(2)}, u32[]{:S(2)}) collective-permute-start(bf16[1024,128]{1,0:T(8,128)(2,1)S(1)} %shard_map.119), channel_id=1, source_target_pairs={{0,4},{2,6},{4,8},{6,10},{8,12},{10,14},{12,0},{14,2},{1,5},{3,7},... | collective-permute-start | bytes 786440 | tf_op jit(solution)/shard_map/ppermute | solution.py:209
  16.2 2.7 %shard_map.121 = (f32[1024,512]{1,0:T(8,128)S(1)}, bf16[1024,2048]{1,0:T(8,128)(2,1)S(1)}) custom-call(bf16[1024,128]{1,0:T(8,128)(2,1)S(1)} %collective-permute-done.far.refs_0_, bf16[1024,128]{1,0:T(8,128)(2,1)S(1)} %get-tuple-element.19.own.refs_1_.refs_2_, bf16[1024,512]{1,0:T(8,128)(2,1)S(1)} %get-tuple-element.18.table.refs_2_.refs_6_, ...), custom_call_target="tpu_custom_call" | custom-call | flops 1 | bytes 1 | tf_op jit(solution)/shard_map/pallas_call | solution.py:280
  18.9 1.5 %shard_map.123.base = f32[1024,128]{1,0:T(8,128)S(1)} custom-call(bf16[1024,128]{1,0:T(8,128)(2,1)S(1)} %collective-permute-done.1.other, bf16[1024,128]{1,0:T(8,128)(2,1)S(1)} %get-tuple-element.29.own, f32[16,128]{1,0:T(8,128)S(1)} %get-tuple-element.22.refs_4_.skip, f32[128,512]{1,0:T(8,128)S(1)} %get-tuple-element.17.spectrum.refs_5_, ...), custom_call_target="tpu_custom_call" | custom-call | flops 1 | bytes 1 | tf_op jit(solution)/shard_map/pallas_call | solution.py:280
  20.5 0.0 collective-permute-done.2.refs_0_
  20.5 1.5 %shard_map.122 = (f32[128,1024]{1,0:T(8,128)S(1)}, bf16[128,1024]{1,0:T(8,128)(2,1)S(1)}) custom-call(bf16[1024,128]{1,0:T(8,128)(2,1)S(1)} %collective-permute-done.2.refs_0_, f32[1024,512]{1,0:T(8,128)S(1)} %get-tuple-element.20.refs_1_, bf16[1024,128]{1,0:T(8,128)(2,1)S(1)} %get-tuple-element.19.own.refs_1_.refs_2_, ...), custom_call_target="tpu_custom_call" | custom-call | flops 1 | bytes 1 | tf_op jit(solution)/shard_map/pallas_call | solution.py:280
  22.0 1.1 %collective-permute-done.3.carried = bf16[1024,128]{1,0:T(8,128)(2,1)S(1)} collective-permute-done((bf16[1024,128]{1,0:T(8,128)(2,1)S(1)}, bf16[1024,128]{1,0:T(8,128)(2,1)S(1)}, u32[]{:S(2)}, u32[]{:S(2)}) %collective-permute-start.3) | collective-permute-done | bytes 262176 | tf_op jit(solution)/shard_map/ppermute | solution.py:209
  23.1 0.5 %shard_map.124 = (bf16[128,1024]{1,0:T(8,128)(2,1)S(1)}, bf16[128,1024]{1,0:T(8,128)(2,1)S(1)}) custom-call(bf16[1024,128]{1,0:T(8,128)(2,1)S(1)} %collective-permute-done.3.carried, f32[1024,128]{1,0:T(8,128)S(1)} %shard_map.123.base, bf16[2048,128]{1,0:T(8,128)(2,1)S(1)} %get-tuple-element.21.refs_3_.query, ...), custom_call_target="tpu_custom_call" | custom-call | flops 1 | bytes 1 | tf_op jit(solution)/shard_map/pallas_call | solution.py:280
  23.6 0.1 collective-permute-start.4
  23.7 0.7 %shard_map.125 = f32[128,1024]{1,0:T(8,128)S(1)} custom-call(bf16[128,1024]{1,0:T(8,128)(2,1)S(1)} %get-tuple-element.24.gated_a, bf16[128,1024]{1,0:T(8,128)(2,1)S(1)} %get-tuple-element.27.gated_b, bf16[1024,2048]{1,0:T(8,128)(2,1)S(1)} %get-tuple-element.23.refs_7_.weight_a, bf16[1024,2048]{1,0:T(8,128)(2,1)S(1)} %get-tuple-element.25.weight.weight_b), custom_call_target="tpu_custom_call" | custom-call | flops 1 | bytes 1 | tf_op jit(solution)/shard_map/pallas_call | solution.py:280
  24.4 0.8 %collective-permute-done.4 = bf16[128,1024]{1,0:T(8,128)(2,1)S(1)} collective-permute-done((bf16[128,1024]{1,0:T(8,128)(2,1)S(1)}, bf16[128,1024]{1,0:T(8,128)(2,1)S(1)}, u32[]{:S(2)}, u32[]{:S(2)}) %collective-permute-start.4) | collective-permute-done | bytes 262176 | tf_op jit(solution)/shard_map/ppermute | solution.py:333
  25.2 0.8 %add_convert_fusion = bf16[128,1024]{1,0:T(8,128)(2,1)} fusion(f32[128,1024]{1,0:T(8,128)S(1)} %shard_map.125, bf16[128,1024]{1,0:T(8,128)(2,1)S(1)} %collective-permute-done.4), kind=kLoop, calls=%fused_computation | loop fusion | flops 393216 | bytes 1048576 | tf_op jit(solution)/shard_map/convert_element_type | solution.py:335
Async XLA Ops:
  1.3 9.4 %collective-permute-start.1 = (bf16[1024,128]{1,0:T(8,128)(2,1)S(1)}, bf16[1024,128]{1,0:T(8,128)(2,1)S(1)}, u32[]{:S(2)}, u32[]{:S(2)}) collective-permute-start(bf16[1024,128]{1,0:T(8,128)(2,1)S(1)} %get-tuple-element.29.own), channel_id=1, source_target_pairs={{0,2},{2,0},{4,6},{6,4},{8,10},{10,8},{12,14},{14,12},{1,3},{3,1},... | collective-permute-start | bytes 786440 | tf_op jit(solution)/shard_map/ppermute | solution.py:213
  4.4 8.7 %collective-permute-start = (bf16[1024,128]{1,0:T(8,128)(2,1)S(1)}, bf16[1024,128]{1,0:T(8,128)(2,1)S(1)}, u32[]{:S(2)}, u32[]{:S(2)}) collective-permute-start(bf16[1024,128]{1,0:T(8,128)(2,1)S(1)} %get-tuple-element.19.own.refs_1_.refs_2_), channel_id=1, source_target_pairs={{0,4},{2,6},{4,8},{6,10},{8,12},{10,14},{1,5},{3,7},{5,9},{7,11},{... | collective-permute-start | bytes 786440 | tf_op jit(solution)/shard_map/ppermute | solution.py:209
  13.2 7.3 %collective-permute-start.2 = (bf16[1024,128]{1,0:T(8,128)(2,1)S(1)}, bf16[1024,128]{1,0:T(8,128)(2,1)S(1)}, u32[]{:S(2)}, u32[]{:S(2)}) collective-permute-start(bf16[1024,128]{1,0:T(8,128)(2,1)S(1)} %shard_map.120), channel_id=1, source_target_pairs={{0,2},{2,0},{4,6},{6,4},{8,10},{10,8},{12,14},{14,12},{1,3},{3,1},... | collective-permute-start | bytes 786440 | tf_op jit(solution)/shard_map/ppermute | solution.py:213
  14.1 9.0 %collective-permute-start.3 = (bf16[1024,128]{1,0:T(8,128)(2,1)S(1)}, bf16[1024,128]{1,0:T(8,128)(2,1)S(1)}, u32[]{:S(2)}, u32[]{:S(2)}) collective-permute-start(bf16[1024,128]{1,0:T(8,128)(2,1)S(1)} %shard_map.119), channel_id=1, source_target_pairs={{0,4},{2,6},{4,8},{6,10},{8,12},{10,14},{12,0},{14,2},{1,5},{3,7},... | collective-permute-start | bytes 786440 | tf_op jit(solution)/shard_map/ppermute | solution.py:209
  23.6 1.6 %collective-permute-start.4 = (bf16[128,1024]{1,0:T(8,128)(2,1)S(1)}, bf16[128,1024]{1,0:T(8,128)(2,1)S(1)}, u32[]{:S(2)}, u32[]{:S(2)}) collective-permute-start(bf16[128,1024]{1,0:T(8,128)(2,1)S(1)} %get-tuple-element.28), channel_id=1, source_target_pairs={{0,1},{1,0},{2,3},{3,2},{4,5},{5,4},{6,7},{7,6},{8,9},{9,8},{10,11... | collective-permute-start | bytes 786440 | tf_op jit(solution)/shard_map/ppermute | solution.py:333

commit v6 on v5

--- a/solution.py
+++ b/solution.py
@@ -13,8 +13,8 @@
 TAIL_COST = 1
 VMEM_BYTES = 24 * 1024 * 1024
 RELAYED = 1024
-WRAP_FAR = False
-WRAP_SENT = True
+WRAP_FAR = True
+WRAP_SENT = False
 
 
 def split_bf16(array):
@@ -37,7 +37,7 @@
     small, weight, spectrum, weight_out, local, sems = refs[:6], refs[9], refs[10], refs[14], refs[15:21], refs[21]
     table = refs[11]
     pairs = list(zip(small, local)) + list(zip(refs[6:9], refs[11:14]))
-    pairs.append((weight.at[: weight_out.shape[0]], weight_out))
+    pairs.append((weight, weight_out))
     copies = [pltpu.make_async_copy(source, target, sems.at[k]) for k, (source, target) in enumerate(pairs)]
     for copy in copies:
         copy.start()
@@ -109,21 +109,6 @@
     return [(start, min(256, channels - start)) for start in range(0, channels, 256)]
 
 
-def early_kernel(window, places, *refs):
-    xs, (table, *fetch) = refs[: len(places)], refs[len(places) :]
-    if len(fetch) > 1:
-        weight, out, weight_out, sem = fetch
-        copy = pltpu.make_async_copy(weight.at[weight.shape[0] - weight_out.shape[0] :], weight_out, sem)
-        copy.start()
-    else:
-        (out,), copy = fetch, None
-    valid = [block_there(window, xs[0].shape[1], place) for place in places]
-    for start, tile in tiles_of(out.shape[0]):
-        out[start : start + tile] = transform(window, places, [0] * len(xs), xs, valid, table, start, tile)
-    if copy is not None:
-        copy.wait()
-
-
 def ahead_kernel(window, per_group, first, own, other, spectrum, table, out):
     even = lax.axis_index("seq") % 2 == 0
     for start, tile in tiles_of(out.shape[0]):
@@ -137,16 +122,18 @@
     return gain if block == 128 else jnp.broadcast_to(gain[:, :1], (128, block))
 
 
-def base_kernel(window, per_group, first, other, own, skip, spectrum, table, out):
-    oldest = window // own.shape[1] - 1
+def base_kernel(window, places, odd_only, per_group, first, *refs):
+    xs, (skip, spectrum, table, out) = refs[: len(places)], refs[len(places) :]
+    block = out.shape[1]
     odd = lax.axis_index("seq") % 2 == 1
+    valid = [odd if odd_only else block_there(window, block, place) for place in places[:-1]] + [None]
     for start, tile in tiles_of(out.shape[0]):
-        freq = transform(window, (oldest - 1, oldest), (0, 0), (other, own), (odd, None), table, start, tile)
+        freq = transform(window, places, [0] * len(xs), xs, valid, table, start, tile)
         mixed = respond(freq, (first + start) // per_group, per_group, window, spectrum, table)
         for low in range(0, tile, 128):
             here = slice(start + low, start + low + 128)
-            gain = gains(skip, (first + start + low) // 128, own.shape[1])
-            out[here] = mixed[low : low + 128] + gain * own[here].astype(jnp.float32)
+            gain = gains(skip, (first + start + low) // 128, block)
+            out[here] = mixed[low : low + 128] + gain * xs[-1][here].astype(jnp.float32)
 
 
 def last_kernel(first, carried, base, query, weight, before, part, gated_t):
@@ -157,7 +144,7 @@
         mixed = base[rows] + jnp.where(arrived, carried[rows].astype(jnp.float32), 0.0)
         gated = query[first + start : first + start + tile].astype(jnp.float32) * mixed
         gated_t[:, rows] = gated.astype(jnp.bfloat16).T
-    total = jnp.dot(gated_t[...], weight[:, there], preferred_element_type=jnp.float32)
+    total = jnp.dot(gated_t[...], weight[first:, there], preferred_element_type=jnp.float32)
     part[...] = (before[...] + total).astype(part.dtype)
 
 
@@ -173,31 +160,39 @@
 
 def part_kernel(window, places, per_group, first, is_first, *refs):
     xs, refs = refs[: len(places)], refs[len(places) :]
-    (early, own, query, skip, spectrum, table, weight), refs = refs[:7], refs[7:]
+    (base, query, spectrum, table, weight), refs = refs[:5], refs[5:]
     part, gated_t = refs[-2:]
     block, channels = gated_t.shape
+    seq = lax.axis_index("seq")
     valid = [block_there(window, block, place) for place in places]
-    for start, tile in tiles_of(channels):
-        freq = early[start : start + tile] + transform(window, places, [0] * len(xs), xs, valid, table, start, tile)
-        mixed = respond(freq, (first + start) // per_group, per_group, window, spectrum, table)
-        for low in range(0, tile, 128):
-            here = slice(start + low, start + low + 128)
-            total = slice(first + start + low, first + start + low + 128)
-            gain = gains(skip, (first + start + low) // 128, block)
-            sums = mixed[low : low + 128] + gain * own[here].astype(jnp.float32)
-            gated_t[:, here] = (query[total].astype(jnp.float32) * sums).astype(jnp.bfloat16).T
+
+    def gate(start, tile, mixed):
+        gated = query[first + start : first + start + tile].astype(jnp.float32) * mixed
+        gated_t[:, start : start + tile] = gated.astype(jnp.bfloat16).T
+
+    @pl.when(seq > 0)
+    def _():
+        for start, tile in tiles_of(channels):
+            freq = transform(window, places, [0] * len(xs), xs, valid, table, start, tile)
+            mixed = respond(freq, (first + start) // per_group, per_group, window, spectrum, table)
+            gate(start, tile, base[start : start + tile] + mixed)
+
+    @pl.when(seq == 0)
+    def _():
+        for start, tile in tiles_of(channels):
+            gate(start, tile, base[start : start + tile])
+
     there = column_halves(weight)[1]
-    total = jnp.dot(gated_t[...], weight[:, there], preferred_element_type=jnp.float32)
+    total = jnp.dot(gated_t[...], weight[first : first + channels, there], preferred_element_type=jnp.float32)
     if not is_first:
         total = refs[0][...] + total
     part[...] = total.astype(part.dtype)
 
 
-def own_kernel(gated_a, gated_b, weight_a, weight_b, out):
-    here = column_halves(weight_a)[0]
-    out[...] = jnp.dot(gated_a[...], weight_a[:, here], preferred_element_type=jnp.float32) + jnp.dot(
-        gated_b[...], weight_b[:, here], preferred_element_type=jnp.float32
-    )
+def own_kernel(gated_a, gated_b, weight, out):
+    here = column_halves(weight)[0]
+    gated_t = jnp.concatenate([gated_a[...], gated_b[...]], axis=1)
+    out[...] = jnp.dot(gated_t, weight[:, here], preferred_element_type=jnp.float32)
 
 
 def cost(bytes_accessed):
@@ -270,37 +265,32 @@
         in_specs=[pl.BlockSpec(memory_space=pltpu.HBM)] * 10,
         out_specs=[vmem] * 5,
         out_shape=[pltpu.VMEM((filters, length), f32)] + [pltpu.VMEM(a.shape, a.dtype) for a in large]
-        + [pltpu.VMEM((RELAYED, out_cols), bf16)],
+        + [pltpu.VMEM(out_weight.shape, bf16)],
         scratch_shapes=[pltpu.VMEM(a.shape, a.dtype) for a in small] + [pltpu.SemaphoreType.DMA((10,))],
         compiler_params=params,
         cost_estimate=cost(SETUP_COST),
     )(*[pltpu.with_memory_space_constraint(a, pltpu.HBM) for a in small + large], weight_in)
 
-    def kernel(call, ins, *outs, fetch=None):
+    def kernel(call, ins, *outs):
         return pl.pallas_call(
             call,
-            in_specs=[vmem] * len(ins) + [pl.BlockSpec(memory_space=pltpu.HBM)] * (fetch is not None),
+            in_specs=[vmem] * len(ins),
             out_specs=[vmem] * len(outs),
             out_shape=outs,
-            scratch_shapes=[pltpu.SemaphoreType.DMA] * (fetch is not None),
             compiler_params=params,
             cost_estimate=cost(TAIL_COST),
-        )(*ins, *[weight_in] * (fetch is not None))
-
-    def early(own, before, fetch=None):
-        outs = [shape((own.shape[0], length), f32)]
-        if fetch is not None:
-            outs.append(pltpu.VMEM((fetch, out_cols), bf16))
-        call = functools.partial(early_kernel, window, tuple(before))
-        return kernel(call, (*before.values(), table), *outs, fetch=fetch)
-
-    def part(own, first, late, transformed, weight, sums, dtype):
-        ins = (*late.values(), transformed, own, query, skip, spectrum, table, weight, *sums)
+        )(*ins)
+
+    def base(first, blocks, odd_only=False):
+        call = functools.partial(base_kernel, window, tuple(blocks), odd_only, per_group, first)
+        return kernel(call, (*blocks.values(), skip, spectrum, table), shape(blocks[reach_max].shape, f32))[0]
+
+    def part(first, late, early, sums, dtype):
+        ins = (*late.values(), early, query, spectrum, table, weight, *sums)
         call = functools.partial(part_kernel, window, tuple(late), per_group, first, not sums)
-        return kernel(call, ins, shape((block, cols), dtype), shape((block, own.shape[0]), bf16))
+        return kernel(call, ins, shape((block, cols), dtype), shape((block, early.shape[0]), bf16))
 
     own_a, own_b = products
-    rest = channels - RELAYED
     if reach_max == 2:
         (sent,) = kernel(
             functools.partial(ahead_kernel, window, per_group, RELAYED),
@@ -311,27 +301,21 @@
         ready, _ = lax.optimization_barrier((own_a, sent))
         (handed,) = kernel(hand_kernel, (far, ready), shape(own_a.shape, bf16))
         near = swap_pairs(handed)
-        transformed, weight_b = early(own_a, {0: far, 2: own_a}, rest)
-        (base,) = kernel(
-            functools.partial(base_kernel, window, per_group, RELAYED),
-            (other, own_b, skip, spectrum, table),
-            shape(own_b.shape, f32),
-        )
-        sums, gated_a = part(own_a, 0, {1: near}, transformed, weight, (), f32)
+        base_a = base(0, {0: far, 2: own_a})
+        base_b = base(RELAYED, {1: other, 2: own_b}, True)
+        sums, gated_a = part(0, {1: near}, base_a, (), f32)
         sums, gated_b = kernel(
             functools.partial(last_kernel, RELAYED),
-            (carried, base, query, weight_b, sums),
+            (carried, base_b, query, weight, sums),
             shape((block, cols), bf16),
-            shape((block, rest), bf16),
+            shape((block, channels - RELAYED), bf16),
         )
     else:
         halos = [{reach_max - back: shift(own, back, False) for back in range(1, reach_max + 1)} for own in products]
-        transformed, weight_b = early(own_a, {reach_max: own_a}, rest)
-        sums, gated_a = part(own_a, 0, halos[0], transformed, weight, (), f32)
-        (transformed,) = early(own_b, {reach_max: own_b})
-        sums, gated_b = part(own_b, RELAYED, halos[1], transformed, weight_b, (sums,), bf16)
+        sums, gated_a = part(0, halos[0], base(0, {reach_max: own_a}), (), f32)
+        sums, gated_b = part(RELAYED, halos[1], base(RELAYED, {reach_max: own_b}), (sums,), bf16)
     received = lax.ppermute(sums, "chan", [(0, 1), (1, 0)])
-    (own,) = kernel(own_kernel, (gated_a, gated_b, weight, weight_b), shape((block, cols), f32))
+    (own,) = kernel(own_kernel, (gated_a, gated_b, weight), shape((block, cols), f32))
     return (own + received.astype(f32)).astype(bf16)
 
 

time: 26.2 us -> 25 us (0.954)
  the two profiles are of different devices: /device:TPU:0 before, /device:TPU:9 now
where the time goes in v6:
time: 25 us; the launch traced here: 24.6 us
  Pallas kernels  11.4 us (46%)
  starting transfers between devices  9.91 us (40%)
  other arithmetic  2.08 us (8%)
  waiting for transfers between devices  1.09 us (4%)
    pallas_call x7, Pallas kernels, kernel(): pl.pallas_call(call, in_specs=[vmem] * len(ins), out_specs=[vmem] * len(o...  7.38 us
    ppermute x2, starting transfers between devices, shift(): lax.ppermute(array, 'seq', [(i, (i + back) % count) for i in range(count...  4.49 us
    pallas_call x1, Pallas kernels, body(): pl.pallas_call(lambda *refs: setup_kernel(block * seq_count, block, 1.0 /...  4.05 us
    ppermute x1, starting transfers between devices, body(): received = lax.ppermute(sums, 'chan', [(0, 1), (1, 0)])  2.81 us
    ppermute x2, starting transfers between devices, swap_pairs(): lax.ppermute(array, 'seq', [(i, i ^ 1) for i in range(lax.axis_size('seq'...  2.61 us
    convert_element_type x1, other arithmetic, body(): (key_feat[low:high].astype(f32) * value_feat[low:high].astype(f32)).astyp...  1.32 us
    convert_element_type x1, other arithmetic, body(): return (own + received.astype(f32)).astype(bf16)  0.76 us
    ppermute x2, waiting for transfers between devices, swap_pairs(): lax.ppermute(array, 'seq', [(i, i ^ 1) for i in range(lax.axis_size('seq'...  0.59 us
  transfers between devices with their start and end apart: 5, of which 3 were waited for; matrix products, arithmetic and copies ran while one was open for 0% of the time, Pallas kernels for 44%

profile of v6, /device:TPU:9, one launch (start us, length us, event | category | flops | bytes accessed | tf_op | source)
XLA Modules:
  0.0 24.6 jit_solution(15086284526020317035)
XLA Ops:
  0.0 1.3 %multiply_convert_fusion = (bf16[1024,128]{1,0:T(8,128)(2,1)S(1)}, bf16[1024,128]{1,0:T(8,128)(2,1)S(1)}) fusion(bf16[2048,128]{1,0:T(8,128)(2,1)} %param.14, bf16[2048,128]{1,0:T(8,128)(2,1)} %param.13), kind=kLoop, calls=%fused_computation.1 | loop fusion | flops 1048576 | bytes 1572864 | tf_op jit(solution)/shard_map/convert_element_type | solution.py:242
  1.3 1.3 %collective-permute-start.1 = (bf16[1024,128]{1,0:T(8,128)(2,1)S(1)}, bf16[1024,128]{1,0:T(8,128)(2,1)S(1)}, u32[]{:S(2)}, u32[]{:S(2)}) collective-permute-start(bf16[1024,128]{1,0:T(8,128)(2,1)S(1)} %get-tuple-element.25.own.refs_1_), channel_id=1, source_target_pairs={{0,2},{2,0},{4,6},{6,4},{8,10},{10,8},{12,14},{14,12},{1,3},{3,1},... | collective-permute-start | bytes 786440 | tf_op jit(solution)/shard_map/ppermute | solution.py:208
  2.6 1.3 %collective-permute-start = (bf16[1024,128]{1,0:T(8,128)(2,1)S(1)}, bf16[1024,128]{1,0:T(8,128)(2,1)S(1)}, u32[]{:S(2)}, u32[]{:S(2)}) collective-permute-start(bf16[1024,128]{1,0:T(8,128)(2,1)S(1)} %get-tuple-element.17.own.refs_1_), channel_id=1, source_target_pairs={{0,4},{2,6},{4,8},{6,10},{8,12},{10,14},{12,0},{14,2},{1,5},{3,7},... | collective-permute-start | bytes 786440 | tf_op jit(solution)/shard_map/ppermute | solution.py:204
  3.9 4.0 %shard_map.118 = (f32[128,512]{1,0:T(8,128)S(1)}, bf16[1024,512]{1,0:T(8,128)(2,1)S(1)}, bf16[2048,128]{1,0:T(8,128)(2,1)S(1)}, f32[16,128]{1,0:T(8,128)S(1)}, bf16[2048,2048]{1,0:T(8,128)(2,1)S(1)}) custom-call(s32[1,16]{1,0:T(1,128)} %bitcast.6, f32[32,64]{1,0:T(8,128)} %refs_1_.1, f32[1,64]{1,0:T(1,128)} %bitcast.7, f32[64,128]{1,0:T(8,128)} %refs_3_.1, ...), custom_call_target="tpu_custom_call" | custom-call | flops 1 | bytes 30000000 | tf_op jit(solution)/shard_map/pallas_call | solution.py:263
  8.0 0.6 %collective-permute-done.1.other.refs_0_ = bf16[1024,128]{1,0:T(8,128)(2,1)S(1)} collective-permute-done((bf16[1024,128]{1,0:T(8,128)(2,1)S(1)}, bf16[1024,128]{1,0:T(8,128)(2,1)S(1)}, u32[]{:S(2)}, u32[]{:S(2)}) %collective-permute-start.1) | collective-permute-done | bytes 262176 | tf_op jit(solution)/shard_map/ppermute | solution.py:208
  8.6 1.5 %shard_map.119 = bf16[1024,128]{1,0:T(8,128)(2,1)S(1)} custom-call(bf16[1024,128]{1,0:T(8,128)(2,1)S(1)} %get-tuple-element.25.own.refs_1_, bf16[1024,128]{1,0:T(8,128)(2,1)S(1)} %collective-permute-done.1.other.refs_0_, f32[128,512]{1,0:T(8,128)S(1)} %get-tuple-element.15.spectrum.refs_3_, bf16[1024,512]{1,0:T(8,128)(2,1)S(1)} %get-tuple-element.16.table.refs_4_), custom_call_target="tpu_custom_call" | custom-call | flops 1 | bytes 1 | tf_op jit(solution)/shard_map/pallas_call | solution.py:275
  10.1 0.0 collective-permute-done.far.refs_0_
  10.1 0.1 shard_map.120
  10.2 1.3 %collective-permute-start.2 = (bf16[1024,128]{1,0:T(8,128)(2,1)S(1)}, bf16[1024,128]{1,0:T(8,128)(2,1)S(1)}, u32[]{:S(2)}, u32[]{:S(2)}) collective-permute-start(bf16[1024,128]{1,0:T(8,128)(2,1)S(1)} %shard_map.120), channel_id=1, source_target_pairs={{0,2},{2,0},{4,6},{6,4},{8,10},{10,8},{12,14},{14,12},{1,3},{3,1},... | collective-permute-start | bytes 786440 | tf_op jit(solution)/shard_map/ppermute | solution.py:208
  11.5 3.2 %collective-permute-start.3 = (bf16[1024,128]{1,0:T(8,128)(2,1)S(1)}, bf16[1024,128]{1,0:T(8,128)(2,1)S(1)}, u32[]{:S(2)}, u32[]{:S(2)}) collective-permute-start(bf16[1024,128]{1,0:T(8,128)(2,1)S(1)} %shard_map.119), channel_id=1, source_target_pairs={{0,4},{2,6},{4,8},{6,10},{8,12},{10,14},{1,5},{3,7},{5,9},{7,11},{... | collective-permute-start | bytes 786440 | tf_op jit(solution)/shard_map/ppermute | solution.py:204
  14.7 1.5 %shard_map.123.base = f32[1024,128]{1,0:T(8,128)S(1)} custom-call(bf16[1024,128]{1,0:T(8,128)(2,1)S(1)} %collective-permute-done.1.other.refs_0_, bf16[1024,128]{1,0:T(8,128)(2,1)S(1)} %get-tuple-element.25.own.refs_1_, f32[16,128]{1,0:T(8,128)S(1)} %get-tuple-element.18.refs_2_, f32[128,512]{1,0:T(8,128)S(1)} %get-tuple-element.15.spectrum.refs_3_, ...), custom_call_target="tpu_custom_call" | custom-call | flops 1 | bytes 1 | tf_op jit(solution)/shard_map/pallas_call | solution.py:275
  16.3 1.5 %shard_map.121.refs_1_ = f32[1024,128]{1,0:T(8,128)S(1)} custom-call(bf16[1024,128]{1,0:T(8,128)(2,1)S(1)} %collective-permute-done.far.refs_0_, bf16[1024,128]{1,0:T(8,128)(2,1)S(1)} %get-tuple-element.17.own.refs_1_, f32[16,128]{1,0:T(8,128)S(1)} %get-tuple-element.18.refs_2_, f32[128,512]{1,0:T(8,128)S(1)} %get-tuple-element.15.spectrum.refs_3_, ...), custom_call_target="tpu_custom_call" | custom-call | flops 1 | bytes 1 | tf_op jit(solution)/shard_map/pallas_call | solution.py:275
  17.8 0.0 collective-permute-done.2.refs_0_
  17.8 1.5 %shard_map.122 = (f32[128,1024]{1,0:T(8,128)S(1)}, bf16[128,1024]{1,0:T(8,128)(2,1)S(1)}) custom-call(bf16[1024,128]{1,0:T(8,128)(2,1)S(1)} %collective-permute-done.2.refs_0_, f32[1024,128]{1,0:T(8,128)S(1)} %shard_map.121.refs_1_, bf16[2048,128]{1,0:T(8,128)(2,1)S(1)} %get-tuple-element.19.refs_2_.query, ...), custom_call_target="tpu_custom_call" | custom-call | flops 1 | bytes 1 | tf_op jit(solution)/shard_map/pallas_call | solution.py:275
  19.3 0.1 collective-permute-done.3.carried
  19.4 0.5 %shard_map.124 = (bf16[128,1024]{1,0:T(8,128)(2,1)S(1)}, bf16[128,1024]{1,0:T(8,128)(2,1)S(1)}) custom-call(bf16[1024,128]{1,0:T(8,128)(2,1)S(1)} %collective-permute-done.3.carried, f32[1024,128]{1,0:T(8,128)S(1)} %shard_map.123.base, bf16[2048,128]{1,0:T(8,128)(2,1)S(1)} %get-tuple-element.19.refs_2_.query, ...), custom_call_target="tpu_custom_call" | custom-call | flops 1 | bytes 1 | tf_op jit(solution)/shard_map/pallas_call | solution.py:275
  19.9 2.8 %collective-permute-start.4 = (bf16[128,1024]{1,0:T(8,128)(2,1)S(1)}, bf16[128,1024]{1,0:T(8,128)(2,1)S(1)}, u32[]{:S(2)}, u32[]{:S(2)}) collective-permute-start(bf16[128,1024]{1,0:T(8,128)(2,1)S(1)} %get-tuple-element.24), channel_id=1, source_target_pairs={{0,1},{1,0},{2,3},{3,2},{4,5},{5,4},{6,7},{7,6},{8,9},{9,8},{10,11... | collective-permute-start | bytes 786440 | tf_op jit(solution)/shard_map/ppermute | solution.py:317
  22.7 0.7 %shard_map.125 = f32[128,1024]{1,0:T(8,128)S(1)} custom-call(bf16[128,1024]{1,0:T(8,128)(2,1)S(1)} %get-tuple-element.21.gated_a, bf16[128,1024]{1,0:T(8,128)(2,1)S(1)} %get-tuple-element.23.gated_b, bf16[2048,2048]{1,0:T(8,128)(2,1)S(1)} %get-tuple-element.20.refs_5_.weight), custom_call_target="tpu_custom_call" | custom-call | flops 1 | bytes 1 | tf_op jit(solution)/shard_map/pallas_call | solution.py:275
  23.4 0.4 %collective-permute-done.4 = bf16[128,1024]{1,0:T(8,128)(2,1)S(1)} collective-permute-done((bf16[128,1024]{1,0:T(8,128)(2,1)S(1)}, bf16[128,1024]{1,0:T(8,128)(2,1)S(1)}, u32[]{:S(2)}, u32[]{:S(2)}) %collective-permute-start.4) | collective-permute-done | bytes 262176 | tf_op jit(solution)/shard_map/ppermute | solution.py:317
  23.8 0.8 %add_convert_fusion = bf16[128,1024]{1,0:T(8,128)(2,1)} fusion(f32[128,1024]{1,0:T(8,128)S(1)} %shard_map.125, bf16[128,1024]{1,0:T(8,128)(2,1)S(1)} %collective-permute-done.4), kind=kLoop, calls=%fused_computation | loop fusion | flops 393216 | bytes 1048576 | tf_op jit(solution)/shard_map/convert_element_type | solution.py:319
Async XLA Ops:
  1.3 7.2 %collective-permute-start.1 = (bf16[1024,128]{1,0:T(8,128)(2,1)S(1)}, bf16[1024,128]{1,0:T(8,128)(2,1)S(1)}, u32[]{:S(2)}, u32[]{:S(2)}) collective-permute-start(bf16[1024,128]{1,0:T(8,128)(2,1)S(1)} %get-tuple-element.25.own.refs_1_), channel_id=1, source_target_pairs={{0,2},{2,0},{4,6},{6,4},{8,10},{10,8},{12,14},{14,12},{1,3},{3,1},... | collective-permute-start | bytes 786440 | tf_op jit(solution)/shard_map/ppermute | solution.py:208
  2.6 7.5 %collective-permute-start = (bf16[1024,128]{1,0:T(8,128)(2,1)S(1)}, bf16[1024,128]{1,0:T(8,128)(2,1)S(1)}, u32[]{:S(2)}, u32[]{:S(2)}) collective-permute-start(bf16[1024,128]{1,0:T(8,128)(2,1)S(1)} %get-tuple-element.17.own.refs_1_), channel_id=1, source_target_pairs={{0,4},{2,6},{4,8},{6,10},{8,12},{10,14},{12,0},{14,2},{1,5},{3,7},... | collective-permute-start | bytes 786440 | tf_op jit(solution)/shard_map/ppermute | solution.py:204
  10.2 7.6 %collective-permute-start.2 = (bf16[1024,128]{1,0:T(8,128)(2,1)S(1)}, bf16[1024,128]{1,0:T(8,128)(2,1)S(1)}, u32[]{:S(2)}, u32[]{:S(2)}) collective-permute-start(bf16[1024,128]{1,0:T(8,128)(2,1)S(1)} %shard_map.120), channel_id=1, source_target_pairs={{0,2},{2,0},{4,6},{6,4},{8,10},{10,8},{12,14},{14,12},{1,3},{3,1},... | collective-permute-start | bytes 786440 | tf_op jit(solution)/shard_map/ppermute | solution.py:208
  11.5 7.9 %collective-permute-start.3 = (bf16[1024,128]{1,0:T(8,128)(2,1)S(1)}, bf16[1024,128]{1,0:T(8,128)(2,1)S(1)}, u32[]{:S(2)}, u32[]{:S(2)}) collective-permute-start(bf16[1024,128]{1,0:T(8,128)(2,1)S(1)} %shard_map.119), channel_id=1, source_target_pairs={{0,4},{2,6},{4,8},{6,10},{8,12},{10,14},{1,5},{3,7},{5,9},{7,11},{... | collective-permute-start | bytes 786440 | tf_op jit(solution)/shard_map/ppermute | solution.py:204
  19.9 4.0 %collective-permute-start.4 = (bf16[128,1024]{1,0:T(8,128)(2,1)S(1)}, bf16[128,1024]{1,0:T(8,128)(2,1)S(1)}, u32[]{:S(2)}, u32[]{:S(2)}) collective-permute-start(bf16[128,1024]{1,0:T(8,128)(2,1)S(1)} %get-tuple-element.24), channel_id=1, source_target_pairs={{0,1},{1,0},{2,3},{3,2},{4,5},{5,4},{6,7},{7,6},{8,9},{9,8},{10,11... | collective-permute-start | bytes 786440 | tf_op jit(solution)/shard_map/ppermute | solution.py:317

commit v7 on v6

--- a/solution.py
+++ b/solution.py
@@ -13,6 +13,7 @@
 TAIL_COST = 1
 VMEM_BYTES = 24 * 1024 * 1024
 RELAYED = 1024
+TILE = 256
 WRAP_FAR = True
 WRAP_SENT = False
 
@@ -44,7 +45,7 @@
     for copy in copies[:7]:
         copy.wait()
     seed, f_in, bias, f_out, decay, reach = local
-    window = table.shape[0] // 2 - block
+    window = (table.shape[0] - block) // 2
     lags = window - block
     lag = lax.broadcasted_iota(jnp.int32, (lags, 1), 0)
     if seq_len & (seq_len - 1) == 0:
@@ -67,18 +68,15 @@
         copy.wait()
 
 
-def transform(window, places, offsets, xs, valid, table, start, tile):
+def transform(places, xs, valid, table, start, tile):
     block = xs[0].shape[1]
-    blocks, factors = [], []
-    for offset, x, there in zip(offsets, xs, valid):
-        rows = x[offset + start : offset + start + tile]
+    blocks = []
+    for x, there in zip(xs, valid):
+        rows = x[start : start + tile]
         blocks.append(rows if there is None else jnp.where(there, rows, jnp.zeros_like(rows)))
-    for base in (0, window):
-        factors += [table[base + place * block : base + (place + 1) * block] for place in places]
+    factors = [table[place * block : (place + 1) * block] for place in places]
     return jnp.dot(
-        jnp.concatenate(blocks + blocks, axis=1),
-        jnp.concatenate(factors, axis=0),
-        preferred_element_type=jnp.float32,
+        jnp.concatenate(blocks, axis=1), jnp.concatenate(factors, axis=0), preferred_element_type=jnp.float32
     )
 
 
@@ -95,26 +93,34 @@
         hc, hs = spectrum[group + g : group + g + 1, :half], spectrum[group + g : group + g + 1, half:]
         xc, xs = part[:, :half], part[:, half:]
         mult.append(jnp.concatenate([xc * hc - xs * hs, xc * hs + xs * hc], axis=1).astype(jnp.bfloat16))
+    block = table.shape[0] - 2 * window
     both = lax.dot_general(
         jnp.concatenate(mult, axis=0),
-        table[2 * window :],
+        table[2 * window - block :],
         (((1,), (1,)), ((), ())),
         preferred_element_type=jnp.float32,
     )
-    block = both.shape[1] // 2
     return both[:, :block] + both[:, block:]
 
 
-def tiles_of(channels):
-    return [(start, min(256, channels - start)) for start in range(0, channels, 256)]
+def in_stages(channels, first, second):
+    tiles = [(start, min(TILE, channels - start)) for start in range(0, channels, TILE)]
+    ready = first(*tiles[0])
+    for k, tile in enumerate(tiles):
+        now = ready
+        if k + 1 < len(tiles):
+            ready = first(*tiles[k + 1])
+        second(*tile, now)
 
 
 def ahead_kernel(window, per_group, first, own, other, spectrum, table, out):
     even = lax.axis_index("seq") % 2 == 0
-    for start, tile in tiles_of(out.shape[0]):
-        freq = transform(window, (0, 1), (0, 0), (own, other), (None, even), table, start, tile)
+
+    def give(start, tile, freq):
         ahead = respond(freq, (first + start) // per_group, per_group, window, spectrum, table)
         out[start : start + tile] = ahead.astype(out.dtype)
+
+    in_stages(out.shape[0], functools.partial(transform, (0, 1), (own, other), (None, even), table), give)
 
 
 def gains(skip, row, block):
@@ -127,22 +133,24 @@
     block = out.shape[1]
     odd = lax.axis_index("seq") % 2 == 1
     valid = [odd if odd_only else block_there(window, block, place) for place in places[:-1]] + [None]
-    for start, tile in tiles_of(out.shape[0]):
-        freq = transform(window, places, [0] * len(xs), xs, valid, table, start, tile)
+
+    def give(start, tile, freq):
         mixed = respond(freq, (first + start) // per_group, per_group, window, spectrum, table)
         for low in range(0, tile, 128):
             here = slice(start + low, start + low + 128)
             gain = gains(skip, (first + start + low) // 128, block)
             out[here] = mixed[low : low + 128] + gain * xs[-1][here].astype(jnp.float32)
 
+    in_stages(out.shape[0], functools.partial(transform, places, xs, valid, table), give)
+
 
 def last_kernel(first, carried, base, query, weight, before, part, gated_t):
     there = column_halves(weight)[1]
     arrived = lax.axis_index("seq") >= 2
-    for start, tile in tiles_of(base.shape[0]):
-        rows = slice(start, start + tile)
+    for start in range(0, base.shape[0], 128):
+        rows = slice(start, start + 128)
         mixed = base[rows] + jnp.where(arrived, carried[rows].astype(jnp.float32), 0.0)
-        gated = query[first + start : first + start + tile].astype(jnp.float32) * mixed
+        gated = query[first + start : first + start + 128].astype(jnp.float32) * mixed
         gated_t[:, rows] = gated.astype(jnp.bfloat16).T
     total = jnp.dot(gated_t[...], weight[first:, there], preferred_element_type=jnp.float32)
     part[...] = (before[...] + total).astype(part.dtype)
@@ -170,17 +178,18 @@
         gated = query[first + start : first + start + tile].astype(jnp.float32) * mixed
         gated_t[:, start : start + tile] = gated.astype(jnp.bfloat16).T
 
+    def add(start, tile, freq):
+        mixed = respond(freq, (first + start) // per_group, per_group, window, spectrum, table)
+        gate(start, tile, base[start : start + tile] + mixed)
+
     @pl.when(seq > 0)
     def _():
-        for start, tile in tiles_of(channels):
-            freq = transform(window, places, [0] * len(xs), xs, valid, table, start, tile)
-            mixed = respond(freq, (first + start) // per_group, per_group, window, spectrum, table)
-            gate(start, tile, base[start : start + tile] + mixed)
+        in_stages(channels, functools.partial(transform, places, xs, valid, table), add)
 
     @pl.when(seq == 0)
     def _():
-        for start, tile in tiles_of(channels):
-            gate(start, tile, base[start : start + tile])
+        for start in range(0, channels, 128):
+            gate(start, 128, base[start : start + 128])
 
     there = column_halves(weight)[1]
     total = jnp.dot(gated_t[...], weight[first : first + channels, there], preferred_element_type=jnp.float32)
@@ -229,7 +238,7 @@
     lags = reach_max * block
     window = lags + block
     (fwd_hi, fwd_lo), (inv_hi, inv_lo) = transform_tables(window, lags, block)
-    table = np.concatenate([fwd_hi, fwd_lo, inv_hi.T, inv_lo.T], axis=0)
+    table = np.concatenate([fwd_hi, fwd_lo[:lags], inv_hi.T, inv_lo.T], axis=0)
     length = table.shape[1]
     out_cols = out_weight.shape[1]
     cols = out_cols // 2
@@ -298,7 +307,7 @@
             shape(own_b.shape, bf16),
         )
         carried = shift(sent, 2, WRAP_SENT)
-        ready, _ = lax.optimization_barrier((own_a, sent))
+        ready, _ = lax.optimization_barrier((own_a, spectrum))
         (handed,) = kernel(hand_kernel, (far, ready), shape(own_a.shape, bf16))
         near = swap_pairs(handed)
         base_a = base(0, {0: far, 2: own_a})

time: 25 us -> 24.3 us (0.972)
  Pallas kernels: 11.4 us -> 9.04 us
  waiting for transfers between devices: 1.09 us -> 2.81 us
    pallas_call x7, Pallas kernels: 7.38 us -> 5.03 us  [kernel(): pl.pallas_call(call, in_specs=[vmem] * len(ins), out_specs=[vmem] * len(o...]
    ppermute x2, waiting for transfers between devices: 0.06 us -> 2.37 us  [shift(): lax.ppermute(array, 'seq', [(i, (i + back) % count) for i in range(count...]
    ppermute x2, waiting for transfers between devices: 0.59 us -> 0.01 us  [swap_pairs(): lax.ppermute(array, 'seq', [(i, i ^ 1) for i in range(lax.axis_size('seq'...]
  transfers between devices with their start and end apart: 5 -> 5, of which waited for: 3 -> 3; matrix products, arithmetic and copies ran while one was open for 0% -> 0% of each run, Pallas kernels for 44% -> 36%
where the time goes in v7:
time: 24.3 us; the launch traced here: 23.9 us
  starting transfers between devices  9.89 us (41%)
  Pallas kernels  9.04 us (37%)
  waiting for transfers between devices  2.81 us (12%)
  other arithmetic  2.08 us (9%)
    pallas_call x7, Pallas kernels, kernel(): pl.pallas_call(call, in_specs=[vmem] * len(ins), out_specs=[vmem] * len(o...  5.03 us
    ppermute x2, starting transfers between devices, shift(): lax.ppermute(array, 'seq', [(i, (i + back) % count) for i in range(count...  4.56 us
    pallas_call x1, Pallas kernels, body(): pl.pallas_call(lambda *refs: setup_kernel(block * seq_count, block, 1.0 /...  4.01 us
    ppermute x1, starting transfers between devices, body(): received = lax.ppermute(sums, 'chan', [(0, 1), (1, 0)])  2.79 us
    ppermute x2, starting transfers between devices, swap_pairs(): lax.ppermute(array, 'seq', [(i, i ^ 1) for i in range(lax.axis_size('seq'...  2.54 us
    ppermute x2, waiting for transfers between devices, shift(): lax.ppermute(array, 'seq', [(i, (i + back) % count) for i in range(count...  2.37 us
    convert_element_type x1, other arithmetic, body(): (key_feat[low:high].astype(f32) * value_feat[low:high].astype(f32)).astyp...  1.32 us
    convert_element_type x1, other arithmetic, body(): return (own + received.astype(f32)).astype(bf16)  0.76 us
  transfers between devices with their start and end apart: 5, of which 3 were waited for; matrix products, arithmetic and copies ran while one was open for 0% of the time, Pallas kernels for 36%

profile of v7, /device:TPU:9, one launch (start us, length us, event | category | flops | bytes accessed | tf_op | source)
XLA Modules:
  0.0 23.9 jit_solution(7827542862414314600)
XLA Ops:
  0.0 1.3 %multiply_convert_fusion = (bf16[1024,128]{1,0:T(8,128)(2,1)S(1)}, bf16[1024,128]{1,0:T(8,128)(2,1)S(1)}) fusion(bf16[2048,128]{1,0:T(8,128)(2,1)} %param.14, bf16[2048,128]{1,0:T(8,128)(2,1)} %param.13), kind=kLoop, calls=%fused_computation.1 | loop fusion | flops 1048576 | bytes 1572864 | tf_op jit(solution)/shard_map/convert_element_type | solution.py:251
  1.3 1.3 %collective-permute-start = (bf16[1024,128]{1,0:T(8,128)(2,1)S(1)}, bf16[1024,128]{1,0:T(8,128)(2,1)S(1)}, u32[]{:S(2)}, u32[]{:S(2)}) collective-permute-start(bf16[1024,128]{1,0:T(8,128)(2,1)S(1)} %get-tuple-element.16.own.refs_1_), channel_id=1, source_target_pairs={{0,4},{2,6},{4,8},{6,10},{8,12},{10,14},{12,0},{14,2},{1,5},{3,7},... | collective-permute-start | bytes 786440 | tf_op jit(solution)/shard_map/ppermute | solution.py:213
  2.7 1.2 %collective-permute-start.2 = (bf16[1024,128]{1,0:T(8,128)(2,1)S(1)}, bf16[1024,128]{1,0:T(8,128)(2,1)S(1)}, u32[]{:S(2)}, u32[]{:S(2)}) collective-permute-start(bf16[1024,128]{1,0:T(8,128)(2,1)S(1)} %get-tuple-element.25.own.refs_1_), channel_id=1, source_target_pairs={{0,2},{2,0},{4,6},{6,4},{8,10},{10,8},{12,14},{14,12},{1,3},{3,1},... | collective-permute-start | bytes 786440 | tf_op jit(solution)/shard_map/ppermute | solution.py:217
  3.9 4.0 %shard_map.118 = (f32[128,512]{1,0:T(8,128)S(1)}, bf16[896,512]{1,0:T(8,128)(2,1)S(1)}, bf16[2048,128]{1,0:T(8,128)(2,1)S(1)}, f32[16,128]{1,0:T(8,128)S(1)}, bf16[2048,2048]{1,0:T(8,128)(2,1)S(1)}) custom-call(s32[1,16]{1,0:T(1,128)} %bitcast.6, f32[32,64]{1,0:T(8,128)} %refs_1_.1, f32[1,64]{1,0:T(1,128)} %bitcast.7, f32[64,128]{1,0:T(8,128)} %refs_3_.1, ...), custom_call_target="tpu_custom_call" | custom-call | flops 1 | bytes 30000000 | tf_op jit(solution)/shard_map/pallas_call | solution.py:272
  7.9 0.6 %collective-permute-done.far.refs_0_ = bf16[1024,128]{1,0:T(8,128)(2,1)S(1)} collective-permute-done((bf16[1024,128]{1,0:T(8,128)(2,1)S(1)}, bf16[1024,128]{1,0:T(8,128)(2,1)S(1)}, u32[]{:S(2)}, u32[]{:S(2)}) %collective-permute-start) | collective-permute-done | bytes 262176 | tf_op jit(solution)/shard_map/ppermute | solution.py:213
  8.6 0.1 shard_map.119
  8.6 1.3 %collective-permute-start.1 = (bf16[1024,128]{1,0:T(8,128)(2,1)S(1)}, bf16[1024,128]{1,0:T(8,128)(2,1)S(1)}, u32[]{:S(2)}, u32[]{:S(2)}) collective-permute-start(bf16[1024,128]{1,0:T(8,128)(2,1)S(1)} %shard_map.119), channel_id=1, source_target_pairs={{0,2},{2,0},{4,6},{6,4},{8,10},{10,8},{12,14},{14,12},{1,3},{3,1},... | collective-permute-start | bytes 786440 | tf_op jit(solution)/shard_map/ppermute | solution.py:217
  9.9 0.0 collective-permute-done.2.other.refs_0_
  9.9 0.8 %shard_map.122 = bf16[1024,128]{1,0:T(8,128)(2,1)S(1)} custom-call(bf16[1024,128]{1,0:T(8,128)(2,1)S(1)} %get-tuple-element.25.own.refs_1_, bf16[1024,128]{1,0:T(8,128)(2,1)S(1)} %collective-permute-done.2.other.refs_0_, f32[128,512]{1,0:T(8,128)S(1)} %get-tuple-element.15.refs_3_.spectrum, bf16[896,512]{1,0:T(8,128)(2,1)S(1)} %get-tuple-element.18.refs_4_.table), custom_call_target="tpu_custom_call" | custom-call | flops 1 | bytes 1 | tf_op jit(solution)/shard_map/pallas_call | solution.py:284
  10.7 3.2 %collective-permute-start.3 = (bf16[1024,128]{1,0:T(8,128)(2,1)S(1)}, bf16[1024,128]{1,0:T(8,128)(2,1)S(1)}, u32[]{:S(2)}, u32[]{:S(2)}) collective-permute-start(bf16[1024,128]{1,0:T(8,128)(2,1)S(1)} %shard_map.122), channel_id=1, source_target_pairs={{0,4},{2,6},{4,8},{6,10},{8,12},{10,14},{1,5},{3,7},{5,9},{7,11},{... | collective-permute-start | bytes 786440 | tf_op jit(solution)/shard_map/ppermute | solution.py:213
  13.9 0.8 %shard_map.120.refs_1_ = f32[1024,128]{1,0:T(8,128)S(1)} custom-call(bf16[1024,128]{1,0:T(8,128)(2,1)S(1)} %collective-permute-done.far.refs_0_, bf16[1024,128]{1,0:T(8,128)(2,1)S(1)} %get-tuple-element.16.own.refs_1_, f32[16,128]{1,0:T(8,128)S(1)} %get-tuple-element.17.refs_2_, f32[128,512]{1,0:T(8,128)S(1)} %get-tuple-element.15.refs_3_.spectrum, ...), custom_call_target="tpu_custom_call" | custom-call | flops 1 | bytes 1 | tf_op jit(solution)/shard_map/pallas_call | solution.py:284
  14.8 0.8 %shard_map.123.base = f32[1024,128]{1,0:T(8,128)S(1)} custom-call(bf16[1024,128]{1,0:T(8,128)(2,1)S(1)} %collective-permute-done.2.other.refs_0_, bf16[1024,128]{1,0:T(8,128)(2,1)S(1)} %get-tuple-element.25.own.refs_1_, f32[16,128]{1,0:T(8,128)S(1)} %get-tuple-element.17.refs_2_, f32[128,512]{1,0:T(8,128)S(1)} %get-tuple-element.15.refs_3_.spectrum, ...), custom_call_target="tpu_custom_call" | custom-call | flops 1 | bytes 1 | tf_op jit(solution)/shard_map/pallas_call | solution.py:284
  15.6 0.0 collective-permute-done.1.refs_0_
  15.6 1.3 %shard_map.121 = (f32[128,1024]{1,0:T(8,128)S(1)}, bf16[128,1024]{1,0:T(8,128)(2,1)S(1)}) custom-call(bf16[1024,128]{1,0:T(8,128)(2,1)S(1)} %collective-permute-done.1.refs_0_, f32[1024,128]{1,0:T(8,128)S(1)} %shard_map.120.refs_1_, bf16[2048,128]{1,0:T(8,128)(2,1)S(1)} %get-tuple-element.19.refs_2_.query, ...), custom_call_target="tpu_custom_call" | custom-call | flops 1 | bytes 1 | tf_op jit(solution)/shard_map/pallas_call | solution.py:284
  16.9 1.7 %collective-permute-done.3.carried = bf16[1024,128]{1,0:T(8,128)(2,1)S(1)} collective-permute-done((bf16[1024,128]{1,0:T(8,128)(2,1)S(1)}, bf16[1024,128]{1,0:T(8,128)(2,1)S(1)}, u32[]{:S(2)}, u32[]{:S(2)}) %collective-permute-start.3) | collective-permute-done | bytes 262176 | tf_op jit(solution)/shard_map/ppermute | solution.py:213
  18.6 0.5 %shard_map.124 = (bf16[128,1024]{1,0:T(8,128)(2,1)S(1)}, bf16[128,1024]{1,0:T(8,128)(2,1)S(1)}) custom-call(bf16[1024,128]{1,0:T(8,128)(2,1)S(1)} %collective-permute-done.3.carried, f32[1024,128]{1,0:T(8,128)S(1)} %shard_map.123.base, bf16[2048,128]{1,0:T(8,128)(2,1)S(1)} %get-tuple-element.19.refs_2_.query, ...), custom_call_target="tpu_custom_call" | custom-call | flops 1 | bytes 1 | tf_op jit(solution)/shard_map/pallas_call | solution.py:284
  19.2 2.8 %collective-permute-start.4 = (bf16[128,1024]{1,0:T(8,128)(2,1)S(1)}, bf16[128,1024]{1,0:T(8,128)(2,1)S(1)}, u32[]{:S(2)}, u32[]{:S(2)}) collective-permute-start(bf16[128,1024]{1,0:T(8,128)(2,1)S(1)} %get-tuple-element.24), channel_id=1, source_target_pairs={{0,1},{1,0},{2,3},{3,2},{4,5},{5,4},{6,7},{7,6},{8,9},{9,8},{10,11... | collective-permute-start | bytes 786440 | tf_op jit(solution)/shard_map/ppermute | solution.py:326
  22.0 0.7 %shard_map.125 = f32[128,1024]{1,0:T(8,128)S(1)} custom-call(bf16[128,1024]{1,0:T(8,128)(2,1)S(1)} %get-tuple-element.21.gated_a, bf16[128,1024]{1,0:T(8,128)(2,1)S(1)} %get-tuple-element.23.gated_b, bf16[2048,2048]{1,0:T(8,128)(2,1)S(1)} %get-tuple-element.20.refs_5_.weight), custom_call_target="tpu_custom_call" | custom-call | flops 1 | bytes 1 | tf_op jit(solution)/shard_map/pallas_call | solution.py:284
  22.7 0.4 %collective-permute-done.4 = bf16[128,1024]{1,0:T(8,128)(2,1)S(1)} collective-permute-done((bf16[128,1024]{1,0:T(8,128)(2,1)S(1)}, bf16[128,1024]{1,0:T(8,128)(2,1)S(1)}, u32[]{:S(2)}, u32[]{:S(2)}) %collective-permute-start.4) | collective-permute-done | bytes 262176 | tf_op jit(solution)/shard_map/ppermute | solution.py:326
  23.1 0.8 %add_convert_fusion = bf16[128,1024]{1,0:T(8,128)(2,1)} fusion(f32[128,1024]{1,0:T(8,128)S(1)} %shard_map.125, bf16[128,1024]{1,0:T(8,128)(2,1)S(1)} %collective-permute-done.4), kind=kLoop, calls=%fused_computation | loop fusion | flops 393216 | bytes 1048576 | tf_op jit(solution)/shard_map/convert_element_type | solution.py:328
Async XLA Ops:
  1.3 7.2 %collective-permute-start = (bf16[1024,128]{1,0:T(8,128)(2,1)S(1)}, bf16[1024,128]{1,0:T(8,128)(2,1)S(1)}, u32[]{:S(2)}, u32[]{:S(2)}) collective-permute-start(bf16[1024,128]{1,0:T(8,128)(2,1)S(1)} %get-tuple-element.16.own.refs_1_), channel_id=1, source_target_pairs={{0,4},{2,6},{4,8},{6,10},{8,12},{10,14},{12,0},{14,2},{1,5},{3,7},... | collective-permute-start | bytes 786440 | tf_op jit(solution)/shard_map/ppermute | solution.py:213
  2.7 7.3 %collective-permute-start.2 = (bf16[1024,128]{1,0:T(8,128)(2,1)S(1)}, bf16[1024,128]{1,0:T(8,128)(2,1)S(1)}, u32[]{:S(2)}, u32[]{:S(2)}) collective-permute-start(bf16[1024,128]{1,0:T(8,128)(2,1)S(1)} %get-tuple-element.25.own.refs_1_), channel_id=1, source_target_pairs={{0,2},{2,0},{4,6},{6,4},{8,10},{10,8},{12,14},{14,12},{1,3},{3,1},... | collective-permute-start | bytes 786440 | tf_op jit(solution)/shard_map/ppermute | solution.py:217
  8.6 6.9 %collective-permute-start.1 = (bf16[1024,128]{1,0:T(8,128)(2,1)S(1)}, bf16[1024,128]{1,0:T(8,128)(2,1)S(1)}, u32[]{:S(2)}, u32[]{:S(2)}) collective-permute-start(bf16[1024,128]{1,0:T(8,128)(2,1)S(1)} %shard_map.119), channel_id=1, source_target_pairs={{0,2},{2,0},{4,6},{6,4},{8,10},{10,8},{12,14},{14,12},{1,3},{3,1},... | collective-permute-start | bytes 786440 | tf_op jit(solution)/shard_map/ppermute | solution.py:217
  10.7 7.9 %collective-permute-start.3 = (bf16[1024,128]{1,0:T(8,128)(2,1)S(1)}, bf16[1024,128]{1,0:T(8,128)(2,1)S(1)}, u32[]{:S(2)}, u32[]{:S(2)}) collective-permute-start(bf16[1024,128]{1,0:T(8,128)(2,1)S(1)} %shard_map.122), channel_id=1, source_target_pairs={{0,4},{2,6},{4,8},{6,10},{8,12},{10,14},{1,5},{3,7},{5,9},{7,11},{... | collective-permute-start | bytes 786440 | tf_op jit(solution)/shard_map/ppermute | solution.py:213
  19.2 4.0 %collective-permute-start.4 = (bf16[128,1024]{1,0:T(8,128)(2,1)S(1)}, bf16[128,1024]{1,0:T(8,128)(2,1)S(1)}, u32[]{:S(2)}, u32[]{:S(2)}) collective-permute-start(bf16[128,1024]{1,0:T(8,128)(2,1)S(1)} %get-tuple-element.24), channel_id=1, source_target_pairs={{0,1},{1,0},{2,3},{3,2},{4,5},{5,4},{6,7},{7,6},{8,9},{9,8},{10,11... | collective-permute-start | bytes 786440 | tf_op jit(solution)/shard_map/ppermute | solution.py:326

commit v8 on v7

--- a/solution.py
+++ b/solution.py
@@ -13,7 +13,7 @@
 TAIL_COST = 1
 VMEM_BYTES = 24 * 1024 * 1024
 RELAYED = 1024
-TILE = 256
+TILE = 512
 WRAP_FAR = True
 WRAP_SENT = False
 
@@ -144,24 +144,47 @@
     in_stages(out.shape[0], functools.partial(transform, places, xs, valid, table), give)
 
 
-def last_kernel(first, carried, base, query, weight, before, part, gated_t):
-    there = column_halves(weight)[1]
-    arrived = lax.axis_index("seq") >= 2
-    for start in range(0, base.shape[0], 128):
-        rows = slice(start, start + 128)
-        mixed = base[rows] + jnp.where(arrived, carried[rows].astype(jnp.float32), 0.0)
-        gated = query[first + start : first + start + 128].astype(jnp.float32) * mixed
-        gated_t[:, rows] = gated.astype(jnp.bfloat16).T
-    total = jnp.dot(gated_t[...], weight[first:, there], preferred_element_type=jnp.float32)
-    part[...] = (before[...] + total).astype(part.dtype)
-
-
 def column_halves(weight):
     cols = weight.shape[1] // 2
     core = lax.axis_index("chan")
     return [pl.ds(pl.multiple_of(part * cols, 128), cols) for part in (core, 1 - core)]
 
 
+def gate(first, query, gated_t, start, mixed):
+    rows = slice(start, start + mixed.shape[0])
+    gated = query[first + start : first + start + mixed.shape[0]].astype(jnp.float32) * mixed
+    gated_t[:, rows] = gated.astype(jnp.bfloat16).T
+
+
+def first_block_kernel(splits, base_a, base_b, query, weight, gated_a, gated_b, part):
+    there = column_halves(weight)[1]
+
+    @pl.when(lax.axis_index("seq") == 0)
+    def _():
+        total = 0.0
+        for first, base, gated_t in zip(splits, (base_a, base_b), (gated_a, gated_b)):
+            channels = base.shape[0]
+            for start in range(0, channels, 128):
+                gate(first, query, gated_t, start, base[start : start + 128])
+            total += jnp.dot(
+                gated_t[...], weight[first : first + channels, there], preferred_element_type=jnp.float32
+            )
+        part[...] = total.astype(part.dtype)
+
+
+def last_kernel(first, carried, base, query, weight, before, gated_in, part_in, gated_t, part):
+    there = column_halves(weight)[1]
+    seq = lax.axis_index("seq")
+
+    @pl.when(seq > 0)
+    def _():
+        for start in range(0, base.shape[0], 128):
+            rows = slice(start, start + 128)
+            gate(first, query, gated_t, start, base[rows] + jnp.where(seq >= 2, carried[rows].astype(jnp.float32), 0.0))
+        total = jnp.dot(gated_t[...], weight[first:, there], preferred_element_type=jnp.float32)
+        part[...] = (before[...] + total).astype(part.dtype)
+
+
 def hand_kernel(far, own, out):
     out[...] = jnp.where(lax.axis_index("seq") % 2 == 1, far[...], own[...])
 
@@ -169,33 +192,23 @@
 def part_kernel(window, places, per_group, first, is_first, *refs):
     xs, refs = refs[: len(places)], refs[len(places) :]
     (base, query, spectrum, table, weight), refs = refs[:5], refs[5:]
-    part, gated_t = refs[-2:]
+    gated_t, part = refs[-2:]
     block, channels = gated_t.shape
     seq = lax.axis_index("seq")
     valid = [block_there(window, block, place) for place in places]
-
-    def gate(start, tile, mixed):
-        gated = query[first + start : first + start + tile].astype(jnp.float32) * mixed
-        gated_t[:, start : start + tile] = gated.astype(jnp.bfloat16).T
+    there = column_halves(weight)[1]
 
     def add(start, tile, freq):
         mixed = respond(freq, (first + start) // per_group, per_group, window, spectrum, table)
-        gate(start, tile, base[start : start + tile] + mixed)
+        gate(first, query, gated_t, start, base[start : start + tile] + mixed)
 
     @pl.when(seq > 0)
     def _():
         in_stages(channels, functools.partial(transform, places, xs, valid, table), add)
-
-    @pl.when(seq == 0)
-    def _():
-        for start in range(0, channels, 128):
-            gate(start, 128, base[start : start + 128])
-
-    there = column_halves(weight)[1]
-    total = jnp.dot(gated_t[...], weight[first : first + channels, there], preferred_element_type=jnp.float32)
-    if not is_first:
-        total = refs[0][...] + total
-    part[...] = total.astype(part.dtype)
+        total = jnp.dot(gated_t[...], weight[first : first + channels, there], preferred_element_type=jnp.float32)
+        if not is_first:
+            total = refs[0][...] + total
+        part[...] = total.astype(part.dtype)
 
 
 def own_kernel(gated_a, gated_b, weight, out):
@@ -280,12 +293,13 @@
         cost_estimate=cost(SETUP_COST),
     )(*[pltpu.with_memory_space_constraint(a, pltpu.HBM) for a in small + large], weight_in)
 
-    def kernel(call, ins, *outs):
+    def kernel(call, ins, *outs, aliases={}):
         return pl.pallas_call(
             call,
             in_specs=[vmem] * len(ins),
             out_specs=[vmem] * len(outs),
             out_shape=outs,
+            input_output_aliases=aliases,
             compiler_params=params,
             cost_estimate=cost(TAIL_COST),
         )(*ins)
@@ -294,10 +308,20 @@
         call = functools.partial(base_kernel, window, tuple(blocks), odd_only, per_group, first)
         return kernel(call, (*blocks.values(), skip, spectrum, table), shape(blocks[reach_max].shape, f32))[0]
 
-    def part(first, late, early, sums, dtype):
-        ins = (*late.values(), early, query, spectrum, table, weight, *sums)
+    def first_block(base_a, base_b):
+        shapes = [shape((block, base.shape[0]), bf16) for base in (base_a, base_b)]
+        call = functools.partial(first_block_kernel, (0, RELAYED))
+        return kernel(call, (base_a, base_b, query, weight), *shapes, shape((block, cols), bf16))
+
+    def part(first, late, early, sums, gated, total=None):
+        ins = (*late.values(), early, query, spectrum, table, weight, *sums, gated)
+        aliases = {len(ins) - 1: 0}
+        outs = [shape(gated.shape, bf16), shape((block, cols), f32)]
+        if total is not None:
+            aliases[len(ins)] = 1
+            ins, outs[1] = (*ins, total), shape(total.shape, bf16)
         call = functools.partial(part_kernel, window, tuple(late), per_group, first, not sums)
-        return kernel(call, ins, shape((block, cols), dtype), shape((block, early.shape[0]), bf16))
+        return kernel(call, ins, *outs, aliases=aliases)
 
     own_a, own_b = products
     if reach_max == 2:
@@ -312,17 +336,21 @@
         near = swap_pairs(handed)
         base_a = base(0, {0: far, 2: own_a})
         base_b = base(RELAYED, {1: other, 2: own_b}, True)
-        sums, gated_a = part(0, {1: near}, base_a, (), f32)
-        sums, gated_b = kernel(
+        gated_a, gated_b, sums_b = first_block(base_a, base_b)
+        gated_a, sums_a = part(0, {1: near}, base_a, (), gated_a)
+        gated_b, sums = kernel(
             functools.partial(last_kernel, RELAYED),
-            (carried, base_b, query, weight, sums),
-            shape((block, cols), bf16),
-            shape((block, channels - RELAYED), bf16),
+            (carried, base_b, query, weight, sums_a, gated_b, sums_b),
+            shape(gated_b.shape, bf16),
+            shape(sums_b.shape, bf16),
+            aliases={5: 0, 6: 1},
         )
     else:
         halos = [{reach_max - back: shift(own, back, False) for back in range(1, reach_max + 1)} for own in products]
-        sums, gated_a = part(0, halos[0], base(0, {reach_max: own_a}), (), f32)
-        sums, gated_b = part(RELAYED, halos[1], base(RELAYED, {reach_max: own_b}), (sums,), bf16)
+        base_a, base_b = base(0, {reach_max: own_a}), base(RELAYED, {reach_max: own_b})
+        gated_a, gated_b, sums_b = first_block(base_a, base_b)
+        gated_a, sums_a = part(0, halos[0], base_a, (), gated_a)
+        gated_b, sums = part(RELAYED, halos[1], base_b, (sums_a,), gated_b, sums_b)
     received = lax.ppermute(sums, "chan", [(0, 1), (1, 0)])
     (own,) = kernel(own_kernel, (gated_a, gated_b, weight), shape((block, cols), f32))
     return (own + received.astype(f32)).astype(bf16)

time: 24.3 us -> 24 us (0.988)
  Pallas kernels: 9.04 us -> 8.64 us
  waiting for transfers between devices: 2.81 us -> 3.11 us
    pallas_call x7 -> x8, Pallas kernels: 5.03 us -> 4.63 us  [kernel(): pl.pallas_call(call, in_specs=[vmem] * len(ins), out_specs=[vmem] * len(o...]
    ppermute x2, waiting for transfers between devices: 2.37 us -> 2.67 us  [shift(): lax.ppermute(array, 'seq', [(i, (i + back) % count) for i in range(count...]
  transfers between devices with their start and end apart: 5 -> 5, of which waited for: 3 -> 3; matrix products, arithmetic and copies ran while one was open for 0% -> 0% of each run, Pallas kernels for 36% -> 34%
where the time goes in v8:
time: 24 us; the launch traced here: 23.8 us
  starting transfers between devices  9.9 us (41%)
  Pallas kernels  8.64 us (36%)
  waiting for transfers between devices  3.11 us (13%)
  other arithmetic  2.08 us (9%)
    pallas_call x8, Pallas kernels, kernel(): pl.pallas_call(call, in_specs=[vmem] * len(ins), out_specs=[vmem] * len(o...  4.63 us
    ppermute x2, starting transfers between devices, shift(): lax.ppermute(array, 'seq', [(i, (i + back) % count) for i in range(count...  4.56 us
    pallas_call x1, Pallas kernels, body(): pl.pallas_call(lambda *refs: setup_kernel(block * seq_count, block, 1.0 /...  4.01 us
    ppermute x1, starting transfers between devices, body(): received = lax.ppermute(sums, 'chan', [(0, 1), (1, 0)])  2.8 us
    ppermute x2, waiting for transfers between devices, shift(): lax.ppermute(array, 'seq', [(i, (i + back) % count) for i in range(count...  2.67 us
    ppermute x2, starting transfers between devices, swap_pairs(): lax.ppermute(array, 'seq', [(i, i ^ 1) for i in range(lax.axis_size('seq'...  2.54 us
    convert_element_type x1, other arithmetic, body(): (key_feat[low:high].astype(f32) * value_feat[low:high].astype(f32)).astyp...  1.32 us
    convert_element_type x1, other arithmetic, body(): return (own + received.astype(f32)).astype(bf16)  0.76 us
  transfers between devices with their start and end apart: 5, of which 3 were waited for; matrix products, arithmetic and copies ran while one was open for 0% of the time, Pallas kernels for 34%

profile of v8, /device:TPU:9, one launch (start us, length us, event | category | flops | bytes accessed | tf_op | source)
XLA Modules:
  0.0 23.8 jit_solution(8025738742767228531)
XLA Ops:
  0.0 1.3 %multiply_convert_fusion = (bf16[1024,128]{1,0:T(8,128)(2,1)S(1)}, bf16[1024,128]{1,0:T(8,128)(2,1)S(1)}) fusion(bf16[2048,128]{1,0:T(8,128)(2,1)} %param.14, bf16[2048,128]{1,0:T(8,128)(2,1)} %param.13), kind=kLoop, calls=%fused_computation.1 | loop fusion | flops 1048576 | bytes 1572864 | tf_op jit(solution)/shard_map/convert_element_type | solution.py:264
  1.3 1.3 %collective-permute-start = (bf16[1024,128]{1,0:T(8,128)(2,1)S(1)}, bf16[1024,128]{1,0:T(8,128)(2,1)S(1)}, u32[]{:S(2)}, u32[]{:S(2)}) collective-permute-start(bf16[1024,128]{1,0:T(8,128)(2,1)S(1)} %get-tuple-element.19.own.refs_1_), channel_id=1, source_target_pairs={{0,4},{2,6},{4,8},{6,10},{8,12},{10,14},{12,0},{14,2},{1,5},{3,7},... | collective-permute-start | bytes 786440 | tf_op jit(solution)/shard_map/ppermute | solution.py:226
  2.7 1.2 %collective-permute-start.2 = (bf16[1024,128]{1,0:T(8,128)(2,1)S(1)}, bf16[1024,128]{1,0:T(8,128)(2,1)S(1)}, u32[]{:S(2)}, u32[]{:S(2)}) collective-permute-start(bf16[1024,128]{1,0:T(8,128)(2,1)S(1)} %get-tuple-element.31.refs_1_.own), channel_id=1, source_target_pairs={{0,2},{2,0},{4,6},{6,4},{8,10},{10,8},{12,14},{14,12},{1,3},{3,1},... | collective-permute-start | bytes 786440 | tf_op jit(solution)/shard_map/ppermute | solution.py:230
  3.9 4.0 %shard_map.118 = (f32[128,512]{1,0:T(8,128)S(1)}, bf16[896,512]{1,0:T(8,128)(2,1)S(1)}, bf16[2048,128]{1,0:T(8,128)(2,1)S(1)}, f32[16,128]{1,0:T(8,128)S(1)}, bf16[2048,2048]{1,0:T(8,128)(2,1)S(1)}) custom-call(s32[1,16]{1,0:T(1,128)} %bitcast.6, f32[32,64]{1,0:T(8,128)} %refs_1_.1, f32[1,64]{1,0:T(1,128)} %bitcast.7, f32[64,128]{1,0:T(8,128)} %refs_3_.1, ...), custom_call_target="tpu_custom_call" | custom-call | flops 1 | bytes 30000000 | tf_op jit(solution)/shard_map/pallas_call | solution.py:285
  7.9 0.6 %collective-permute-done.far.refs_0_ = bf16[1024,128]{1,0:T(8,128)(2,1)S(1)} collective-permute-done((bf16[1024,128]{1,0:T(8,128)(2,1)S(1)}, bf16[1024,128]{1,0:T(8,128)(2,1)S(1)}, u32[]{:S(2)}, u32[]{:S(2)}) %collective-permute-start) | collective-permute-done | bytes 262176 | tf_op jit(solution)/shard_map/ppermute | solution.py:226
  8.6 0.1 shard_map.119
  8.6 1.3 %collective-permute-start.1 = (bf16[1024,128]{1,0:T(8,128)(2,1)S(1)}, bf16[1024,128]{1,0:T(8,128)(2,1)S(1)}, u32[]{:S(2)}, u32[]{:S(2)}) collective-permute-start(bf16[1024,128]{1,0:T(8,128)(2,1)S(1)} %shard_map.119), channel_id=1, source_target_pairs={{0,2},{2,0},{4,6},{6,4},{8,10},{10,8},{12,14},{14,12},{1,3},{3,1},... | collective-permute-start | bytes 786440 | tf_op jit(solution)/shard_map/ppermute | solution.py:230
  9.9 0.0 collective-permute-done.2.refs_0_.other
  9.9 0.7 %shard_map.124 = bf16[1024,128]{1,0:T(8,128)(2,1)S(1)} custom-call(bf16[1024,128]{1,0:T(8,128)(2,1)S(1)} %get-tuple-element.31.refs_1_.own, bf16[1024,128]{1,0:T(8,128)(2,1)S(1)} %collective-permute-done.2.refs_0_.other, f32[128,512]{1,0:T(8,128)S(1)} %get-tuple-element.18.refs_3_.spectrum, bf16[896,512]{1,0:T(8,128)(2,1)S(1)} %get-tuple-element.21.refs_4_.table), custom_call_target="tpu_custom_call" | custom-call | flops 1 | bytes 1 | tf_op jit(solution)/shard_map/pallas_call | solution.py:297
  10.7 3.2 %collective-permute-start.3 = (bf16[1024,128]{1,0:T(8,128)(2,1)S(1)}, bf16[1024,128]{1,0:T(8,128)(2,1)S(1)}, u32[]{:S(2)}, u32[]{:S(2)}) collective-permute-start(bf16[1024,128]{1,0:T(8,128)(2,1)S(1)} %shard_map.124), channel_id=1, source_target_pairs={{0,4},{2,6},{4,8},{6,10},{8,12},{10,14},{1,5},{3,7},{5,9},{7,11},{... | collective-permute-start | bytes 786440 | tf_op jit(solution)/shard_map/ppermute | solution.py:226
  13.9 0.7 %shard_map.120.base_a.refs_1_ = f32[1024,128]{1,0:T(8,128)S(1)} custom-call(bf16[1024,128]{1,0:T(8,128)(2,1)S(1)} %collective-permute-done.far.refs_0_, bf16[1024,128]{1,0:T(8,128)(2,1)S(1)} %get-tuple-element.19.own.refs_1_, f32[16,128]{1,0:T(8,128)S(1)} %get-tuple-element.20.refs_2_, f32[128,512]{1,0:T(8,128)S(1)} %get-tuple-element.18.refs_3_.spectrum, ...), custom_call_target="tpu_custom_call" | custom-call | flops 1 | bytes 1 | tf_op jit(solution)/shard_map/pallas_call | solution.py:297
  14.6 0.7 %shard_map.121.base_b.base = f32[1024,128]{1,0:T(8,128)S(1)} custom-call(bf16[1024,128]{1,0:T(8,128)(2,1)S(1)} %collective-permute-done.2.refs_0_.other, bf16[1024,128]{1,0:T(8,128)(2,1)S(1)} %get-tuple-element.31.refs_1_.own, f32[16,128]{1,0:T(8,128)S(1)} %get-tuple-element.20.refs_2_, f32[128,512]{1,0:T(8,128)S(1)} %get-tuple-element.18.refs_3_.spectrum, ...), custom_call_target="tpu_custom_call" | custom-call | flops 1 | bytes 1 | tf_op jit(solution)/shard_map/pallas_call | solution.py:297
  15.4 0.0 collective-permute-done.1.refs_0_
  15.4 1.2 %shard_map.123 = (bf16[128,1024]{1,0:T(8,128)(2,1)S(1)}, f32[128,1024]{1,0:T(8,128)S(1)}) custom-call(bf16[1024,128]{1,0:T(8,128)(2,1)S(1)} %collective-permute-done.1.refs_0_, f32[1024,128]{1,0:T(8,128)S(1)} %shard_map.120.base_a.refs_1_, bf16[2048,128]{1,0:T(8,128)(2,1)S(1)} %get-tuple-element.22.query.refs_2_, ...), custom_call_target="tpu_custom_call", output_to_operand_aliasing={{0}: (6, {})} | custom-call | flops 1 | bytes 1 | tf_op jit(solution)/shard_map/pallas_call | solution.py:297
  16.5 2.0 %collective-permute-done.3.carried = bf16[1024,128]{1,0:T(8,128)(2,1)S(1)} collective-permute-done((bf16[1024,128]{1,0:T(8,128)(2,1)S(1)}, bf16[1024,128]{1,0:T(8,128)(2,1)S(1)}, u32[]{:S(2)}, u32[]{:S(2)}) %collective-permute-start.3) | collective-permute-done | bytes 262176 | tf_op jit(solution)/shard_map/ppermute | solution.py:226
  18.6 0.5 %shard_map.125 = (bf16[128,1024]{1,0:T(8,128)(2,1)S(1)}, bf16[128,1024]{1,0:T(8,128)(2,1)S(1)}) custom-call(bf16[1024,128]{1,0:T(8,128)(2,1)S(1)} %collective-permute-done.3.carried, f32[1024,128]{1,0:T(8,128)S(1)} %shard_map.121.base_b.base, bf16[2048,128]{1,0:T(8,128)(2,1)S(1)} %get-tuple-element.22.query.refs_2_, ...), custom_call_target="tpu_custom_call", output_to_operand_aliasing={{0}: (5, {}), {1}: (6, {})} | custom-call | flops 1 | bytes 1 | tf_op jit(solution)/shard_map/pallas_call | solution.py:297
  19.1 2.8 %collective-permute-start.4 = (bf16[128,1024]{1,0:T(8,128)(2,1)S(1)}, bf16[128,1024]{1,0:T(8,128)(2,1)S(1)}, u32[]{:S(2)}, u32[]{:S(2)}) collective-permute-start(bf16[128,1024]{1,0:T(8,128)(2,1)S(1)} %get-tuple-element.30), channel_id=1, source_target_pairs={{0,1},{1,0},{2,3},{3,2},{4,5},{5,4},{6,7},{7,6},{8,9},{9,8},{10,11... | collective-permute-start | bytes 786440 | tf_op jit(solution)/shard_map/ppermute | solution.py:354
  21.9 0.7 %shard_map.126 = f32[128,1024]{1,0:T(8,128)S(1)} custom-call(bf16[128,1024]{1,0:T(8,128)(2,1)S(1)} %get-tuple-element.25.gated_a, bf16[128,1024]{1,0:T(8,128)(2,1)S(1)} %get-tuple-element.29.gated_b, bf16[2048,2048]{1,0:T(8,128)(2,1)S(1)} %get-tuple-element.23.weight.refs_5_), custom_call_target="tpu_custom_call" | custom-call | flops 1 | bytes 1 | tf_op jit(solution)/shard_map/pallas_call | solution.py:297
  22.6 0.4 %collective-permute-done.4 = bf16[128,1024]{1,0:T(8,128)(2,1)S(1)} collective-permute-done((bf16[128,1024]{1,0:T(8,128)(2,1)S(1)}, bf16[128,1024]{1,0:T(8,128)(2,1)S(1)}, u32[]{:S(2)}, u32[]{:S(2)}) %collective-permute-start.4) | collective-permute-done | bytes 262176 | tf_op jit(solution)/shard_map/ppermute | solution.py:354
  23.1 0.8 %add_convert_fusion = bf16[128,1024]{1,0:T(8,128)(2,1)} fusion(f32[128,1024]{1,0:T(8,128)S(1)} %shard_map.126, bf16[128,1024]{1,0:T(8,128)(2,1)S(1)} %collective-permute-done.4), kind=kLoop, calls=%fused_computation | loop fusion | flops 393216 | bytes 1048576 | tf_op jit(solution)/shard_map/convert_element_type | solution.py:356
  (1 shorter events, 0.0 us)
Async XLA Ops:
  1.3 7.2 %collective-permute-start = (bf16[1024,128]{1,0:T(8,128)(2,1)S(1)}, bf16[1024,128]{1,0:T(8,128)(2,1)S(1)}, u32[]{:S(2)}, u32[]{:S(2)}) collective-permute-start(bf16[1024,128]{1,0:T(8,128)(2,1)S(1)} %get-tuple-element.19.own.refs_1_), channel_id=1, source_target_pairs={{0,4},{2,6},{4,8},{6,10},{8,12},{10,14},{12,0},{14,2},{1,5},{3,7},... | collective-permute-start | bytes 786440 | tf_op jit(solution)/shard_map/ppermute | solution.py:226
  2.7 7.3 %collective-permute-start.2 = (bf16[1024,128]{1,0:T(8,128)(2,1)S(1)}, bf16[1024,128]{1,0:T(8,128)(2,1)S(1)}, u32[]{:S(2)}, u32[]{:S(2)}) collective-permute-start(bf16[1024,128]{1,0:T(8,128)(2,1)S(1)} %get-tuple-element.31.refs_1_.own), channel_id=1, source_target_pairs={{0,2},{2,0},{4,6},{6,4},{8,10},{10,8},{12,14},{14,12},{1,3},{3,1},... | collective-permute-start | bytes 786440 | tf_op jit(solution)/shard_map/ppermute | solution.py:230
  8.6 6.7 %collective-permute-start.1 = (bf16[1024,128]{1,0:T(8,128)(2,1)S(1)}, bf16[1024,128]{1,0:T(8,128)(2,1)S(1)}, u32[]{:S(2)}, u32[]{:S(2)}) collective-permute-start(bf16[1024,128]{1,0:T(8,128)(2,1)S(1)} %shard_map.119), channel_id=1, source_target_pairs={{0,2},{2,0},{4,6},{6,4},{8,10},{10,8},{12,14},{14,12},{1,3},{3,1},... | collective-permute-start | bytes 786440 | tf_op jit(solution)/shard_map/ppermute | solution.py:230
  10.7 7.9 %collective-permute-start.3 = (bf16[1024,128]{1,0:T(8,128)(2,1)S(1)}, bf16[1024,128]{1,0:T(8,128)(2,1)S(1)}, u32[]{:S(2)}, u32[]{:S(2)}) collective-permute-start(bf16[1024,128]{1,0:T(8,128)(2,1)S(1)} %shard_map.124), channel_id=1, source_target_pairs={{0,4},{2,6},{4,8},{6,10},{8,12},{10,14},{1,5},{3,7},{5,9},{7,11},{... | collective-permute-start | bytes 786440 | tf_op jit(solution)/shard_map/ppermute | solution.py:226
  19.1 4.0 %collective-permute-start.4 = (bf16[128,1024]{1,0:T(8,128)(2,1)S(1)}, bf16[128,1024]{1,0:T(8,128)(2,1)S(1)}, u32[]{:S(2)}, u32[]{:S(2)}) collective-permute-start(bf16[128,1024]{1,0:T(8,128)(2,1)S(1)} %get-tuple-element.30), channel_id=1, source_target_pairs={{0,1},{1,0},{2,3},{3,2},{4,5},{5,4},{6,7},{7,6},{8,9},{9,8},{10,11... | collective-permute-start | bytes 786440 | tf_op jit(solution)/shard_map/ppermute | solution.py:354

commit v9 on v8

--- a/solution.py
+++ b/solution.py
@@ -211,10 +211,11 @@
         part[...] = total.astype(part.dtype)
 
 
-def own_kernel(gated_a, gated_b, weight, out):
+def own_kernel(first, gated_t, weight, *refs):
     here = column_halves(weight)[0]
-    gated_t = jnp.concatenate([gated_a[...], gated_b[...]], axis=1)
-    out[...] = jnp.dot(gated_t, weight[:, here], preferred_element_type=jnp.float32)
+    rows = slice(first, first + gated_t.shape[1])
+    total = jnp.dot(gated_t[...], weight[rows, here], preferred_element_type=jnp.float32)
+    refs[-1][...] = total if len(refs) == 1 else refs[0][...] + total
 
 
 def cost(bytes_accessed):
@@ -338,6 +339,8 @@
         base_b = base(RELAYED, {1: other, 2: own_b}, True)
         gated_a, gated_b, sums_b = first_block(base_a, base_b)
         gated_a, sums_a = part(0, {1: near}, base_a, (), gated_a)
+        (own,) = kernel(functools.partial(own_kernel, 0), (gated_a, weight), shape((block, cols), f32))
+        sums_a, own = lax.optimization_barrier((sums_a, own))
         gated_b, sums = kernel(
             functools.partial(last_kernel, RELAYED),
             (carried, base_b, query, weight, sums_a, gated_b, sums_b),
@@ -350,9 +353,10 @@
         base_a, base_b = base(0, {reach_max: own_a}), base(RELAYED, {reach_max: own_b})
         gated_a, gated_b, sums_b = first_block(base_a, base_b)
         gated_a, sums_a = part(0, halos[0], base_a, (), gated_a)
+        (own,) = kernel(functools.partial(own_kernel, 0), (gated_a, weight), shape((block, cols), f32))
         gated_b, sums = part(RELAYED, halos[1], base_b, (sums_a,), gated_b, sums_b)
     received = lax.ppermute(sums, "chan", [(0, 1), (1, 0)])
-    (own,) = kernel(own_kernel, (gated_a, gated_b, weight), shape((block, cols), f32))
+    (own,) = kernel(functools.partial(own_kernel, RELAYED), (gated_b, weight, own), shape((block, cols), f32))
     return (own + received.astype(f32)).astype(bf16)
 
 

time: 24 us -> 24 us (level)
    ppermute x2, waiting for transfers between devices: 2.67 us -> 2.22 us  [shift(): lax.ppermute(array, 'seq', [(i, (i + back) % count) for i in range(count...]
    ppermute x1, waiting for transfers between devices: 0.44 us -> 0.7 us  [body(): received = lax.ppermute(sums, 'chan', [(0, 1), (1, 0)])]
    pallas_call x8 -> x9, Pallas kernels: 4.63 us -> 4.82 us  [kernel(): pl.pallas_call(call, in_specs=[vmem] * len(ins), out_specs=[vmem] * len(o...]
  transfers between devices with their start and end apart: 5 -> 5, of which waited for: 3 -> 3; matrix products, arithmetic and copies ran while one was open for 0% -> 0% of each run, Pallas kernels for 34% -> 35%
where the time goes in v9:
time: 24 us; the launch traced here: 23.8 us
  starting transfers between devices  9.88 us (41%)
  Pallas kernels  8.83 us (37%)
  waiting for transfers between devices  2.93 us (12%)
  other arithmetic  2.08 us (9%)
    pallas_call x9, Pallas kernels, kernel(): pl.pallas_call(call, in_specs=[vmem] * len(ins), out_specs=[vmem] * len(o...  4.82 us
    ppermute x2, starting transfers between devices, shift(): lax.ppermute(array, 'seq', [(i, (i + back) % count) for i in range(count...  4.55 us
    pallas_call x1, Pallas kernels, body(): pl.pallas_call(lambda *refs: setup_kernel(block * seq_count, block, 1.0 /...  4.01 us
    ppermute x1, starting transfers between devices, body(): received = lax.ppermute(sums, 'chan', [(0, 1), (1, 0)])  2.78 us
    ppermute x2, starting transfers between devices, swap_pairs(): lax.ppermute(array, 'seq', [(i, i ^ 1) for i in range(lax.axis_size('seq'...  2.54 us
    ppermute x2, waiting for transfers between devices, shift(): lax.ppermute(array, 'seq', [(i, (i + back) % count) for i in range(count...  2.22 us
    convert_element_type x1, other arithmetic, body(): (key_feat[low:high].astype(f32) * value_feat[low:high].astype(f32)).astyp...  1.32 us
    convert_element_type x1, other arithmetic, body(): return (own + received.astype(f32)).astype(bf16)  0.76 us
  transfers between devices with their start and end apart: 5, of which 3 were waited for; matrix products, arithmetic and copies ran while one was open for 0% of the time, Pallas kernels for 35%

profile of v9, /device:TPU:9, one launch (start us, length us, event | category | flops | bytes accessed | tf_op | source)
XLA Modules:
  0.0 23.8 jit_solution(254581988053315384)
XLA Ops:
  0.0 1.3 %multiply_convert_fusion = (bf16[1024,128]{1,0:T(8,128)(2,1)S(1)}, bf16[1024,128]{1,0:T(8,128)(2,1)S(1)}) fusion(bf16[2048,128]{1,0:T(8,128)(2,1)} %param.14, bf16[2048,128]{1,0:T(8,128)(2,1)} %param.13), kind=kLoop, calls=%fused_computation.1 | loop fusion | flops 1048576 | bytes 1572864 | tf_op jit(solution)/shard_map/convert_element_type | solution.py:265
  1.3 1.3 %collective-permute-start.2 = (bf16[1024,128]{1,0:T(8,128)(2,1)S(1)}, bf16[1024,128]{1,0:T(8,128)(2,1)S(1)}, u32[]{:S(2)}, u32[]{:S(2)}) collective-permute-start(bf16[1024,128]{1,0:T(8,128)(2,1)S(1)} %get-tuple-element.25.own.refs_1_), channel_id=1, source_target_pairs={{0,4},{2,6},{4,8},{6,10},{8,12},{10,14},{12,0},{14,2},{1,5},{3,7},... | collective-permute-start | bytes 786440 | tf_op jit(solution)/shard_map/ppermute | solution.py:227
  2.7 1.2 %collective-permute-start = (bf16[1024,128]{1,0:T(8,128)(2,1)S(1)}, bf16[1024,128]{1,0:T(8,128)(2,1)S(1)}, u32[]{:S(2)}, u32[]{:S(2)}) collective-permute-start(bf16[1024,128]{1,0:T(8,128)(2,1)S(1)} %get-tuple-element.36.own.refs_1_), channel_id=1, source_target_pairs={{0,2},{2,0},{4,6},{6,4},{8,10},{10,8},{12,14},{14,12},{1,3},{3,1},... | collective-permute-start | bytes 786440 | tf_op jit(solution)/shard_map/ppermute | solution.py:231
  3.9 4.0 %shard_map.118 = (f32[128,512]{1,0:T(8,128)S(1)}, bf16[896,512]{1,0:T(8,128)(2,1)S(1)}, bf16[2048,128]{1,0:T(8,128)(2,1)S(1)}, f32[16,128]{1,0:T(8,128)S(1)}, bf16[2048,2048]{1,0:T(8,128)(2,1)S(1)}) custom-call(s32[1,16]{1,0:T(1,128)} %bitcast.6, f32[32,64]{1,0:T(8,128)} %refs_1_.1, f32[1,64]{1,0:T(1,128)} %bitcast.7, f32[64,128]{1,0:T(8,128)} %refs_3_.1, ...), custom_call_target="tpu_custom_call" | custom-call | flops 1 | bytes 30000000 | tf_op jit(solution)/shard_map/pallas_call | solution.py:286
  7.9 0.6 %collective-permute-done.2.far.refs_0_ = bf16[1024,128]{1,0:T(8,128)(2,1)S(1)} collective-permute-done((bf16[1024,128]{1,0:T(8,128)(2,1)S(1)}, bf16[1024,128]{1,0:T(8,128)(2,1)S(1)}, u32[]{:S(2)}, u32[]{:S(2)}) %collective-permute-start.2) | collective-permute-done | bytes 262176 | tf_op jit(solution)/shard_map/ppermute | solution.py:227
  8.6 0.1 shard_map.121
  8.6 1.3 %collective-permute-start.3 = (bf16[1024,128]{1,0:T(8,128)(2,1)S(1)}, bf16[1024,128]{1,0:T(8,128)(2,1)S(1)}, u32[]{:S(2)}, u32[]{:S(2)}) collective-permute-start(bf16[1024,128]{1,0:T(8,128)(2,1)S(1)} %shard_map.121), channel_id=1, source_target_pairs={{0,2},{2,0},{4,6},{6,4},{8,10},{10,8},{12,14},{14,12},{1,3},{3,1},... | collective-permute-start | bytes 786440 | tf_op jit(solution)/shard_map/ppermute | solution.py:231
  9.9 0.0 collective-permute-done.other.refs_0_
  9.9 0.7 %shard_map.119 = bf16[1024,128]{1,0:T(8,128)(2,1)S(1)} custom-call(bf16[1024,128]{1,0:T(8,128)(2,1)S(1)} %get-tuple-element.36.own.refs_1_, bf16[1024,128]{1,0:T(8,128)(2,1)S(1)} %collective-permute-done.other.refs_0_, f32[128,512]{1,0:T(8,128)S(1)} %get-tuple-element.20.spectrum.refs_3_, bf16[896,512]{1,0:T(8,128)(2,1)S(1)} %get-tuple-element.21.table.refs_4_), custom_call_target="tpu_custom_call" | custom-call | flops 1 | bytes 1 | tf_op jit(solution)/shard_map/pallas_call | solution.py:298
  10.7 3.2 %collective-permute-start.1 = (bf16[1024,128]{1,0:T(8,128)(2,1)S(1)}, bf16[1024,128]{1,0:T(8,128)(2,1)S(1)}, u32[]{:S(2)}, u32[]{:S(2)}) collective-permute-start(bf16[1024,128]{1,0:T(8,128)(2,1)S(1)} %shard_map.119), channel_id=1, source_target_pairs={{0,4},{2,6},{4,8},{6,10},{8,12},{10,14},{1,5},{3,7},{5,9},{7,11},{... | collective-permute-start | bytes 786440 | tf_op jit(solution)/shard_map/ppermute | solution.py:227
  13.9 0.7 %shard_map.122.base_a.refs_1_ = f32[1024,128]{1,0:T(8,128)S(1)} custom-call(bf16[1024,128]{1,0:T(8,128)(2,1)S(1)} %collective-permute-done.2.far.refs_0_, bf16[1024,128]{1,0:T(8,128)(2,1)S(1)} %get-tuple-element.25.own.refs_1_, f32[16,128]{1,0:T(8,128)S(1)} %get-tuple-element.22.refs_2_, f32[128,512]{1,0:T(8,128)S(1)} %get-tuple-element.20.spectrum.refs_3_, ...), custom_call_target="tpu_custom_call" | custom-call | flops 1 | bytes 1 | tf_op jit(solution)/shard_map/pallas_call | solution.py:298
  14.6 0.7 %shard_map.120.base_b.base = f32[1024,128]{1,0:T(8,128)S(1)} custom-call(bf16[1024,128]{1,0:T(8,128)(2,1)S(1)} %collective-permute-done.other.refs_0_, bf16[1024,128]{1,0:T(8,128)(2,1)S(1)} %get-tuple-element.36.own.refs_1_, f32[16,128]{1,0:T(8,128)S(1)} %get-tuple-element.22.refs_2_, f32[128,512]{1,0:T(8,128)S(1)} %get-tuple-element.20.spectrum.refs_3_, ...), custom_call_target="tpu_custom_call" | custom-call | flops 1 | bytes 1 | tf_op jit(solution)/shard_map/pallas_call | solution.py:298
  15.3 0.0 collective-permute-done.3.refs_0_
  15.4 1.2 %shard_map.124 = (bf16[128,1024]{1,0:T(8,128)(2,1)S(1)}, f32[128,1024]{1,0:T(8,128)S(1)}) custom-call(bf16[1024,128]{1,0:T(8,128)(2,1)S(1)} %collective-permute-done.3.refs_0_, f32[1024,128]{1,0:T(8,128)S(1)} %shard_map.122.base_a.refs_1_, bf16[2048,128]{1,0:T(8,128)(2,1)S(1)} %get-tuple-element.23.query.refs_2_, ...), custom_call_target="tpu_custom_call", output_to_operand_aliasing={{0}: (6, {})} | custom-call | flops 1 | bytes 1 | tf_op jit(solution)/shard_map/pallas_call | solution.py:298
  16.5 0.5 %shard_map.125.refs_0_ = f32[128,1024]{1,0:T(8,128)S(1)} custom-call(bf16[128,1024]{1,0:T(8,128)(2,1)S(1)} %get-tuple-element.28.gated_t, bf16[2048,2048]{1,0:T(8,128)(2,1)S(1)} %get-tuple-element.24.weight.refs_5_), custom_call_target="tpu_custom_call" | custom-call | flops 1 | bytes 1 | tf_op jit(solution)/shard_map/pallas_call | solution.py:298
  17.0 1.6 %collective-permute-done.1.carried = bf16[1024,128]{1,0:T(8,128)(2,1)S(1)} collective-permute-done((bf16[1024,128]{1,0:T(8,128)(2,1)S(1)}, bf16[1024,128]{1,0:T(8,128)(2,1)S(1)}, u32[]{:S(2)}, u32[]{:S(2)}) %collective-permute-start.1) | collective-permute-done | bytes 262176 | tf_op jit(solution)/shard_map/ppermute | solution.py:227
  18.6 0.5 %shard_map.126 = (bf16[128,1024]{1,0:T(8,128)(2,1)S(1)}, bf16[128,1024]{1,0:T(8,128)(2,1)S(1)}) custom-call(bf16[1024,128]{1,0:T(8,128)(2,1)S(1)} %collective-permute-done.1.carried, f32[1024,128]{1,0:T(8,128)S(1)} %shard_map.120.base_b.base, bf16[2048,128]{1,0:T(8,128)(2,1)S(1)} %get-tuple-element.23.query.refs_2_, ...), custom_call_target="tpu_custom_call", output_to_operand_aliasing={{0}: (5, {}), {1}: (6, {})} | custom-call | flops 1 | bytes 1 | tf_op jit(solution)/shard_map/pallas_call | solution.py:298
  19.1 2.8 %collective-permute-start.4 = (bf16[128,1024]{1,0:T(8,128)(2,1)S(1)}, bf16[128,1024]{1,0:T(8,128)(2,1)S(1)}, u32[]{:S(2)}, u32[]{:S(2)}) collective-permute-start(bf16[128,1024]{1,0:T(8,128)(2,1)S(1)} %get-tuple-element.34), channel_id=1, source_target_pairs={{0,1},{1,0},{2,3},{3,2},{4,5},{5,4},{6,7},{7,6},{8,9},{9,8},{10,11... | collective-permute-start | bytes 786440 | tf_op jit(solution)/shard_map/ppermute | solution.py:358
  21.9 0.5 %shard_map.127 = f32[128,1024]{1,0:T(8,128)S(1)} custom-call(bf16[128,1024]{1,0:T(8,128)(2,1)S(1)} %get-tuple-element.32.gated_t, bf16[2048,2048]{1,0:T(8,128)(2,1)S(1)} %get-tuple-element.24.weight.refs_5_, f32[128,1024]{1,0:T(8,128)S(1)} %shard_map.125.refs_0_), custom_call_target="tpu_custom_call" | custom-call | flops 1 | bytes 1 | tf_op jit(solution)/shard_map/pallas_call | solution.py:298
  22.4 0.7 %collective-permute-done.4 = bf16[128,1024]{1,0:T(8,128)(2,1)S(1)} collective-permute-done((bf16[128,1024]{1,0:T(8,128)(2,1)S(1)}, bf16[128,1024]{1,0:T(8,128)(2,1)S(1)}, u32[]{:S(2)}, u32[]{:S(2)}) %collective-permute-start.4) | collective-permute-done | bytes 262176 | tf_op jit(solution)/shard_map/ppermute | solution.py:358
  23.1 0.8 %add_convert_fusion = bf16[128,1024]{1,0:T(8,128)(2,1)} fusion(f32[128,1024]{1,0:T(8,128)S(1)} %shard_map.127, bf16[128,1024]{1,0:T(8,128)(2,1)S(1)} %collective-permute-done.4), kind=kLoop, calls=%fused_computation | loop fusion | flops 393216 | bytes 1048576 | tf_op jit(solution)/shard_map/convert_element_type | solution.py:360
  (1 shorter events, 0.0 us)
Async XLA Ops:
  1.3 7.2 %collective-permute-start.2 = (bf16[1024,128]{1,0:T(8,128)(2,1)S(1)}, bf16[1024,128]{1,0:T(8,128)(2,1)S(1)}, u32[]{:S(2)}, u32[]{:S(2)}) collective-permute-start(bf16[1024,128]{1,0:T(8,128)(2,1)S(1)} %get-tuple-element.25.own.refs_1_), channel_id=1, source_target_pairs={{0,4},{2,6},{4,8},{6,10},{8,12},{10,14},{12,0},{14,2},{1,5},{3,7},... | collective-permute-start | bytes 786440 | tf_op jit(solution)/shard_map/ppermute | solution.py:227
  2.7 7.3 %collective-permute-start = (bf16[1024,128]{1,0:T(8,128)(2,1)S(1)}, bf16[1024,128]{1,0:T(8,128)(2,1)S(1)}, u32[]{:S(2)}, u32[]{:S(2)}) collective-permute-start(bf16[1024,128]{1,0:T(8,128)(2,1)S(1)} %get-tuple-element.36.own.refs_1_), channel_id=1, source_target_pairs={{0,2},{2,0},{4,6},{6,4},{8,10},{10,8},{12,14},{14,12},{1,3},{3,1},... | collective-permute-start | bytes 786440 | tf_op jit(solution)/shard_map/ppermute | solution.py:231
  8.6 6.7 %collective-permute-start.3 = (bf16[1024,128]{1,0:T(8,128)(2,1)S(1)}, bf16[1024,128]{1,0:T(8,128)(2,1)S(1)}, u32[]{:S(2)}, u32[]{:S(2)}) collective-permute-start(bf16[1024,128]{1,0:T(8,128)(2,1)S(1)} %shard_map.121), channel_id=1, source_target_pairs={{0,2},{2,0},{4,6},{6,4},{8,10},{10,8},{12,14},{14,12},{1,3},{3,1},... | collective-permute-start | bytes 786440 | tf_op jit(solution)/shard_map/ppermute | solution.py:231
  10.7 7.9 %collective-permute-start.1 = (bf16[1024,128]{1,0:T(8,128)(2,1)S(1)}, bf16[1024,128]{1,0:T(8,128)(2,1)S(1)}, u32[]{:S(2)}, u32[]{:S(2)}) collective-permute-start(bf16[1024,128]{1,0:T(8,128)(2,1)S(1)} %shard_map.119), channel_id=1, source_target_pairs={{0,4},{2,6},{4,8},{6,10},{8,12},{10,14},{1,5},{3,7},{5,9},{7,11},{... | collective-permute-start | bytes 786440 | tf_op jit(solution)/shard_map/ppermute | solution.py:227
  19.1 3.9 %collective-permute-start.4 = (bf16[128,1024]{1,0:T(8,128)(2,1)S(1)}, bf16[128,1024]{1,0:T(8,128)(2,1)S(1)}, u32[]{:S(2)}, u32[]{:S(2)}) collective-permute-start(bf16[128,1024]{1,0:T(8,128)(2,1)S(1)} %get-tuple-element.34), channel_id=1, source_target_pairs={{0,1},{1,0},{2,3},{3,2},{4,5},{5,4},{6,7},{7,6},{8,9},{9,8},{10,11... | collective-permute-start | bytes 786440 | tf_op jit(solution)/shard_map/ppermute | solution.py:358

commit v10 on v8

--- a/solution.py
+++ b/solution.py
@@ -45,7 +45,7 @@
     for copy in copies[:7]:
         copy.wait()
     seed, f_in, bias, f_out, decay, reach = local
-    window = (table.shape[0] - block) // 2
+    window = table.shape[0] // 2
     lags = window - block
     lag = lax.broadcasted_iota(jnp.int32, (lags, 1), 0)
     if seq_len & (seq_len - 1) == 0:
@@ -85,7 +85,7 @@
     return None if back == 0 else lax.axis_index("seq") >= back
 
 
-def respond(freq, group, per_group, window, spectrum, table):
+def respond(freq, group, per_group, block, spectrum, table):
     half = table.shape[1] // 2
     mult = []
     for g in range(freq.shape[0] // per_group):
@@ -93,14 +93,12 @@
         hc, hs = spectrum[group + g : group + g + 1, :half], spectrum[group + g : group + g + 1, half:]
         xc, xs = part[:, :half], part[:, half:]
         mult.append(jnp.concatenate([xc * hc - xs * hs, xc * hs + xs * hc], axis=1).astype(jnp.bfloat16))
-    block = table.shape[0] - 2 * window
-    both = lax.dot_general(
+    return lax.dot_general(
         jnp.concatenate(mult, axis=0),
-        table[2 * window - block :],
+        table[table.shape[0] - block :],
         (((1,), (1,)), ((), ())),
         preferred_element_type=jnp.float32,
     )
-    return both[:, :block] + both[:, block:]
 
 
 def in_stages(channels, first, second):
@@ -117,7 +115,7 @@
     even = lax.axis_index("seq") % 2 == 0
 
     def give(start, tile, freq):
-        ahead = respond(freq, (first + start) // per_group, per_group, window, spectrum, table)
+        ahead = respond(freq, (first + start) // per_group, per_group, out.shape[1], spectrum, table)
         out[start : start + tile] = ahead.astype(out.dtype)
 
     in_stages(out.shape[0], functools.partial(transform, (0, 1), (own, other), (None, even), table), give)
@@ -135,7 +133,7 @@
     valid = [odd if odd_only else block_there(window, block, place) for place in places[:-1]] + [None]
 
     def give(start, tile, freq):
-        mixed = respond(freq, (first + start) // per_group, per_group, window, spectrum, table)
+        mixed = respond(freq, (first + start) // per_group, per_group, block, spectrum, table)
         for low in range(0, tile, 128):
             here = slice(start + low, start + low + 128)
             gain = gains(skip, (first + start + low) // 128, block)
@@ -199,7 +197,7 @@
     there = column_halves(weight)[1]
 
     def add(start, tile, freq):
-        mixed = respond(freq, (first + start) // per_group, per_group, window, spectrum, table)
+        mixed = respond(freq, (first + start) // per_group, per_group, block, spectrum, table)
         gate(first, query, gated_t, start, base[start : start + tile] + mixed)
 
     @pl.when(seq > 0)
@@ -251,7 +249,7 @@
     lags = reach_max * block
     window = lags + block
     (fwd_hi, fwd_lo), (inv_hi, inv_lo) = transform_tables(window, lags, block)
-    table = np.concatenate([fwd_hi, fwd_lo[:lags], inv_hi.T, inv_lo.T], axis=0)
+    table = np.concatenate([fwd_hi, fwd_lo[:lags], inv_hi.T], axis=0)
     length = table.shape[1]
     out_cols = out_weight.shape[1]
     cols = out_cols // 2

time: 24 us -> 24 us (level)
  no operation moved by 1% of the time
where the time goes in v10:
time: 24 us; the launch traced here: 23.8 us
  starting transfers between devices  9.89 us (41%)
  Pallas kernels  8.56 us (36%)
  waiting for transfers between devices  3.22 us (13%)
  other arithmetic  2.08 us (9%)
    pallas_call x8, Pallas kernels, kernel(): pl.pallas_call(call, in_specs=[vmem] * len(ins), out_specs=[vmem] * len(o...  4.59 us
    ppermute x2, starting transfers between devices, shift(): lax.ppermute(array, 'seq', [(i, (i + back) % count) for i in range(count...  4.56 us
    pallas_call x1, Pallas kernels, body(): pl.pallas_call(lambda *refs: setup_kernel(block * seq_count, block, 1.0 /...  3.97 us
    ppermute x1, starting transfers between devices, body(): received = lax.ppermute(sums, 'chan', [(0, 1), (1, 0)])  2.79 us
    ppermute x2, waiting for transfers between devices, shift(): lax.ppermute(array, 'seq', [(i, (i + back) % count) for i in range(count...  2.77 us
    ppermute x2, starting transfers between devices, swap_pairs(): lax.ppermute(array, 'seq', [(i, i ^ 1) for i in range(lax.axis_size('seq'...  2.54 us
    convert_element_type x1, other arithmetic, body(): (key_feat[low:high].astype(f32) * value_feat[low:high].astype(f32)).astyp...  1.32 us
    convert_element_type x1, other arithmetic, body(): return (own + received.astype(f32)).astype(bf16)  0.76 us
  transfers between devices with their start and end apart: 5, of which 3 were waited for; matrix products, arithmetic and copies ran while one was open for 0% of the time, Pallas kernels for 34%

profile of v10, /device:TPU:9, one launch (start us, length us, event | category | flops | bytes accessed | tf_op | source)
XLA Modules:
  0.0 23.8 jit_solution(16788291400800210547)
XLA Ops:
  0.0 1.3 %multiply_convert_fusion = (bf16[1024,128]{1,0:T(8,128)(2,1)S(1)}, bf16[1024,128]{1,0:T(8,128)(2,1)S(1)}) fusion(bf16[2048,128]{1,0:T(8,128)(2,1)} %param.14, bf16[2048,128]{1,0:T(8,128)(2,1)} %param.13), kind=kLoop, calls=%fused_computation.1 | loop fusion | flops 1048576 | bytes 1572864 | tf_op jit(solution)/shard_map/convert_element_type | solution.py:262
  1.3 1.3 %collective-permute-start = (bf16[1024,128]{1,0:T(8,128)(2,1)S(1)}, bf16[1024,128]{1,0:T(8,128)(2,1)S(1)}, u32[]{:S(2)}, u32[]{:S(2)}) collective-permute-start(bf16[1024,128]{1,0:T(8,128)(2,1)S(1)} %get-tuple-element.19.own.refs_1_), channel_id=1, source_target_pairs={{0,4},{2,6},{4,8},{6,10},{8,12},{10,14},{12,0},{14,2},{1,5},{3,7},... | collective-permute-start | bytes 786440 | tf_op jit(solution)/shard_map/ppermute | solution.py:224
  2.7 1.2 %collective-permute-start.2 = (bf16[1024,128]{1,0:T(8,128)(2,1)S(1)}, bf16[1024,128]{1,0:T(8,128)(2,1)S(1)}, u32[]{:S(2)}, u32[]{:S(2)}) collective-permute-start(bf16[1024,128]{1,0:T(8,128)(2,1)S(1)} %get-tuple-element.31.refs_1_.own), channel_id=1, source_target_pairs={{0,2},{2,0},{4,6},{6,4},{8,10},{10,8},{12,14},{14,12},{1,3},{3,1},... | collective-permute-start | bytes 786440 | tf_op jit(solution)/shard_map/ppermute | solution.py:228
  3.9 4.0 %shard_map.118 = (f32[128,512]{1,0:T(8,128)S(1)}, bf16[768,512]{1,0:T(8,128)(2,1)S(1)}, bf16[2048,128]{1,0:T(8,128)(2,1)S(1)}, f32[16,128]{1,0:T(8,128)S(1)}, bf16[2048,2048]{1,0:T(8,128)(2,1)S(1)}) custom-call(s32[1,16]{1,0:T(1,128)} %bitcast.6, f32[32,64]{1,0:T(8,128)} %refs_1_.1, f32[1,64]{1,0:T(1,128)} %bitcast.7, f32[64,128]{1,0:T(8,128)} %refs_3_.1, ...), custom_call_target="tpu_custom_call" | custom-call | flops 1 | bytes 30000000 | tf_op jit(solution)/shard_map/pallas_call | solution.py:283
  7.9 0.7 %collective-permute-done.far.refs_0_ = bf16[1024,128]{1,0:T(8,128)(2,1)S(1)} collective-permute-done((bf16[1024,128]{1,0:T(8,128)(2,1)S(1)}, bf16[1024,128]{1,0:T(8,128)(2,1)S(1)}, u32[]{:S(2)}, u32[]{:S(2)}) %collective-permute-start) | collective-permute-done | bytes 262176 | tf_op jit(solution)/shard_map/ppermute | solution.py:224
  8.6 0.1 shard_map.119
  8.6 1.3 %collective-permute-start.1 = (bf16[1024,128]{1,0:T(8,128)(2,1)S(1)}, bf16[1024,128]{1,0:T(8,128)(2,1)S(1)}, u32[]{:S(2)}, u32[]{:S(2)}) collective-permute-start(bf16[1024,128]{1,0:T(8,128)(2,1)S(1)} %shard_map.119), channel_id=1, source_target_pairs={{0,2},{2,0},{4,6},{6,4},{8,10},{10,8},{12,14},{14,12},{1,3},{3,1},... | collective-permute-start | bytes 786440 | tf_op jit(solution)/shard_map/ppermute | solution.py:228
  9.9 0.0 collective-permute-done.2.refs_0_.other
  9.9 0.7 %shard_map.124 = bf16[1024,128]{1,0:T(8,128)(2,1)S(1)} custom-call(bf16[1024,128]{1,0:T(8,128)(2,1)S(1)} %get-tuple-element.31.refs_1_.own, bf16[1024,128]{1,0:T(8,128)(2,1)S(1)} %collective-permute-done.2.refs_0_.other, f32[128,512]{1,0:T(8,128)S(1)} %get-tuple-element.18.refs_3_.spectrum, bf16[768,512]{1,0:T(8,128)(2,1)S(1)} %get-tuple-element.21.refs_4_.table), custom_call_target="tpu_custom_call" | custom-call | flops 1 | bytes 1 | tf_op jit(solution)/shard_map/pallas_call | solution.py:295
  10.7 3.2 %collective-permute-start.3 = (bf16[1024,128]{1,0:T(8,128)(2,1)S(1)}, bf16[1024,128]{1,0:T(8,128)(2,1)S(1)}, u32[]{:S(2)}, u32[]{:S(2)}) collective-permute-start(bf16[1024,128]{1,0:T(8,128)(2,1)S(1)} %shard_map.124), channel_id=1, source_target_pairs={{0,4},{2,6},{4,8},{6,10},{8,12},{10,14},{1,5},{3,7},{5,9},{7,11},{... | collective-permute-start | bytes 786440 | tf_op jit(solution)/shard_map/ppermute | solution.py:224
  13.9 0.7 %shard_map.120.base_a.refs_1_ = f32[1024,128]{1,0:T(8,128)S(1)} custom-call(bf16[1024,128]{1,0:T(8,128)(2,1)S(1)} %collective-permute-done.far.refs_0_, bf16[1024,128]{1,0:T(8,128)(2,1)S(1)} %get-tuple-element.19.own.refs_1_, f32[16,128]{1,0:T(8,128)S(1)} %get-tuple-element.20.refs_2_, f32[128,512]{1,0:T(8,128)S(1)} %get-tuple-element.18.refs_3_.spectrum, ...), custom_call_target="tpu_custom_call" | custom-call | flops 1 | bytes 1 | tf_op jit(solution)/shard_map/pallas_call | solution.py:295
  14.6 0.7 %shard_map.121.base_b.base = f32[1024,128]{1,0:T(8,128)S(1)} custom-call(bf16[1024,128]{1,0:T(8,128)(2,1)S(1)} %collective-permute-done.2.refs_0_.other, bf16[1024,128]{1,0:T(8,128)(2,1)S(1)} %get-tuple-element.31.refs_1_.own, f32[16,128]{1,0:T(8,128)S(1)} %get-tuple-element.20.refs_2_, f32[128,512]{1,0:T(8,128)S(1)} %get-tuple-element.18.refs_3_.spectrum, ...), custom_call_target="tpu_custom_call" | custom-call | flops 1 | bytes 1 | tf_op jit(solution)/shard_map/pallas_call | solution.py:295
  15.4 0.0 collective-permute-done.1.refs_0_
  15.4 1.1 %shard_map.123 = (bf16[128,1024]{1,0:T(8,128)(2,1)S(1)}, f32[128,1024]{1,0:T(8,128)S(1)}) custom-call(bf16[1024,128]{1,0:T(8,128)(2,1)S(1)} %collective-permute-done.1.refs_0_, f32[1024,128]{1,0:T(8,128)S(1)} %shard_map.120.base_a.refs_1_, bf16[2048,128]{1,0:T(8,128)(2,1)S(1)} %get-tuple-element.22.query.refs_2_, ...), custom_call_target="tpu_custom_call", output_to_operand_aliasing={{0}: (6, {})} | custom-call | flops 1 | bytes 1 | tf_op jit(solution)/shard_map/pallas_call | solution.py:295
  16.5 2.1 %collective-permute-done.3.carried = bf16[1024,128]{1,0:T(8,128)(2,1)S(1)} collective-permute-done((bf16[1024,128]{1,0:T(8,128)(2,1)S(1)}, bf16[1024,128]{1,0:T(8,128)(2,1)S(1)}, u32[]{:S(2)}, u32[]{:S(2)}) %collective-permute-start.3) | collective-permute-done | bytes 262176 | tf_op jit(solution)/shard_map/ppermute | solution.py:224
  18.6 0.5 %shard_map.125 = (bf16[128,1024]{1,0:T(8,128)(2,1)S(1)}, bf16[128,1024]{1,0:T(8,128)(2,1)S(1)}) custom-call(bf16[1024,128]{1,0:T(8,128)(2,1)S(1)} %collective-permute-done.3.carried, f32[1024,128]{1,0:T(8,128)S(1)} %shard_map.121.base_b.base, bf16[2048,128]{1,0:T(8,128)(2,1)S(1)} %get-tuple-element.22.query.refs_2_, ...), custom_call_target="tpu_custom_call", output_to_operand_aliasing={{0}: (5, {}), {1}: (6, {})} | custom-call | flops 1 | bytes 1 | tf_op jit(solution)/shard_map/pallas_call | solution.py:295
  19.1 2.8 %collective-permute-start.4 = (bf16[128,1024]{1,0:T(8,128)(2,1)S(1)}, bf16[128,1024]{1,0:T(8,128)(2,1)S(1)}, u32[]{:S(2)}, u32[]{:S(2)}) collective-permute-start(bf16[128,1024]{1,0:T(8,128)(2,1)S(1)} %get-tuple-element.30), channel_id=1, source_target_pairs={{0,1},{1,0},{2,3},{3,2},{4,5},{5,4},{6,7},{7,6},{8,9},{9,8},{10,11... | collective-permute-start | bytes 786440 | tf_op jit(solution)/shard_map/ppermute | solution.py:352
  21.9 0.7 %shard_map.126 = f32[128,1024]{1,0:T(8,128)S(1)} custom-call(bf16[128,1024]{1,0:T(8,128)(2,1)S(1)} %get-tuple-element.25.gated_a, bf16[128,1024]{1,0:T(8,128)(2,1)S(1)} %get-tuple-element.29.gated_b, bf16[2048,2048]{1,0:T(8,128)(2,1)S(1)} %get-tuple-element.23.weight.refs_5_), custom_call_target="tpu_custom_call" | custom-call | flops 1 | bytes 1 | tf_op jit(solution)/shard_map/pallas_call | solution.py:295
  22.6 0.4 %collective-permute-done.4 = bf16[128,1024]{1,0:T(8,128)(2,1)S(1)} collective-permute-done((bf16[128,1024]{1,0:T(8,128)(2,1)S(1)}, bf16[128,1024]{1,0:T(8,128)(2,1)S(1)}, u32[]{:S(2)}, u32[]{:S(2)}) %collective-permute-start.4) | collective-permute-done | bytes 262176 | tf_op jit(solution)/shard_map/ppermute | solution.py:352
  23.1 0.8 %add_convert_fusion = bf16[128,1024]{1,0:T(8,128)(2,1)} fusion(f32[128,1024]{1,0:T(8,128)S(1)} %shard_map.126, bf16[128,1024]{1,0:T(8,128)(2,1)S(1)} %collective-permute-done.4), kind=kLoop, calls=%fused_computation | loop fusion | flops 393216 | bytes 1048576 | tf_op jit(solution)/shard_map/convert_element_type | solution.py:354
  (1 shorter events, 0.0 us)
Async XLA Ops:
  1.3 7.2 %collective-permute-start = (bf16[1024,128]{1,0:T(8,128)(2,1)S(1)}, bf16[1024,128]{1,0:T(8,128)(2,1)S(1)}, u32[]{:S(2)}, u32[]{:S(2)}) collective-permute-start(bf16[1024,128]{1,0:T(8,128)(2,1)S(1)} %get-tuple-element.19.own.refs_1_), channel_id=1, source_target_pairs={{0,4},{2,6},{4,8},{6,10},{8,12},{10,14},{12,0},{14,2},{1,5},{3,7},... | collective-permute-start | bytes 786440 | tf_op jit(solution)/shard_map/ppermute | solution.py:224
  2.7 7.3 %collective-permute-start.2 = (bf16[1024,128]{1,0:T(8,128)(2,1)S(1)}, bf16[1024,128]{1,0:T(8,128)(2,1)S(1)}, u32[]{:S(2)}, u32[]{:S(2)}) collective-permute-start(bf16[1024,128]{1,0:T(8,128)(2,1)S(1)} %get-tuple-element.31.refs_1_.own), channel_id=1, source_target_pairs={{0,2},{2,0},{4,6},{6,4},{8,10},{10,8},{12,14},{14,12},{1,3},{3,1},... | collective-permute-start | bytes 786440 | tf_op jit(solution)/shard_map/ppermute | solution.py:228
  8.6 6.7 %collective-permute-start.1 = (bf16[1024,128]{1,0:T(8,128)(2,1)S(1)}, bf16[1024,128]{1,0:T(8,128)(2,1)S(1)}, u32[]{:S(2)}, u32[]{:S(2)}) collective-permute-start(bf16[1024,128]{1,0:T(8,128)(2,1)S(1)} %shard_map.119), channel_id=1, source_target_pairs={{0,2},{2,0},{4,6},{6,4},{8,10},{10,8},{12,14},{14,12},{1,3},{3,1},... | collective-permute-start | bytes 786440 | tf_op jit(solution)/shard_map/ppermute | solution.py:228
  10.7 7.9 %collective-permute-start.3 = (bf16[1024,128]{1,0:T(8,128)(2,1)S(1)}, bf16[1024,128]{1,0:T(8,128)(2,1)S(1)}, u32[]{:S(2)}, u32[]{:S(2)}) collective-permute-start(bf16[1024,128]{1,0:T(8,128)(2,1)S(1)} %shard_map.124), channel_id=1, source_target_pairs={{0,4},{2,6},{4,8},{6,10},{8,12},{10,14},{1,5},{3,7},{5,9},{7,11},{... | collective-permute-start | bytes 786440 | tf_op jit(solution)/shard_map/ppermute | solution.py:224
  19.1 4.0 %collective-permute-start.4 = (bf16[128,1024]{1,0:T(8,128)(2,1)S(1)}, bf16[128,1024]{1,0:T(8,128)(2,1)S(1)}, u32[]{:S(2)}, u32[]{:S(2)}) collective-permute-start(bf16[128,1024]{1,0:T(8,128)(2,1)S(1)} %get-tuple-element.30), channel_id=1, source_target_pairs={{0,1},{1,0},{2,3},{3,2},{4,5},{5,4},{6,7},{7,6},{8,9},{9,8},{10,11... | collective-permute-start | bytes 786440 | tf_op jit(solution)/shard_map/ppermute | solution.py:352
